TPU v7x, 32 devices: a whole 2x2x4 slice. The times are simulated.
32 devices in a mesh: grp: 2 (over x), head: 8 (over z, y), tok: 2 (over core).
Axes of the slice: x: 2, y: 2, z: 4, core: 2. Of those that a mesh axis runs over, the one named last changes fastest.
Arguments:
- queries: bfloat16 [1024, 16384], P(('grp', 'tok'), 'head'), parts along dimension 0, may hold values from -18 to 18
- key_rows: bfloat16 [1024, 1024], P(('grp', 'tok')), parts along dimension 0, may hold values from -5 to 5
- values: bfloat16 [1024, 1024], P(('grp', 'tok')), parts along dimension 0, may hold values from -15 to 15
- sign_bits: int32 [16384], replicated, may hold values from 0 to 1
Outputs:
- hessian: bfloat16 [32768, 16384], P(('grp', 'tok'), 'head'), parts along dimension 0
There are 2 independent parts, one for each index of `grp`. A program takes and returns all parts, laid end to end along the dimension named above; an argument that names none is the same for every part. Nothing has to cross between parts.
All inputs are finite; a program needn't handle non-finite values.
Results may differ from a plain program's by a relative error of at most 0.0055.
Values may be sent and summed in bfloat16 or wider, within the bound.
No kernel may reach another device: no remote copies, remote signals or barrier semaphores. Data moves between devices by JAX's collectives and lax.ppermute only.
A program may use at most 448 MiB of HBM per device.

v0:
```python
import math

import jax
import jax.numpy as jnp
from jax import lax
from jax.sharding import PartitionSpec as P

HEADS = 128
DH = 128


def from_behind(value, axis, by):
    devices = lax.axis_size(axis)
    pairs = [(i, i + by) for i in range(devices) if 0 <= i + by < devices]
    return lax.ppermute(value, axis, pairs)


def sylvester(order):
    counter = jnp.arange(order, dtype=jnp.int32)
    anded = counter[:, None] & counter[None, :]
    parity = jnp.zeros_like(anded)
    for bit_level in range(max(order.bit_length(), 1)):
        parity = parity ^ anded >> bit_level & 1
    return (1 - 2 * parity).astype(jnp.float32)


def mix_heads(row_block, head_table):
    count_rows = row_block.shape[0]
    cube = row_block.reshape(count_rows, HEADS, DH)
    mixed = jnp.einsum("rhe,hg->rge", cube, head_table, preferred_element_type=jnp.float32)
    mixed = mixed * (1.0 / math.sqrt(HEADS))
    return mixed.astype(jnp.bfloat16).reshape(count_rows, HEADS * DH)


def spread_heads(block_rows, kv_count, local_heads, share):
    count_rows = block_rows.shape[0]
    cube = block_rows.reshape(count_rows, kv_count, DH)
    if local_heads >= share:
        return jnp.repeat(cube, share, axis=1)
    return jnp.broadcast_to(cube, (count_rows, local_heads, DH))


def local(queries, key_rows, values, sign_bits):
    tok_rows = queries.shape[0]
    local_width = queries.shape[1]
    local_heads = local_width // DH
    share = HEADS // (key_rows.shape[1] // DH)
    inv_dh = 1.0 / math.sqrt(DH)
    head_index = lax.axis_index("head")
    if local_heads >= share:
        kv_count = local_heads // share
        kv_first = head_index * kv_count
    else:
        kv_count = 1
        kv_first = head_index * local_heads // share
    own_keys = lax.dynamic_slice_in_dim(key_rows, kv_first * DH, kv_count * DH, 1)
    own_values = lax.dynamic_slice_in_dim(values, kv_first * DH, kv_count * DH, 1)
    prev_keys, prev_values = from_behind((own_keys, own_values), "tok", 1)
    key_block = spread_heads(
        jnp.concatenate([prev_keys, own_keys], 0), kv_count, local_heads, share
    )
    value_block = spread_heads(
        jnp.concatenate([prev_values, own_values], 0), kv_count, local_heads, share
    )
    query_block = queries.reshape(tok_rows, local_heads, DH)
    scores = (
        jnp.einsum("thd,shd->hts", query_block, key_block, preferred_element_type=jnp.float32)
        * inv_dh
    )
    row_pos = jnp.arange(tok_rows, dtype=jnp.int32)[:, None]
    col_pos = jnp.arange(2 * tok_rows, dtype=jnp.int32)[None, :]
    earlier = lax.axis_index("tok") > 0
    allowed = jnp.where(col_pos < tok_rows, earlier, col_pos - tok_rows <= row_pos)
    scores = jnp.where(allowed[None], scores, -1e30)
    row_max = jnp.max(scores, axis=-1, keepdims=True)
    expo = jnp.exp(scores - row_max)
    row_total = jnp.sum(expo, axis=-1, keepdims=True)
    attended = (
        jnp.einsum(
            "hts,shd->htd",
            expo.astype(jnp.bfloat16),
            value_block,
            preferred_element_type=jnp.float32,
        )
        / row_total
    )
    sign_local = lax.dynamic_slice_in_dim(sign_bits, head_index * local_width, local_width, 0)
    sign_vals = (1 - 2 * sign_local).astype(jnp.float32).reshape(local_heads, 1, DH)
    inner_rot = jnp.einsum(
        "htd,de->the", attended * sign_vals, sylvester(DH), precision=lax.Precision.HIGHEST
    )
    inner_rot = (inner_rot * inv_dh).astype(jnp.bfloat16).reshape(tok_rows, local_width)
    head_table = sylvester(HEADS).astype(jnp.bfloat16)
    gathered = lax.all_gather(inner_rot, "head", axis=1, tiled=True)
    rotated = mix_heads(gathered, head_table)
    tok_count = lax.axis_size("tok")
    gram_scale = 2.0 / (tok_rows * tok_count)
    strip_start = head_index * local_width
    own_strip = lax.dynamic_slice_in_dim(rotated, strip_start, local_width, 1)
    gram = lax.dot_general(
        rotated, own_strip, (((0,), (0,)), ((), ())), preferred_element_type=jnp.float32
    )
    hessian = lax.psum_scatter(gram * gram_scale, "tok", scatter_dimension=0, tiled=True)
    return hessian.astype(jnp.bfloat16)


def solution(mesh):
    placed = (P(("grp", "tok"), "head"), P(("grp", "tok"), None), P(("grp", "tok"), None), P())
    return jax.shard_map(
        local, mesh=mesh, in_specs=placed, out_specs=P(("grp", "tok"), "head"), check_vma=False
    )
```

profile of v0, /device:TPU:0, one launch (start us, length us, event | category | flops | bytes accessed | tf_op | source)
XLA Modules:
  0.0 438.2 jit_solution(6525734609049951741)
XLA Ops:
  6.5 0.0 copy-start
  6.5 0.0 all-gather.2.cloned.1.call-start
  6.5 0.9 constant_dynamic-slice_fusion
  7.5 2.3 collective-permute-start.1
  9.8 0.9 constant_dynamic-slice_fusion.1
  10.7 1.3 collective-permute-start
  12.0 0.2 fusion.19
  12.2 0.7 convert_bitcast_fusion
  12.9 0.0 collective-permute-done
  12.9 0.0 copy-done
  12.9 1.4 fusion.2
  14.4 1.7 fusion
  16.1 0.0 collective-permute-done.1
  16.1 2.3 fusion.3
  18.5 3.3 multiply_convert_fusion.1
  21.8 0.0 all-gather.2.cloned.1.call-update
  21.8 0.0 reduce-scatter.5.cloned.1.call-start
  21.9 127.1 %all-gather.2.cloned.1.call-done = bf16[256,16384]{0,1:T(8,128)(2,1)} async-done(((bf16[256,2048]{0,1:T(8,128)(2,1)}), bf16[256,16384]{0,1:T(8,128)(2,1)}) %all-gather.2.cloned.1.call-update) | async-done | bytes 8388624 | tf_op jit(solution)/shard_map/all_gather | solution.py:94
  149.0 12.3 %copy.10 = bf16[256,128,128]{2,1,0:T(8,128)(2,1)} copy(bf16[256,128,128]{0,2,1:T(8,128)(2,1)} %bitcast.41) | data formatting | bytes 16777216 | tf_op jit(solution)/shard_map/reshape | solution.py:29
  161.3 9.0 %multiply_convert_fusion = bf16[128,256,128]{2,0,1:T(8,128)(2,1)} fusion(bf16[256,128,128]{2,1,0:T(8,128)(2,1)} %copy.10), kind=kOutput, calls=%fused_computation.1 | convolution fusion | flops 1082589184 | bytes 16777216 | tf_op jit(solution)/shard_map/rhe,hg->rge/dot_general | solution.py:30
  170.3 23.3 %copy.21 = bf16[32,8,128,128]{3,1,2,0:T(8,128)(2,1)} copy(bf16[32,8,128,128]{3,2,1,0:T(8,128)(2,1)} %bitcast.40) | data formatting | bytes 16777216
  193.6 48.5 %convolution_multiply_fusion = f32[16384,2048]{1,0:T(8,128)} fusion(bf16[256,16384]{1,0:T(8,128)(2,1)} %bitcast.39, s32[]{:T(128)S(6)} %select_n.23), kind=kOutput, calls=%fused_computation | convolution fusion | flops 17213423616 | bytes 143654912 | tf_op jit(solution)/shard_map/dot_general | solution.py:100
  242.1 0.0 reduce-scatter.5.cloned.1.call-update
  242.1 156.8 %reduce-scatter.5.cloned.1.call-done = f32[8192,2048]{1,0:T(8,128)} async-done(((f32[16384,2048]{1,0:T(8,128)}), f32[8192,2048]{1,0:T(8,128)}) %reduce-scatter.5.cloned.1.call-update) | async-done | bytes 67108880
  398.9 0.0 copy-start.1
  398.9 32.5 %convert_element_type.38 = bf16[8192,2048]{1,0:T(8,128)(2,1)} convert(f32[8192,2048]{1,0:T(8,128)} %reduce-scatter.5.cloned.1.call-done) | non-fusion elementwise | flops 16777216 | bytes 100663296 | tf_op jit(solution)/shard_map/convert_element_type | solution.py:104
  431.4 0.0 copy-done.1
  (4 shorter events, 0.0 us)
Async XLA Ops:
  6.5 6.4 %copy-start = (bf16[256,2048]{1,0:T(8,128)(2,1)S(1)}, bf16[256,2048]{1,0:T(8,128)(2,1)}, u32[]{:S(2)}) copy-start(bf16[256,2048]{1,0:T(8,128)(2,1)} %param.4) | copy-start | bytes 3145732
  6.5 142.5 %all-gather.2.cloned.1.call-start = ((), (), s32[]{:S(2)}) async-start(), calls=%async_computation.1 | async-start | bytes 9437184 | tf_op jit(solution)/shard_map/all_gather | solution.py:94
  7.5 8.6 %collective-permute-start.1 = (bf16[256,128]{1,0:T(8,128)(2,1)S(1)}, bf16[256,128]{1,0:T(8,128)(2,1)S(1)}, u32[]{:S(2)}, u32[]{:S(2)}) collective-permute-start(bf16[256,128]{1,0:T(8,128)(2,1)S(1)} %constant_dynamic-slice_fusion), channel_id=1, source_target_pairs={{0,1},{2,3},{4,5},{6,7},{8,9},{10,11},{12,13},{14,15},{16,17},{18,... | collective-permute-start | bytes 196616 | tf_op jit(solution)/shard_map/ppermute | solution.py:15
  10.7 2.2 collective-permute-start
  21.8 377.1 %reduce-scatter.5.cloned.1.call-start = ((), (), s32[]{:S(2)}) async-start(), calls=%async_computation.2 | async-start | bytes 201326592
  398.9 32.5 %copy-start.1 = (bf16[256,2048]{1,0:T(8,128)(2,1)S(1)}, bf16[256,2048]{1,0:T(8,128)(2,1)}, u32[]{:S(2)}) copy-start(bf16[256,2048]{1,0:T(8,128)(2,1)} %param.4) | copy-start | bytes 3145732
Sparse Core Ops, SparseCore 0:
  21.9 127.0 all-gather.1
  242.2 156.6 reduce-scatter.4
where the time goes:
time: 439 us; the launch traced here: 438 us
  waiting for transfers between devices  284 us (65%)
  matrix products  64.5 us (15%)
  local copies, waits for them, and re-layouts  37.5 us (9%)
  other arithmetic  35.2 us (8%)
  between operations  13.5 us (3%)
    unnamed x3, waiting for transfers between devices  157 us
    all_gather x1, waiting for transfers between devices, local(): gathered = lax.all_gather(inner_rot, 'head', axis=1, tiled=True)  127 us
    dot_general x1, matrix products, local(): lax.dot_general(rotated, own_strip, (((0,), (0,)), ((), ())), preferred_e...  48.5 us
    convert_element_type x1, other arithmetic, local(): return hessian.astype(jnp.bfloat16)  32.5 us
    unnamed x5, local copies, waits for them, and re-layouts  23.4 us
    reshape x1, local copies, waits for them, and re-layouts, mix_heads(): cube = row_block.reshape(count_rows, HEADS, DH)  12.3 us
    dot_general x1, matrix products, mix_heads(): jnp.einsum('rhe,hg->rge', cube, head_table, preferred_element_type=jnp.fl...  8.97 us
  transfers between devices with their start and end apart: 4, of which 2 were waited for; matrix products, arithmetic and copies ran while one was open for 1% of the time, Pallas kernels for 0%

commit v1 on v0

v1 whole, which is shorter than its diff:
```python
import functools
import math

import jax
import jax.numpy as jnp
from jax import lax
from jax.experimental import pallas as pl
from jax.experimental.pallas import tpu as pltpu
from jax.sharding import PartitionSpec as P

HEADS = 128
DH = 128
MIB = 1024 * 1024
ATTEND_UNROLL = 4
MIX_WAIT, MIX_DUE = 1, 4
GRAM_WAIT, GRAM_DUE = 3, 6


def butterfly(tiles):
    if len(tiles) == 1:
        return tiles
    half = len(tiles) // 2
    low = [tiles[i] + tiles[i + half] for i in range(half)]
    high = [tiles[i] - tiles[i + half] for i in range(half)]
    return butterfly(low) + butterfly(high)


def nt_dot(left, right):
    return lax.dot_general(left, right, (((1,), (1,)), ((), ())), preferred_element_type=jnp.float32)


def ring_place(device, devices):
    if devices != 8:
        return device
    upward = device // 2
    return jnp.where(lax.rem(device, 2) == 0, upward, devices - 1 - upward)


def ring_device(place, devices):
    if devices != 8:
        return place
    return jnp.where(place < devices // 2, 2 * place, 2 * (devices - 1 - place) + 1)


def attend_kernel(kv_share, unroll, q_hbm, ko_hbm, vo_hbm, sign_hbm, kp_any, vp_any, out_ref, *scratch):
    q_ref, kv_ref, sign_ref, inner_ref, vt_ref, bar_ref, sem = scratch
    rows, width = q_ref.shape
    heads = width // DH
    scale = math.log2(math.e) / math.sqrt(DH)
    first_head = lax.axis_index("head") * heads
    columns = pl.ds(pl.multiple_of(first_head // kv_share * DH, DH), DH)
    copies = [
        pltpu.make_async_copy(ko_hbm.at[:, columns], kv_ref.at[0], sem.at[0]),
        pltpu.make_async_copy(kp_any.at[:, columns], kv_ref.at[1], sem.at[1]),
        pltpu.make_async_copy(vo_hbm.at[:, columns], kv_ref.at[2], sem.at[2]),
        pltpu.make_async_copy(vp_any.at[:, columns], kv_ref.at[3], sem.at[3]),
        pltpu.make_async_copy(sign_hbm, sign_ref, sem.at[4]),
        pltpu.make_async_copy(q_hbm, q_ref, sem.at[5]),
    ]
    for copy in copies:
        copy.start()
    core = lax.axis_index("tok")
    key_pos = lax.broadcasted_iota(jnp.int32, (rows, rows), 0)
    query_pos = lax.broadcasted_iota(jnp.int32, (rows, rows), 1)
    bar_ref[...] = jnp.where(key_pos <= query_pos, 0.0, -1e30)
    anded = lax.broadcasted_iota(jnp.int32, (DH, DH), 0) & lax.broadcasted_iota(jnp.int32, (DH, DH), 1)
    odd = jnp.zeros_like(anded)
    for level in range(7):
        odd = odd ^ (anded >> level) & 1
    table = (1 - 2 * odd).astype(jnp.float32)
    for copy in copies[2:4]:
        copy.wait()
    vt_ref[:, :rows] = kv_ref[3].astype(jnp.float32).T.astype(jnp.bfloat16)
    vt_ref[:, rows:] = kv_ref[2].astype(jnp.float32).T.astype(jnp.bfloat16)
    for copy in copies[:2] + copies[4:]:
        copy.wait()

    def one(h, earlier):
        q = q_ref[:, pl.ds(pl.multiple_of(h * DH, DH), DH)]
        own = nt_dot(kv_ref[0], q) + bar_ref[...]
        top = jnp.max(own, axis=0, keepdims=True)
        if earlier:
            before = nt_dot(kv_ref[1], q)
            top = jnp.maximum(top, jnp.max(before, axis=0, keepdims=True))
        weights = jnp.exp2((own - top) * scale)
        total = jnp.sum(weights, axis=0, keepdims=True)
        attended = jnp.dot(vt_ref[:, rows:], weights.astype(jnp.bfloat16), preferred_element_type=jnp.float32)
        if earlier:
            weights = jnp.exp2((before - top) * scale)
            total += jnp.sum(weights, axis=0, keepdims=True)
            attended += jnp.dot(vt_ref[:, :rows], weights.astype(jnp.bfloat16), preferred_element_type=jnp.float32)
        attended = attended * (1.0 / total)
        coarse = attended.astype(jnp.bfloat16)
        fine = (attended - coarse.astype(jnp.float32)).astype(jnp.bfloat16)
        signs = (1 - 2 * sign_ref[pl.ds(first_head + h, 1), :]).astype(jnp.float32)
        turn = (table * signs).astype(jnp.bfloat16)
        inner = jnp.dot(turn, coarse, preferred_element_type=jnp.float32) + jnp.dot(
            turn, fine, preferred_element_type=jnp.float32
        )
        inner_ref[h] = (inner * (1.0 / math.sqrt(DH))).astype(jnp.bfloat16)

    unroll = math.gcd(heads, unroll)

    def every(earlier):
        @pl.loop(0, heads // unroll)
        def _(step):
            for u in range(unroll):
                one(step * unroll + u, earlier)

    pl.when(core > 0)(lambda: every(True))
    pl.when(core == 0)(lambda: every(False))

    shrink = 1.0 / math.sqrt(heads)

    @pl.loop(0, DH // 16)
    def _(block):
        band = pl.ds(pl.multiple_of(block * 16, 16), 16)
        for lane in range(0, rows, 128):
            tiles = [inner_ref[h, band, lane : lane + 128].astype(jnp.float32) for h in range(heads)]
            for h, tile in enumerate(butterfly(tiles)):
                at = pl.ds(pl.multiple_of(h * DH + block * 16, 16), 16)
                out_ref[at, lane : lane + 128] = (tile * shrink).astype(jnp.bfloat16)


def attend(queries, own_keys, own_values, signs, prev_keys, prev_values):
    rows, width = queries.shape
    kv_share = HEADS // (own_keys.shape[1] // DH)
    heads = width // DH
    hbm, anywhere = pl.BlockSpec(memory_space=pltpu.HBM), pl.BlockSpec(memory_space=pl.ANY)
    return pl.pallas_call(
        functools.partial(attend_kernel, kv_share, ATTEND_UNROLL),
        in_specs=[hbm] * 4 + [anywhere] * 2,
        out_specs=pl.BlockSpec(memory_space=pltpu.VMEM),
        scratch_shapes=[
            pltpu.VMEM((rows, width), jnp.bfloat16),
            pltpu.VMEM((4, rows, DH), jnp.bfloat16),
            pltpu.VMEM((HEADS, DH), jnp.int32),
            pltpu.VMEM((heads, DH, rows), jnp.bfloat16),
            pltpu.VMEM((DH, 2 * rows), jnp.bfloat16),
            pltpu.VMEM((rows, rows), jnp.float32),
            pltpu.SemaphoreType.DMA((6,)),
        ],
        out_shape=jax.ShapeDtypeStruct((width, rows), jnp.bfloat16),
        compiler_params=pltpu.CompilerParams(vmem_limit_bytes=60 * MIB),
        cost_estimate=pl.CostEstimate(flops=20000000000, bytes_accessed=1024, transcendentals=0),
        name="attend",
    )(queries, own_keys, own_values, signs, prev_keys, prev_values)


def mix_kernel(devices, offset, *refs):
    count = devices + 1
    pieces, (keep_ref, send_ref, held, sem) = refs[:count], refs[count:]
    rows = keep_ref.shape[1]
    lanes = keep_ref.shape[2]
    half = devices // 2
    head, core = lax.axis_index("head"), lax.axis_index("tok")
    place = ring_place(head, devices)
    shifts = [0] + [shift for step in range(1, half) for shift in (devices - step, step)] + [half]
    slots = [ring_device(lax.rem(place + shift, devices), devices) for shift in shifts]
    copies = []
    for p, piece in enumerate(pieces):
        if p == 0:
            source, target = piece.at[pl.ds(offset, rows), :], held.at[slots[0]]
        elif p < devices - 1:
            source, target = piece, held.at[slots[p]]
        else:
            part = (p - (devices - 1)) * (rows // 2)
            source, target = piece, held.at[slots[devices - 1], pl.ds(part, rows // 2), :]
        copies.append(pltpu.make_async_copy(source, target, sem.at[p]))
    for copy in copies:
        copy.start()
    for copy in copies:
        copy.wait()
    flip = jnp.where(core > 0, -1.0, 1.0).astype(jnp.float32)
    shrink = 1.0 / math.sqrt(devices)
    in_keep = (head // half) == core
    own_slot = lax.rem(head, half)

    @pl.loop(0, rows // 16)
    def _(block):
        band = pl.ds(pl.multiple_of(block * 16, 16), 16)
        for lane in range(0, lanes, 128):
            span = slice(lane, lane + 128)
            tiles = [held[d, band, span].astype(jnp.float32) for d in range(devices)]
            flipped = [tiles[d + half] * flip for d in range(half)]
            stay = butterfly([tiles[d] + flipped[d] for d in range(half)])
            leave = butterfly([tiles[d] - flipped[d] for d in range(half)])
            for d in range(half):
                keep_ref[d, band, span] = (stay[d] * shrink).astype(jnp.bfloat16)
                send_ref[d, band, span] = (leave[d] * shrink).astype(jnp.bfloat16)

    @pl.when(in_keep)
    def _():
        strip = keep_ref[own_slot]
        keep_ref[half] = strip
        send_ref[half] = strip

    @pl.when(jnp.logical_not(in_keep))
    def _():
        strip = send_ref[own_slot]
        keep_ref[half] = strip
        send_ref[half] = strip


def mix(devices, offset, rows, own, pieces):
    lanes = own.shape[1]
    half = devices // 2
    shape = (half + 1, rows, lanes)
    return pl.pallas_call(
        functools.partial(mix_kernel, devices, offset),
        in_specs=[pl.BlockSpec(memory_space=pl.ANY)] * (devices + 1),
        out_specs=[pl.BlockSpec(memory_space=pltpu.VMEM)] * 2,
        scratch_shapes=[
            pltpu.VMEM((devices, rows, lanes), jnp.bfloat16),
            pltpu.SemaphoreType.DMA((devices + 1,)),
        ],
        out_shape=[jax.ShapeDtypeStruct(shape, jnp.bfloat16)] * 2,
        compiler_params=pltpu.CompilerParams(vmem_limit_bytes=24 * MIB),
        cost_estimate=pl.CostEstimate(flops=20000000000, bytes_accessed=1024, transcendentals=0),
        name="mix",
    )(own, *pieces)


def gram_kernel(starts, sizes, chunk, scale, aliased, *refs):
    refs = list(refs)
    take = lambda n: [refs.pop(0) for _ in range(n)]
    if aliased:
        take(1)
    keep_rows, recv_rows = take(chunk + 1), take(chunk + 1)
    keep_cols, recv_cols = take(chunk + 1), take(chunk + 1)
    (out_ref,) = take(1)
    wide, sem = take(2)
    tall = take(1)[0] if chunk else None
    r, steps = pl.program_id(0), pl.num_programs(0)
    slot = lax.rem(r, 2)
    first, size = starts[chunk], sizes[chunk]

    def wide_copy(at, s):
        return pltpu.make_async_copy(
            wide.at[s], out_ref.at[at, pl.ds(first, size), pl.ds(0, first + size)], sem.at[0, s]
        )

    def tall_copy(at, s):
        return pltpu.make_async_copy(
            tall.at[s], out_ref.at[at, pl.ds(0, first), pl.ds(first, size)], sem.at[1, s]
        )

    @pl.when(r >= 2)
    def _():
        wide_copy(r - 2, slot).wait()
        if chunk:
            tall_copy(r - 2, slot).wait()

    def block(a_keep, a_recv, b_keep, b_recv, store):
        height, width = a_keep.shape[1], b_keep.shape[1]
        tile_m = math.gcd(height, 256)
        tile_n = math.gcd(width, 512)
        for i in range(0, height, tile_m):
            left, left_other = a_keep[0, i : i + tile_m, :], a_recv[0, i : i + tile_m, :]
            for k in range(0, width, tile_n):
                total = nt_dot(left, b_keep[0, k : k + tile_n, :]) + nt_dot(left_other, b_recv[0, k : k + tile_n, :])
                store(i, tile_m, k, tile_n, (total * scale).astype(jnp.bfloat16))

    for c in range(chunk + 1):

        def store_wide(i, m, k, n, value):
            wide[slot, i : i + m, starts[c] + k : starts[c] + k + n] = value

        block(keep_rows[chunk], recv_rows[chunk], keep_cols[c], recv_cols[c], store_wide)
    wide_copy(r, slot).start()
    for c in range(chunk):

        def store_tall(i, m, k, n, value):
            tall[slot, starts[c] + i : starts[c] + i + m, k : k + n] = value

        block(keep_rows[c], recv_rows[c], keep_cols[chunk], recv_cols[chunk], store_tall)
    if chunk:
        tall_copy(r, slot).start()

    @pl.when(r == steps - 1)
    def _():
        for back in (1, 0):
            at = r - back
            wide_copy(at, lax.rem(at, 2)).wait()
            if chunk:
                tall_copy(at, lax.rem(at, 2)).wait()


def gram(out, keeps, recvs, starts, sizes, chunk, scale, shape):
    half = keeps[0].shape[0] - 1
    lanes = keeps[0].shape[2]
    first, size = starts[chunk], sizes[chunk]
    row_spec = [pl.BlockSpec((1, sizes[c], lanes), lambda r: (r, 0, 0)) for c in range(chunk + 1)]
    col_spec = [pl.BlockSpec((1, sizes[c], lanes), lambda r: (half, 0, 0)) for c in range(chunk + 1)]
    aliased = out is not None
    anywhere = pl.BlockSpec(memory_space=pl.ANY)
    scratch = [pltpu.VMEM((2, size, first + size), jnp.bfloat16), pltpu.SemaphoreType.DMA((2, 2))]
    if chunk:
        scratch.append(pltpu.VMEM((2, first, size), jnp.bfloat16))
    area = half * (size * (first + size) + first * size)
    return pl.pallas_call(
        functools.partial(gram_kernel, starts, sizes, chunk, scale, aliased),
        grid=(half,),
        in_specs=([anywhere] if aliased else []) + row_spec * 2 + col_spec * 2,
        out_specs=anywhere,
        out_shape=jax.ShapeDtypeStruct(shape, jnp.bfloat16),
        scratch_shapes=scratch,
        input_output_aliases={0: 0} if aliased else {},
        compiler_params=pltpu.CompilerParams(vmem_limit_bytes=40 * MIB),
        cost_estimate=pl.CostEstimate(flops=20000000000, bytes_accessed=1024, transcendentals=0),
        name=f"gram{chunk}",
    )(*(([out] if aliased else []) + keeps + recvs + keeps + recvs))


PLANS = {(16, 4): ([4, 4, 4, 4], [0, 1, 0, 1, 0, 1, 0, 2, 1, 2, 3, 2, 3, 2, 3, 3])}


def plan(local_heads, hops):
    if (local_heads, hops) in PLANS:
        return PLANS[local_heads, hops]
    done = [0] * local_heads
    sequence = []
    while min(done) < hops:
        last = sequence[-1] if sequence else -1
        ready = [c for c in range(local_heads) if done[c] < hops]
        pick = next((c for c in ready if c != last), ready[0])
        done[pick] += 1
        sequence.append(pick)
    return [1] * local_heads, sequence


def after(values, *others):
    return lax.optimization_barrier((tuple(values), others))[0]


def local(devices, queries, key_rows, values, sign_bits):
    rows, width = queries.shape
    tok_count = lax.axis_size("tok")
    half = devices // 2
    order = list(range(devices))
    if devices == 8:
        order = order[0::2] + order[:0:-2]
    forward = [(order[i], order[(i + 1) % devices]) for i in range(devices)]
    backward = [(b, a) for a, b in forward]
    prev_keys, prev_values = lax.ppermute((key_rows, values), "tok", [(0, 1)])
    mixed = attend(queries, key_rows, values, sign_bits.reshape(HEADS, DH), prev_keys, prev_values)

    heads_of, sequence = plan(width // DH, half)
    sizes = [c * DH for c in heads_of]
    chunks = len(sizes)
    starts = [sum(sizes[:c]) for c in range(chunks)]
    held = [[mixed[starts[c] : starts[c] + sizes[c]]] * 2 for c in range(chunks)]
    pieces = [[] for _ in range(chunks)]
    scale = 2.0 / (rows * tok_count)
    keeps, recvs, out = [None] * chunks, [None] * chunks, None
    landed, due, pending = [], {}, []
    for k, c in enumerate(sequence):
        going, coming = held[c]
        if len(pieces[c]) == 2 * (half - 1):
            going, coming = going[: sizes[c] // 2], coming[sizes[c] // 2 :]
        waits = landed[max(0, k - 3) : max(0, k - 1)] + due.pop(k, [])
        if waits:
            going, coming = after((going, coming), *waits)
        with jax.named_scope(f"up{k}c{c}"):
            going = lax.ppermute(going, "head", forward)
        with jax.named_scope(f"down{k}c{c}"):
            coming = lax.ppermute(coming, "head", backward)
        landed.append((going, coming))
        held[c] = [going, coming]
        pieces[c] += [going, coming]
        if len(pieces[c]) == 2 * half:
            pending.append(("mix", c, k + MIX_WAIT, k + MIX_DUE))
            pending.append(("gram", c, k + GRAM_WAIT, k + GRAM_DUE))
        final = k == len(sequence) - 1
        for task in list(pending):
            kind, which, ready, deadline = task
            if ready > k and not final:
                continue
            pending.remove(task)
            if kind == "mix":
                own = mixed
                if not final:
                    own, pieces[which] = after((mixed, pieces[which]), landed[k])
                keeps[which], send = mix(devices, starts[which], sizes[which], own, pieces[which])
                with jax.named_scope(f"swap{which}"):
                    recvs[which] = lax.ppermute(send, "tok", [(0, 1), (1, 0)])
                done = keeps[which]
            else:
                n = which + 1
                if not final:
                    keeps[which] = after((keeps[which],), landed[k])[0]
                out = gram(out, keeps[:n], recvs[:n], starts, sizes, which, scale, (half, width, width))
                done = out
            due.setdefault(deadline, []).append(done)
    return out.reshape(half * width, width)


def solution(mesh):
    placed = (P(("grp", "tok"), "head"), P(("grp", "tok"), None), P(("grp", "tok"), None), P())
    return jax.shard_map(
        functools.partial(local, mesh.shape["head"]),
        mesh=mesh,
        in_specs=placed,
        out_specs=P(("grp", "tok"), "head"),
        check_vma=False,
    )
```

time: 439 us -> 138 us (0.31)
  waiting for transfers between devices: 284 us -> 57.3 us
  matrix products: 64.5 us -> 0 us
  Pallas kernels: 0 us -> 40.9 us
  local copies, waits for them, and re-layouts: 37.5 us -> 2.26 us
  other arithmetic: 35.2 us -> 0 us
  starting transfers between devices: 3.67 us -> 37.5 us
  between operations: 13.5 us -> 0.38 us
    unnamed x3 -> x0, waiting for transfers between devices: 157 us -> none
    all_gather x1 -> x0, waiting for transfers between devices: 127 us -> none  [local(): gathered = lax.all_gather(inner_rot, 'head', axis=1, tiled=True)]
    dot_general x5 -> x0, matrix products: 64.5 us -> none  [the longest x1 48.5 us: local(): lax.dot_general(rotated, own_strip, (((0,), (0,)), ((), ())), preferred_e...]
    ppermute x2 -> x38, waiting for transfers between devices: 0.01 us -> 57.3 us  [the longest x16 42.1 us: local(): going = lax.ppermute(going, 'head', forward)]
    pallas_call x0 -> x9, Pallas kernels: none -> 40.9 us  [the longest x4 25.1 us: gram(): pl.pallas_call(functools.partial(gram_kernel, starts, sizes, chunk, scale...]
    ppermute x2 -> x38, starting transfers between devices: 3.63 us -> 37.5 us  [the longest x16 18.3 us: local(): coming = lax.ppermute(coming, 'head', backward)]
    convert_element_type x1 -> x0, other arithmetic: 32.5 us -> none  [local(): return hessian.astype(jnp.bfloat16)]
    unnamed x5 -> x6, local copies, waits for them, and re-layouts: 23.4 us -> 0.84 us
  transfers between devices with their start and end apart: 4 -> 38, of which waited for: 2 -> 24; matrix products, arithmetic and copies ran while one was open for 1% -> 0% of each run, Pallas kernels for 0% -> 16%
where the time goes in v1:
time: 138 us
  waiting for transfers between devices  57.3 us (42%)
  Pallas kernels  40.9 us (30%)
  starting transfers between devices  37.5 us (27%)
  local copies, waits for them, and re-layouts  2.26 us (2%)
    ppermute x16, waiting for transfers between devices, local(): going = lax.ppermute(going, 'head', forward)  42.1 us
    pallas_call x4, Pallas kernels, gram(): pl.pallas_call(functools.partial(gram_kernel, starts, sizes, chunk, scale...  25.1 us
    ppermute x16, starting transfers between devices, local(): coming = lax.ppermute(coming, 'head', backward)  18.3 us
    ppermute x16, starting transfers between devices, local(): going = lax.ppermute(going, 'head', forward)  14.8 us
    ppermute x16, waiting for transfers between devices, local(): coming = lax.ppermute(coming, 'head', backward)  13.4 us
    pallas_call x1, Pallas kernels, attend(): pl.pallas_call(functools.partial(attend_kernel, kv_share, ATTEND_UNROLL),...  8.7 us
    pallas_call x4, Pallas kernels, mix(): pl.pallas_call(functools.partial(mix_kernel, devices, offset), in_specs=[...  7.11 us
    ppermute x2, starting transfers between devices, local(): prev_keys, prev_values = lax.ppermute((key_rows, values), 'tok', [(0, 1)])  3.7 us
  transfers between devices with their start and end apart: 38, of which 24 were waited for; matrix products, arithmetic and copies ran while one was open for 0% of the time, Pallas kernels for 16%

profile of v1, /device:TPU:0, one launch (start us, length us, event | category | flops | bytes accessed | tf_op | source)
XLA Modules:
  0.0 138.2 jit_solution(169622581844945903)
XLA Ops:
  0.0 2.4 %collective-permute-start = (bf16[256,1024]{1,0:T(8,128)(2,1)}, bf16[256,1024]{1,0:T(8,128)(2,1)S(1)}, u32[]{:S(2)}, u32[]{:S(2)}) collective-permute-start(bf16[256,1024]{1,0:T(8,128)(2,1)} %ko_hbm.1), channel_id=1, source_target_pairs={{0,1},{2,3},{4,5},{6,7},{8,9},{10,11},{12,13},{14,15},{16,17},{18,... | collective-permute-start | bytes 1572872 | tf_op jit(solution)/shard_map/ppermute | solution.py:345
  6.2 8.7 %attend.1.refs_0_ = bf16[2048,256]{1,0:T(8,128)(2,1)} custom-call(bf16[256,2048]{1,0:T(8,128)(2,1)} %q_hbm.1, bf16[256,1024]{1,0:T(8,128)(2,1)} %ko_hbm.1, bf16[256,1024]{1,0:T(8,128)(2,1)} %vo_hbm.1, s32[128,128]{1,0:T(8,128)} %bitcast.2, bf16[256,1024]{1,0:T(8,128)(2,1)} %copy-done.1, bf16[256,1024]{1,0:T(8,128)(2,1)} %copy-done.2), custom_call_target="tpu_custom_call" | custom-call | flops 20000000000 | bytes 1024 | tf_op jit(solution)/shard_map/attend/pallas_call | solution.py:130
  16.3 2.4 %collective-permute-start.3 = (bf16[512,256]{1,0:T(8,128)(2,1)S(1)}, bf16[512,256]{1,0:T(8,128)(2,1)S(1)}, u32[]{:S(2)}, u32[]{:S(2)}) collective-permute-start(bf16[512,256]{1,0:T(8,128)(2,1)S(1)} %get-tuple-element.138), channel_id=1, source_target_pairs={{4,0},{8,4},{12,8},{14,12},{10,14},{6,10},{2,6},{0,2},{5,1},{9,5},... | collective-permute-start | bytes 786440 | tf_op jit(solution)/shard_map/down0c0/ppermute | solution.py:367
  18.8 1.9 %collective-permute-start.7 = (bf16[512,256]{1,0:T(8,128)(2,1)S(1)}, bf16[512,256]{1,0:T(8,128)(2,1)S(1)}, u32[]{:S(2)}, u32[]{:S(2)}) collective-permute-start(bf16[512,256]{1,0:T(8,128)(2,1)S(1)} %get-tuple-element.137), channel_id=1, source_target_pairs={{4,0},{8,4},{12,8},{14,12},{10,14},{6,10},{2,6},{0,2},{5,1},{9,5},... | collective-permute-start | bytes 786440 | tf_op jit(solution)/shard_map/down1c1/ppermute | solution.py:367
  20.9 2.3 %collective-permute-done.3.refs_2_ = bf16[512,256]{1,0:T(8,128)(2,1)S(1)} collective-permute-done((bf16[512,256]{1,0:T(8,128)(2,1)S(1)}, bf16[512,256]{1,0:T(8,128)(2,1)S(1)}, u32[]{:S(2)}, u32[]{:S(2)}) %collective-permute-start.3) | collective-permute-done | bytes 262176 | tf_op jit(solution)/shard_map/down0c0/ppermute | solution.py:367
  23.1 2.0 %collective-permute-done.2.refs_1_ = bf16[512,256]{1,0:T(8,128)(2,1)S(1)} collective-permute-done((bf16[512,256]{1,0:T(8,128)(2,1)S(1)}, bf16[512,256]{1,0:T(8,128)(2,1)S(1)}, u32[]{:S(2)}, u32[]{:S(2)}) %collective-permute-start.2) | collective-permute-done | bytes 262176 | tf_op jit(solution)/shard_map/up0c0/ppermute | solution.py:365
  25.2 1.9 %collective-permute-start.5 = (bf16[512,256]{1,0:T(8,128)(2,1)S(1)}, bf16[512,256]{1,0:T(8,128)(2,1)S(1)}, u32[]{:S(2)}, u32[]{:S(2)}) collective-permute-start(bf16[512,256]{1,0:T(8,128)(2,1)S(1)} %collective-permute-done.3.refs_2_), channel_id=1, source_target_pairs={{4,0},{8,4},{12,8},{14,12},{10,14},{6,10},{2,6},{0,2},{5,1},{9,5},... | collective-permute-start | bytes 786440 | tf_op jit(solution)/shard_map/down2c0/ppermute | solution.py:367
  28.0 2.5 %collective-permute-done.6.refs_1_ = bf16[512,256]{1,0:T(8,128)(2,1)S(1)} collective-permute-done((bf16[512,256]{1,0:T(8,128)(2,1)S(1)}, bf16[512,256]{1,0:T(8,128)(2,1)S(1)}, u32[]{:S(2)}, u32[]{:S(2)}) %collective-permute-start.6) | collective-permute-done | bytes 262176 | tf_op jit(solution)/shard_map/up1c1/ppermute | solution.py:365
  30.5 2.0 %collective-permute-start.11 = (bf16[512,256]{1,0:T(8,128)(2,1)S(1)}, bf16[512,256]{1,0:T(8,128)(2,1)S(1)}, u32[]{:S(2)}, u32[]{:S(2)}) collective-permute-start(bf16[512,256]{1,0:T(8,128)(2,1)S(1)} %collective-permute-done.7.refs_2_), channel_id=1, source_target_pairs={{4,0},{8,4},{12,8},{14,12},{10,14},{6,10},{2,6},{0,2},{5,1},{9,5},... | collective-permute-start | bytes 786440 | tf_op jit(solution)/shard_map/down3c1/ppermute | solution.py:367
  32.5 3.6 %collective-permute-done.4.refs_3_ = bf16[512,256]{1,0:T(8,128)(2,1)S(1)} collective-permute-done((bf16[512,256]{1,0:T(8,128)(2,1)S(1)}, bf16[512,256]{1,0:T(8,128)(2,1)S(1)}, u32[]{:S(2)}, u32[]{:S(2)}) %collective-permute-start.4) | collective-permute-done | bytes 262176 | tf_op jit(solution)/shard_map/up2c0/ppermute | solution.py:365
  36.4 1.7 %collective-permute-start.9 = (bf16[512,256]{1,0:T(8,128)(2,1)S(1)}, bf16[512,256]{1,0:T(8,128)(2,1)S(1)}, u32[]{:S(2)}, u32[]{:S(2)}) collective-permute-start(bf16[512,256]{1,0:T(8,128)(2,1)S(1)} %collective-permute-done.5.refs_4_), channel_id=1, source_target_pairs={{4,0},{8,4},{12,8},{14,12},{10,14},{6,10},{2,6},{0,2},{5,1},{9,5},... | collective-permute-start | bytes 786440 | tf_op jit(solution)/shard_map/down4c0/ppermute | solution.py:367
  38.2 3.6 %collective-permute-done.10.refs_3_ = bf16[512,256]{1,0:T(8,128)(2,1)S(1)} collective-permute-done((bf16[512,256]{1,0:T(8,128)(2,1)S(1)}, bf16[512,256]{1,0:T(8,128)(2,1)S(1)}, u32[]{:S(2)}, u32[]{:S(2)}) %collective-permute-start.10) | collective-permute-done | bytes 262176 | tf_op jit(solution)/shard_map/up3c1/ppermute | solution.py:365
  42.0 1.7 %collective-permute-start.15 = (bf16[512,256]{1,0:T(8,128)(2,1)S(1)}, bf16[512,256]{1,0:T(8,128)(2,1)S(1)}, u32[]{:S(2)}, u32[]{:S(2)}) collective-permute-start(bf16[512,256]{1,0:T(8,128)(2,1)S(1)} %collective-permute-done.11.refs_4_), channel_id=1, source_target_pairs={{4,0},{8,4},{12,8},{14,12},{10,14},{6,10},{2,6},{0,2},{5,1},{9,5},... | collective-permute-start | bytes 786440 | tf_op jit(solution)/shard_map/down5c1/ppermute | solution.py:367
  43.8 3.6 %collective-permute-done.8.refs_5_ = bf16[512,256]{1,0:T(8,128)(2,1)S(1)} collective-permute-done((bf16[512,256]{1,0:T(8,128)(2,1)S(1)}, bf16[512,256]{1,0:T(8,128)(2,1)S(1)}, u32[]{:S(2)}, u32[]{:S(2)}) %collective-permute-start.8) | collective-permute-done | bytes 262176 | tf_op jit(solution)/shard_map/up4c0/ppermute | solution.py:365
  47.4 5.6 %collective-permute-done.14.refs_5_ = bf16[512,256]{1,0:T(8,128)(2,1)S(1)} collective-permute-done((bf16[512,256]{1,0:T(8,128)(2,1)S(1)}, bf16[512,256]{1,0:T(8,128)(2,1)S(1)}, u32[]{:S(2)}, u32[]{:S(2)}) %collective-permute-start.14) | collective-permute-done | bytes 262176 | tf_op jit(solution)/shard_map/up5c1/ppermute | solution.py:365
  53.3 1.8 %collective-permute-start.17 = (bf16[512,256]{1,0:T(8,128)(2,1)S(1)}, bf16[512,256]{1,0:T(8,128)(2,1)S(1)}, u32[]{:S(2)}, u32[]{:S(2)}) collective-permute-start(bf16[512,256]{1,0:T(8,128)(2,1)S(1)} %get-tuple-element.81), channel_id=1, source_target_pairs={{4,0},{8,4},{12,8},{14,12},{10,14},{6,10},{2,6},{0,2},{5,1},{9,5},... | collective-permute-start | bytes 786440 | tf_op jit(solution)/shard_map/down7c2/ppermute | solution.py:367
  55.4 1.8 %collective-permute-start.13 = (bf16[256,256]{1,0:T(8,128)(2,1)S(1)}, bf16[256,256]{1,0:T(8,128)(2,1)S(1)}, u32[]{:S(2)}, u32[]{:S(2)}) collective-permute-start(bf16[256,256]{1,0:T(8,128)(2,1)S(1)} %slice.51), channel_id=1, source_target_pairs={{4,0},{8,4},{12,8},{14,12},{10,14},{6,10},{2,6},{0,2},{5,1},{9,5},... | collective-permute-start | bytes 393224 | tf_op jit(solution)/shard_map/down6c0/ppermute | solution.py:367
  57.2 5.9 %collective-permute-done.12.refs_7_ = bf16[256,256]{1,0:T(8,128)(2,1)S(1)} collective-permute-done((bf16[256,256]{1,0:T(8,128)(2,1)S(1)}, bf16[256,256]{1,0:T(8,128)(2,1)S(1)}, u32[]{:S(2)}, u32[]{:S(2)}) %collective-permute-start.12) | collective-permute-done | bytes 131104 | tf_op jit(solution)/shard_map/up6c0/ppermute | solution.py:365
  63.6 1.8 %collective-permute-start.21 = (bf16[256,256]{1,0:T(8,128)(2,1)S(1)}, bf16[256,256]{1,0:T(8,128)(2,1)S(1)}, u32[]{:S(2)}, u32[]{:S(2)}) collective-permute-start(bf16[256,256]{1,0:T(8,128)(2,1)S(1)} %slice.53), channel_id=1, source_target_pairs={{0,4},{4,8},{8,12},{12,14},{14,10},{10,6},{6,2},{2,0},{1,5},{5,9},... | collective-permute-start | bytes 393224 | tf_op jit(solution)/shard_map/up8c1/ppermute | solution.py:365
  65.6 1.8 %collective-permute-start.18 = (bf16[512,256]{1,0:T(8,128)(2,1)S(1)}, bf16[512,256]{1,0:T(8,128)(2,1)S(1)}, u32[]{:S(2)}, u32[]{:S(2)}) collective-permute-start(bf16[512,256]{1,0:T(8,128)(2,1)S(1)} %collective-permute-done.16.refs_1_), channel_id=1, source_target_pairs={{0,4},{4,8},{8,12},{12,14},{14,10},{10,6},{6,2},{2,0},{1,5},{5,9},... | collective-permute-start | bytes 786440 | tf_op jit(solution)/shard_map/up9c2/ppermute | solution.py:365
  67.6 1.7 %mix.4 = (bf16[5,512,256]{2,1,0:T(8,128)(2,1)S(1)}, bf16[5,512,256]{2,1,0:T(8,128)(2,1)S(1)}) custom-call(bf16[2048,256]{1,0:T(8,128)(2,1)S(1)} %copy-done, bf16[512,256]{1,0:T(8,128)(2,1)S(1)} %collective-permute-done.2.refs_1_, bf16[512,256]{1,0:T(8,128)(2,1)S(1)} %collective-permute-done.3.refs_2_, bf16[512,256]{1,0:T(8,128)(2,1)S(1)} %collective-permute-done.4.refs_3_, ...), custom_call_target="tpu_custom_call" | custom-call | flops 20000000000 | bytes 1024 | tf_op jit(solution)/shard_map/mix/pallas_call | solution.py:209
  69.4 2.1 %collective-permute-done.22.refs_8_ = bf16[256,256]{1,0:T(8,128)(2,1)S(1)} collective-permute-done((bf16[256,256]{1,0:T(8,128)(2,1)S(1)}, bf16[256,256]{1,0:T(8,128)(2,1)S(1)}, u32[]{:S(2)}, u32[]{:S(2)}) %collective-permute-start.22) | collective-permute-done | bytes 131104 | tf_op jit(solution)/shard_map/down8c1/ppermute | solution.py:367
  75.1 2.1 %collective-permute-done.19.refs_4_ = bf16[512,256]{1,0:T(8,128)(2,1)S(1)} collective-permute-done((bf16[512,256]{1,0:T(8,128)(2,1)S(1)}, bf16[512,256]{1,0:T(8,128)(2,1)S(1)}, u32[]{:S(2)}, u32[]{:S(2)}) %collective-permute-start.19) | collective-permute-done | bytes 262176 | tf_op jit(solution)/shard_map/down9c2/ppermute | solution.py:367
  79.2 1.7 %mix.5 = (bf16[5,512,256]{2,1,0:T(8,128)(2,1)S(1)}, bf16[5,512,256]{2,1,0:T(8,128)(2,1)S(1)}) custom-call(bf16[2048,256]{1,0:T(8,128)(2,1)S(1)} %copy-done, bf16[512,256]{1,0:T(8,128)(2,1)S(1)} %collective-permute-done.6.refs_1_, bf16[512,256]{1,0:T(8,128)(2,1)S(1)} %collective-permute-done.7.refs_2_, bf16[512,256]{1,0:T(8,128)(2,1)S(1)} %collective-permute-done.10.refs_3_, ...), custom_call_target="tpu_custom_call" | custom-call | flops 20000000000 | bytes 1024 | tf_op jit(solution)/shard_map/mix/pallas_call | solution.py:209
  80.9 5.5 %collective-permute-done.23.refs_5_ = bf16[512,256]{1,0:T(8,128)(2,1)S(1)} collective-permute-done((bf16[512,256]{1,0:T(8,128)(2,1)S(1)}, bf16[512,256]{1,0:T(8,128)(2,1)S(1)}, u32[]{:S(2)}, u32[]{:S(2)}) %collective-permute-start.23) | collective-permute-done | bytes 262176 | tf_op jit(solution)/shard_map/up11c2/ppermute | solution.py:365
  88.4 3.0 %gram0.1.refs_0_ = bf16[4,2048,2048]{2,1,0:T(8,128)(2,1)} custom-call(bf16[5,512,256]{2,1,0:T(8,128)(2,1)S(1)} %get-tuple-element.94.refs_0_.refs_2_.refs_1_.refs_5_.refs_7_.refs_9_, bf16[5,512,256]{2,1,0:T(8,128)(2,1)S(1)} %collective-permute-done.20.refs_1_.refs_3_.refs_7_.refs_4_.refs_10_.refs_5_.refs_13_, ...), custom_call_target="tpu_custom_call" | custom-call | flops 20000000000 | bytes 1024 | tf_op jit(solution)/shard_map/gram0/pallas_call | solution.py:301
  93.6 5.0 %gram1.1.refs_0_ = bf16[4,2048,2048]{2,1,0:T(8,128)(2,1)} custom-call(bf16[4,2048,2048]{2,1,0:T(8,128)(2,1)} %gram0.1.refs_0_, bf16[5,512,256]{2,1,0:T(8,128)(2,1)S(1)} %get-tuple-element.94.refs_0_.refs_2_.refs_1_.refs_5_.refs_7_.refs_9_, ...), custom_call_target="tpu_custom_call", output_to_operand_aliasing={{}: (0, {})} | custom-call | flops 20000000000 | bytes 1024 | tf_op jit(solution)/shard_map/gram1/pallas_call | solution.py:301
  105.3 5.8 %collective-permute-done.28.refs_7_ = bf16[256,256]{1,0:T(8,128)(2,1)S(1)} collective-permute-done((bf16[256,256]{1,0:T(8,128)(2,1)S(1)}, bf16[256,256]{1,0:T(8,128)(2,1)S(1)}, u32[]{:S(2)}, u32[]{:S(2)}) %collective-permute-start.28) | collective-permute-done | bytes 131104 | tf_op jit(solution)/shard_map/up13c2/ppermute | solution.py:365
  114.6 1.7 %mix.6 = (bf16[5,512,256]{2,1,0:T(8,128)(2,1)S(1)}, bf16[5,512,256]{2,1,0:T(8,128)(2,1)S(1)}) custom-call(bf16[2048,256]{1,0:T(8,128)(2,1)S(1)} %copy-done, bf16[512,256]{1,0:T(8,128)(2,1)S(1)} %collective-permute-done.16.refs_1_, bf16[512,256]{1,0:T(8,128)(2,1)S(1)} %collective-permute-done.17.refs_2_, ...), custom_call_target="tpu_custom_call" | custom-call | flops 20000000000 | bytes 1024 | tf_op jit(solution)/shard_map/mix/pallas_call | solution.py:209
  119.0 1.9 %mix.7 = (bf16[5,512,256]{2,1,0:T(8,128)(2,1)S(1)}, bf16[5,512,256]{2,1,0:T(8,128)(2,1)S(1)}) custom-call(bf16[2048,256]{1,0:T(8,128)(2,1)S(1)} %copy-done, bf16[512,256]{1,0:T(8,128)(2,1)S(1)} %collective-permute-done.26.refs_1_, bf16[512,256]{1,0:T(8,128)(2,1)S(1)} %collective-permute-done.27.refs_2_, ...), custom_call_target="tpu_custom_call" | custom-call | flops 20000000000 | bytes 1024 | tf_op jit(solution)/shard_map/mix/pallas_call | solution.py:209
  121.0 7.3 %gram2.1.refs_0_ = bf16[4,2048,2048]{2,1,0:T(8,128)(2,1)} custom-call(bf16[4,2048,2048]{2,1,0:T(8,128)(2,1)} %gram1.1.refs_0_, bf16[5,512,256]{2,1,0:T(8,128)(2,1)S(1)} %get-tuple-element.94.refs_0_.refs_2_.refs_1_.refs_5_.refs_7_.refs_9_, ...), custom_call_target="tpu_custom_call", output_to_operand_aliasing={{}: (0, {})} | custom-call | flops 20000000000 | bytes 1024 | tf_op jit(solution)/shard_map/gram2/pallas_call | solution.py:301
  128.4 9.7 %gram3.1 = bf16[4,2048,2048]{2,1,0:T(8,128)(2,1)} custom-call(bf16[4,2048,2048]{2,1,0:T(8,128)(2,1)} %gram2.1.refs_0_, bf16[5,512,256]{2,1,0:T(8,128)(2,1)S(1)} %get-tuple-element.94.refs_0_.refs_2_.refs_1_.refs_5_.refs_7_.refs_9_, bf16[5,512,256]{2,1,0:T(8,128)(2,1)S(1)} %get-tuple-element.110.refs_2_.refs_6_.refs_8_.refs_10_, ...), custom_call_target="tpu_custom_call", output_to_operand_aliasing={{}: (0, {})} | custom-call | flops 20000000000 | bytes 1024 | tf_op jit(solution)/shard_map/gram3/pallas_call | solution.py:301
  (68 shorter events, 31.1 us)
Async XLA Ops:
  16.3 6.8 %collective-permute-start.3 = (bf16[512,256]{1,0:T(8,128)(2,1)S(1)}, bf16[512,256]{1,0:T(8,128)(2,1)S(1)}, u32[]{:S(2)}, u32[]{:S(2)}) collective-permute-start(bf16[512,256]{1,0:T(8,128)(2,1)S(1)} %get-tuple-element.138), channel_id=1, source_target_pairs={{4,0},{8,4},{12,8},{14,12},{10,14},{6,10},{2,6},{0,2},{5,1},{9,5},... | collective-permute-start | bytes 786440 | tf_op jit(solution)/shard_map/down0c0/ppermute | solution.py:367
  18.7 6.4 %collective-permute-start.2 = (bf16[512,256]{1,0:T(8,128)(2,1)S(1)}, bf16[512,256]{1,0:T(8,128)(2,1)S(1)}, u32[]{:S(2)}, u32[]{:S(2)}) collective-permute-start(bf16[512,256]{1,0:T(8,128)(2,1)S(1)} %get-tuple-element.138), channel_id=1, source_target_pairs={{0,4},{4,8},{8,12},{12,14},{14,10},{10,6},{6,2},{2,0},{1,5},{5,9},... | collective-permute-start | bytes 786440 | tf_op jit(solution)/shard_map/up0c0/ppermute | solution.py:365
  18.8 9.1 %collective-permute-start.7 = (bf16[512,256]{1,0:T(8,128)(2,1)S(1)}, bf16[512,256]{1,0:T(8,128)(2,1)S(1)}, u32[]{:S(2)}, u32[]{:S(2)}) collective-permute-start(bf16[512,256]{1,0:T(8,128)(2,1)S(1)} %get-tuple-element.137), channel_id=1, source_target_pairs={{4,0},{8,4},{12,8},{14,12},{10,14},{6,10},{2,6},{0,2},{5,1},{9,5},... | collective-permute-start | bytes 786440 | tf_op jit(solution)/shard_map/down1c1/ppermute | solution.py:367
  20.7 9.8 %collective-permute-start.6 = (bf16[512,256]{1,0:T(8,128)(2,1)S(1)}, bf16[512,256]{1,0:T(8,128)(2,1)S(1)}, u32[]{:S(2)}, u32[]{:S(2)}) collective-permute-start(bf16[512,256]{1,0:T(8,128)(2,1)S(1)} %get-tuple-element.137), channel_id=1, source_target_pairs={{0,4},{4,8},{8,12},{12,14},{14,10},{10,6},{6,2},{2,0},{1,5},{5,9},... | collective-permute-start | bytes 786440 | tf_op jit(solution)/shard_map/up1c1/ppermute | solution.py:365
  25.1 11.0 %collective-permute-start.4 = (bf16[512,256]{1,0:T(8,128)(2,1)S(1)}, bf16[512,256]{1,0:T(8,128)(2,1)S(1)}, u32[]{:S(2)}, u32[]{:S(2)}) collective-permute-start(bf16[512,256]{1,0:T(8,128)(2,1)S(1)} %collective-permute-done.2.refs_1_), channel_id=1, source_target_pairs={{0,4},{4,8},{8,12},{12,14},{14,10},{10,6},{6,2},{2,0},{1,5},{5,9},... | collective-permute-start | bytes 786440 | tf_op jit(solution)/shard_map/up2c0/ppermute | solution.py:365
  25.2 10.9 %collective-permute-start.5 = (bf16[512,256]{1,0:T(8,128)(2,1)S(1)}, bf16[512,256]{1,0:T(8,128)(2,1)S(1)}, u32[]{:S(2)}, u32[]{:S(2)}) collective-permute-start(bf16[512,256]{1,0:T(8,128)(2,1)S(1)} %collective-permute-done.3.refs_2_), channel_id=1, source_target_pairs={{4,0},{8,4},{12,8},{14,12},{10,14},{6,10},{2,6},{0,2},{5,1},{9,5},... | collective-permute-start | bytes 786440 | tf_op jit(solution)/shard_map/down2c0/ppermute | solution.py:367
  30.5 11.2 %collective-permute-start.10 = (bf16[512,256]{1,0:T(8,128)(2,1)S(1)}, bf16[512,256]{1,0:T(8,128)(2,1)S(1)}, u32[]{:S(2)}, u32[]{:S(2)}) collective-permute-start(bf16[512,256]{1,0:T(8,128)(2,1)S(1)} %collective-permute-done.6.refs_1_), channel_id=1, source_target_pairs={{0,4},{4,8},{8,12},{12,14},{14,10},{10,6},{6,2},{2,0},{1,5},{5,9},... | collective-permute-start | bytes 786440 | tf_op jit(solution)/shard_map/up3c1/ppermute | solution.py:365
  30.5 11.2 %collective-permute-start.11 = (bf16[512,256]{1,0:T(8,128)(2,1)S(1)}, bf16[512,256]{1,0:T(8,128)(2,1)S(1)}, u32[]{:S(2)}, u32[]{:S(2)}) collective-permute-start(bf16[512,256]{1,0:T(8,128)(2,1)S(1)} %collective-permute-done.7.refs_2_), channel_id=1, source_target_pairs={{4,0},{8,4},{12,8},{14,12},{10,14},{6,10},{2,6},{0,2},{5,1},{9,5},... | collective-permute-start | bytes 786440 | tf_op jit(solution)/shard_map/down3c1/ppermute | solution.py:367
  36.1 11.2 %collective-permute-start.8 = (bf16[512,256]{1,0:T(8,128)(2,1)S(1)}, bf16[512,256]{1,0:T(8,128)(2,1)S(1)}, u32[]{:S(2)}, u32[]{:S(2)}) collective-permute-start(bf16[512,256]{1,0:T(8,128)(2,1)S(1)} %collective-permute-done.4.refs_3_), channel_id=1, source_target_pairs={{0,4},{4,8},{8,12},{12,14},{14,10},{10,6},{6,2},{2,0},{1,5},{5,9},... | collective-permute-start | bytes 786440 | tf_op jit(solution)/shard_map/up4c0/ppermute | solution.py:365
  36.4 11.0 %collective-permute-start.9 = (bf16[512,256]{1,0:T(8,128)(2,1)S(1)}, bf16[512,256]{1,0:T(8,128)(2,1)S(1)}, u32[]{:S(2)}, u32[]{:S(2)}) collective-permute-start(bf16[512,256]{1,0:T(8,128)(2,1)S(1)} %collective-permute-done.5.refs_4_), channel_id=1, source_target_pairs={{4,0},{8,4},{12,8},{14,12},{10,14},{6,10},{2,6},{0,2},{5,1},{9,5},... | collective-permute-start | bytes 786440 | tf_op jit(solution)/shard_map/down4c0/ppermute | solution.py:367
  41.8 11.2 %collective-permute-start.14 = (bf16[512,256]{1,0:T(8,128)(2,1)S(1)}, bf16[512,256]{1,0:T(8,128)(2,1)S(1)}, u32[]{:S(2)}, u32[]{:S(2)}) collective-permute-start(bf16[512,256]{1,0:T(8,128)(2,1)S(1)} %collective-permute-done.10.refs_3_), channel_id=1, source_target_pairs={{0,4},{4,8},{8,12},{12,14},{14,10},{10,6},{6,2},{2,0},{1,5},{5,9},... | collective-permute-start | bytes 786440 | tf_op jit(solution)/shard_map/up5c1/ppermute | solution.py:365
  42.0 11.0 %collective-permute-start.15 = (bf16[512,256]{1,0:T(8,128)(2,1)S(1)}, bf16[512,256]{1,0:T(8,128)(2,1)S(1)}, u32[]{:S(2)}, u32[]{:S(2)}) collective-permute-start(bf16[512,256]{1,0:T(8,128)(2,1)S(1)} %collective-permute-done.11.refs_4_), channel_id=1, source_target_pairs={{4,0},{8,4},{12,8},{14,12},{10,14},{6,10},{2,6},{0,2},{5,1},{9,5},... | collective-permute-start | bytes 786440 | tf_op jit(solution)/shard_map/down5c1/ppermute | solution.py:367
  53.0 12.6 %collective-permute-start.16 = (bf16[512,256]{1,0:T(8,128)(2,1)S(1)}, bf16[512,256]{1,0:T(8,128)(2,1)S(1)}, u32[]{:S(2)}, u32[]{:S(2)}) collective-permute-start(bf16[512,256]{1,0:T(8,128)(2,1)S(1)} %get-tuple-element.81), channel_id=1, source_target_pairs={{0,4},{4,8},{8,12},{12,14},{14,10},{10,6},{6,2},{2,0},{1,5},{5,9},... | collective-permute-start | bytes 786440 | tf_op jit(solution)/shard_map/up7c2/ppermute | solution.py:365
  53.3 12.3 %collective-permute-start.17 = (bf16[512,256]{1,0:T(8,128)(2,1)S(1)}, bf16[512,256]{1,0:T(8,128)(2,1)S(1)}, u32[]{:S(2)}, u32[]{:S(2)}) collective-permute-start(bf16[512,256]{1,0:T(8,128)(2,1)S(1)} %get-tuple-element.81), channel_id=1, source_target_pairs={{4,0},{8,4},{12,8},{14,12},{10,14},{6,10},{2,6},{0,2},{5,1},{9,5},... | collective-permute-start | bytes 786440 | tf_op jit(solution)/shard_map/down7c2/ppermute | solution.py:367
  55.1 8.0 %collective-permute-start.12 = (bf16[256,256]{1,0:T(8,128)(2,1)S(1)}, bf16[256,256]{1,0:T(8,128)(2,1)S(1)}, u32[]{:S(2)}, u32[]{:S(2)}) collective-permute-start(bf16[256,256]{1,0:T(8,128)(2,1)S(1)} %slice.50), channel_id=1, source_target_pairs={{0,4},{4,8},{8,12},{12,14},{14,10},{10,6},{6,2},{2,0},{1,5},{5,9},... | collective-permute-start | bytes 393224 | tf_op jit(solution)/shard_map/up6c0/ppermute | solution.py:365
  55.4 8.2 %collective-permute-start.13 = (bf16[256,256]{1,0:T(8,128)(2,1)S(1)}, bf16[256,256]{1,0:T(8,128)(2,1)S(1)}, u32[]{:S(2)}, u32[]{:S(2)}) collective-permute-start(bf16[256,256]{1,0:T(8,128)(2,1)S(1)} %slice.51), channel_id=1, source_target_pairs={{4,0},{8,4},{12,8},{14,12},{10,14},{6,10},{2,6},{0,2},{5,1},{9,5},... | collective-permute-start | bytes 393224 | tf_op jit(solution)/shard_map/down6c0/ppermute | solution.py:367
  65.4 6.1 %collective-permute-start.22 = (bf16[256,256]{1,0:T(8,128)(2,1)S(1)}, bf16[256,256]{1,0:T(8,128)(2,1)S(1)}, u32[]{:S(2)}, u32[]{:S(2)}) collective-permute-start(bf16[256,256]{1,0:T(8,128)(2,1)S(1)} %slice.54), channel_id=1, source_target_pairs={{4,0},{8,4},{12,8},{14,12},{10,14},{6,10},{2,6},{0,2},{5,1},{9,5},... | collective-permute-start | bytes 393224 | tf_op jit(solution)/shard_map/down8c1/ppermute | solution.py:367
  65.6 9.5 %collective-permute-start.18 = (bf16[512,256]{1,0:T(8,128)(2,1)S(1)}, bf16[512,256]{1,0:T(8,128)(2,1)S(1)}, u32[]{:S(2)}, u32[]{:S(2)}) collective-permute-start(bf16[512,256]{1,0:T(8,128)(2,1)S(1)} %collective-permute-done.16.refs_1_), channel_id=1, source_target_pairs={{0,4},{4,8},{8,12},{12,14},{14,10},{10,6},{6,2},{2,0},{1,5},{5,9},... | collective-permute-start | bytes 786440 | tf_op jit(solution)/shard_map/up9c2/ppermute | solution.py:365
  67.4 9.7 %collective-permute-start.19 = (bf16[512,256]{1,0:T(8,128)(2,1)S(1)}, bf16[512,256]{1,0:T(8,128)(2,1)S(1)}, u32[]{:S(2)}, u32[]{:S(2)}) collective-permute-start(bf16[512,256]{1,0:T(8,128)(2,1)S(1)} %collective-permute-done.17.refs_2_), channel_id=1, source_target_pairs={{4,0},{8,4},{12,8},{14,12},{10,14},{6,10},{2,6},{0,2},{5,1},{9,5},... | collective-permute-start | bytes 786440 | tf_op jit(solution)/shard_map/down9c2/ppermute | solution.py:367
  71.5 19.9 %collective-permute-start.26 = (bf16[512,256]{1,0:T(8,128)(2,1)S(1)}, bf16[512,256]{1,0:T(8,128)(2,1)S(1)}, u32[]{:S(2)}, u32[]{:S(2)}) collective-permute-start(bf16[512,256]{1,0:T(8,128)(2,1)S(1)} %get-tuple-element.113), channel_id=1, source_target_pairs={{0,4},{4,8},{8,12},{12,14},{14,10},{10,6},{6,2},{2,0},{1,5},{5,9},... | collective-permute-start | bytes 786440 | tf_op jit(solution)/shard_map/up10c3/ppermute | solution.py:365
  73.1 18.3 %collective-permute-start.27 = (bf16[512,256]{1,0:T(8,128)(2,1)S(1)}, bf16[512,256]{1,0:T(8,128)(2,1)S(1)}, u32[]{:S(2)}, u32[]{:S(2)}) collective-permute-start(bf16[512,256]{1,0:T(8,128)(2,1)S(1)} %get-tuple-element.113), channel_id=1, source_target_pairs={{4,0},{8,4},{12,8},{14,12},{10,14},{6,10},{2,6},{0,2},{5,1},{9,5},... | collective-permute-start | bytes 786440 | tf_op jit(solution)/shard_map/down10c3/ppermute | solution.py:367
  73.6 14.8 %collective-permute-start.20 = (bf16[5,512,256]{2,1,0:T(8,128)(2,1)S(1)}, bf16[5,512,256]{2,1,0:T(8,128)(2,1)S(1)}, u32[]{:S(2)}, u32[]{:S(2)}) collective-permute-start(bf16[5,512,256]{2,1,0:T(8,128)(2,1)S(1)} %get-tuple-element.95), channel_id=1, source_target_pairs={{0,1},{1,0},{2,3},{3,2},{4,5},{5,4},{6,7},{7,6},{8,9},{9,8},{10,11... | collective-permute-start | bytes 3932168 | tf_op jit(solution)/shard_map/swap0/ppermute | solution.py:386
  77.2 9.2 %collective-permute-start.23 = (bf16[512,256]{1,0:T(8,128)(2,1)S(1)}, bf16[512,256]{1,0:T(8,128)(2,1)S(1)}, u32[]{:S(2)}, u32[]{:S(2)}) collective-permute-start(bf16[512,256]{1,0:T(8,128)(2,1)S(1)} %collective-permute-done.18.refs_3_), channel_id=1, source_target_pairs={{0,4},{4,8},{8,12},{12,14},{14,10},{10,6},{6,2},{2,0},{1,5},{5,9},... | collective-permute-start | bytes 786440 | tf_op jit(solution)/shard_map/up11c2/ppermute | solution.py:365
  78.8 9.6 %collective-permute-start.24 = (bf16[512,256]{1,0:T(8,128)(2,1)S(1)}, bf16[512,256]{1,0:T(8,128)(2,1)S(1)}, u32[]{:S(2)}, u32[]{:S(2)}) collective-permute-start(bf16[512,256]{1,0:T(8,128)(2,1)S(1)} %collective-permute-done.19.refs_4_), channel_id=1, source_target_pairs={{4,0},{8,4},{12,8},{14,12},{10,14},{6,10},{2,6},{0,2},{5,1},{9,5},... | collective-permute-start | bytes 786440 | tf_op jit(solution)/shard_map/down11c2/ppermute | solution.py:367
  86.4 7.1 %collective-permute-start.25 = (bf16[5,512,256]{2,1,0:T(8,128)(2,1)S(1)}, bf16[5,512,256]{2,1,0:T(8,128)(2,1)S(1)}, u32[]{:S(2)}, u32[]{:S(2)}) collective-permute-start(bf16[5,512,256]{2,1,0:T(8,128)(2,1)S(1)} %get-tuple-element.111), channel_id=1, source_target_pairs={{0,1},{1,0},{2,3},{3,2},{4,5},{5,4},{6,7},{7,6},{8,9},{9,8},{10,11... | collective-permute-start | bytes 3932168 | tf_op jit(solution)/shard_map/swap1/ppermute | solution.py:386
  91.5 8.4 %collective-permute-start.30 = (bf16[512,256]{1,0:T(8,128)(2,1)S(1)}, bf16[512,256]{1,0:T(8,128)(2,1)S(1)}, u32[]{:S(2)}, u32[]{:S(2)}) collective-permute-start(bf16[512,256]{1,0:T(8,128)(2,1)S(1)} %collective-permute-done.26.refs_1_), channel_id=1, source_target_pairs={{0,4},{4,8},{8,12},{12,14},{14,10},{10,6},{6,2},{2,0},{1,5},{5,9},... | collective-permute-start | bytes 786440 | tf_op jit(solution)/shard_map/up12c3/ppermute | solution.py:365
  93.1 8.0 %collective-permute-start.31 = (bf16[512,256]{1,0:T(8,128)(2,1)S(1)}, bf16[512,256]{1,0:T(8,128)(2,1)S(1)}, u32[]{:S(2)}, u32[]{:S(2)}) collective-permute-start(bf16[512,256]{1,0:T(8,128)(2,1)S(1)} %collective-permute-done.27.refs_2_), channel_id=1, source_target_pairs={{4,0},{8,4},{12,8},{14,12},{10,14},{6,10},{2,6},{0,2},{5,1},{9,5},... | collective-permute-start | bytes 786440 | tf_op jit(solution)/shard_map/down12c3/ppermute | solution.py:367
  101.2 11.3 %collective-permute-start.32 = (bf16[512,256]{1,0:T(8,128)(2,1)S(1)}, bf16[512,256]{1,0:T(8,128)(2,1)S(1)}, u32[]{:S(2)}, u32[]{:S(2)}) collective-permute-start(bf16[512,256]{1,0:T(8,128)(2,1)S(1)} %collective-permute-done.30.refs_3_), channel_id=1, source_target_pairs={{0,4},{4,8},{8,12},{12,14},{14,10},{10,6},{6,2},{2,0},{1,5},{5,9},... | collective-permute-start | bytes 786440 | tf_op jit(solution)/shard_map/up14c3/ppermute | solution.py:365
  102.7 9.7 %collective-permute-start.33 = (bf16[512,256]{1,0:T(8,128)(2,1)S(1)}, bf16[512,256]{1,0:T(8,128)(2,1)S(1)}, u32[]{:S(2)}, u32[]{:S(2)}) collective-permute-start(bf16[512,256]{1,0:T(8,128)(2,1)S(1)} %collective-permute-done.31.refs_4_), channel_id=1, source_target_pairs={{4,0},{8,4},{12,8},{14,12},{10,14},{6,10},{2,6},{0,2},{5,1},{9,5},... | collective-permute-start | bytes 786440 | tf_op jit(solution)/shard_map/down14c3/ppermute | solution.py:367
  103.2 7.9 %collective-permute-start.28 = (bf16[256,256]{1,0:T(8,128)(2,1)S(1)}, bf16[256,256]{1,0:T(8,128)(2,1)S(1)}, u32[]{:S(2)}, u32[]{:S(2)}) collective-permute-start(bf16[256,256]{1,0:T(8,128)(2,1)S(1)} %slice.55), channel_id=1, source_target_pairs={{0,4},{4,8},{8,12},{12,14},{14,10},{10,6},{6,2},{2,0},{1,5},{5,9},... | collective-permute-start | bytes 393224 | tf_op jit(solution)/shard_map/up13c2/ppermute | solution.py:365
  104.9 7.6 %collective-permute-start.29 = (bf16[256,256]{1,0:T(8,128)(2,1)S(1)}, bf16[256,256]{1,0:T(8,128)(2,1)S(1)}, u32[]{:S(2)}, u32[]{:S(2)}) collective-permute-start(bf16[256,256]{1,0:T(8,128)(2,1)S(1)} %slice.56), channel_id=1, source_target_pairs={{4,0},{8,4},{12,8},{14,12},{10,14},{6,10},{2,6},{0,2},{5,1},{9,5},... | collective-permute-start | bytes 393224 | tf_op jit(solution)/shard_map/down13c2/ppermute | solution.py:367
  120.9 7.4 %collective-permute-start.37 = (bf16[5,512,256]{2,1,0:T(8,128)(2,1)S(1)}, bf16[5,512,256]{2,1,0:T(8,128)(2,1)S(1)}, u32[]{:S(2)}, u32[]{:S(2)}) collective-permute-start(bf16[5,512,256]{2,1,0:T(8,128)(2,1)S(1)} %get-tuple-element.134), channel_id=1, source_target_pairs={{0,1},{1,0},{2,3},{3,2},{4,5},{5,4},{6,7},{7,6},{8,9},{9,8},{10,11... | collective-permute-start | bytes 3932168 | tf_op jit(solution)/shard_map/swap3/ppermute | solution.py:386
  (9 other events, 82.5 us)

commit v2 on v1

--- a/solution.py
+++ b/solution.py
@@ -11,9 +11,9 @@
 HEADS = 128
 DH = 128
 MIB = 1024 * 1024
-ATTEND_UNROLL = 4
-MIX_WAIT, MIX_DUE = 1, 4
-GRAM_WAIT, GRAM_DUE = 3, 6
+ATTEND_UNROLL = 8
+DEPTH = 3
+GATES = {"mix": (1, 4), "swap": (2, 5), "gram": (3, 6)}
 
 
 def butterfly(tiles):
@@ -42,7 +42,9 @@
     return jnp.where(place < devices // 2, 2 * place, 2 * (devices - 1 - place) + 1)
 
 
-def attend_kernel(kv_share, unroll, q_hbm, ko_hbm, vo_hbm, sign_hbm, kp_any, vp_any, out_ref, *scratch):
+def attend_kernel(kv_share, unroll, heads_of, q_hbm, ko_hbm, vo_hbm, sign_hbm, kp_any, vp_any, *scratch):
+    out_refs, scratch = scratch[: len(heads_of)], scratch[len(heads_of) :]
+    homes = [(ref, h) for ref, count in zip(out_refs, heads_of) for h in range(count)]
     q_ref, kv_ref, sign_ref, inner_ref, vt_ref, bar_ref, sem = scratch
     rows, width = q_ref.shape
     heads = width // DH
@@ -118,19 +120,20 @@
         for lane in range(0, rows, 128):
             tiles = [inner_ref[h, band, lane : lane + 128].astype(jnp.float32) for h in range(heads)]
             for h, tile in enumerate(butterfly(tiles)):
-                at = pl.ds(pl.multiple_of(h * DH + block * 16, 16), 16)
+                out_ref, slot = homes[h]
+                at = pl.ds(pl.multiple_of(slot * DH + block * 16, 16), 16)
                 out_ref[at, lane : lane + 128] = (tile * shrink).astype(jnp.bfloat16)
 
 
-def attend(queries, own_keys, own_values, signs, prev_keys, prev_values):
+def attend(heads_of, queries, own_keys, own_values, signs, prev_keys, prev_values):
     rows, width = queries.shape
     kv_share = HEADS // (own_keys.shape[1] // DH)
     heads = width // DH
     hbm, anywhere = pl.BlockSpec(memory_space=pltpu.HBM), pl.BlockSpec(memory_space=pl.ANY)
     return pl.pallas_call(
-        functools.partial(attend_kernel, kv_share, ATTEND_UNROLL),
+        functools.partial(attend_kernel, kv_share, ATTEND_UNROLL, heads_of),
         in_specs=[hbm] * 4 + [anywhere] * 2,
-        out_specs=pl.BlockSpec(memory_space=pltpu.VMEM),
+        out_specs=[pl.BlockSpec(memory_space=pltpu.VMEM)] * len(heads_of),
         scratch_shapes=[
             pltpu.VMEM((rows, width), jnp.bfloat16),
             pltpu.VMEM((4, rows, DH), jnp.bfloat16),
@@ -140,14 +143,14 @@
             pltpu.VMEM((rows, rows), jnp.float32),
             pltpu.SemaphoreType.DMA((6,)),
         ],
-        out_shape=jax.ShapeDtypeStruct((width, rows), jnp.bfloat16),
+        out_shape=[jax.ShapeDtypeStruct((count * DH, rows), jnp.bfloat16) for count in heads_of],
         compiler_params=pltpu.CompilerParams(vmem_limit_bytes=60 * MIB),
         cost_estimate=pl.CostEstimate(flops=20000000000, bytes_accessed=1024, transcendentals=0),
         name="attend",
     )(queries, own_keys, own_values, signs, prev_keys, prev_values)
 
 
-def mix_kernel(devices, offset, *refs):
+def mix_kernel(devices, scale, *refs):
     count = devices + 1
     pieces, (keep_ref, send_ref, held, sem) = refs[:count], refs[count:]
     rows = keep_ref.shape[1]
@@ -160,7 +163,7 @@
     copies = []
     for p, piece in enumerate(pieces):
         if p == 0:
-            source, target = piece.at[pl.ds(offset, rows), :], held.at[slots[0]]
+            source, target = piece, held.at[slots[0]]
         elif p < devices - 1:
             source, target = piece, held.at[slots[p]]
         else:
@@ -191,23 +194,23 @@
 
     @pl.when(in_keep)
     def _():
-        strip = keep_ref[own_slot]
+        strip = (keep_ref[own_slot] * scale).astype(jnp.bfloat16)
         keep_ref[half] = strip
         send_ref[half] = strip
 
     @pl.when(jnp.logical_not(in_keep))
     def _():
-        strip = send_ref[own_slot]
+        strip = (send_ref[own_slot] * scale).astype(jnp.bfloat16)
         keep_ref[half] = strip
         send_ref[half] = strip
 
 
-def mix(devices, offset, rows, own, pieces):
-    lanes = own.shape[1]
+def mix(devices, scale, own, pieces):
+    rows, lanes = own.shape
     half = devices // 2
     shape = (half + 1, rows, lanes)
     return pl.pallas_call(
-        functools.partial(mix_kernel, devices, offset),
+        functools.partial(mix_kernel, devices, scale),
         in_specs=[pl.BlockSpec(memory_space=pl.ANY)] * (devices + 1),
         out_specs=[pl.BlockSpec(memory_space=pltpu.VMEM)] * 2,
         scratch_shapes=[
@@ -221,13 +224,13 @@
     )(own, *pieces)
 
 
-def gram_kernel(starts, sizes, chunk, scale, aliased, *refs):
+def gram_kernel(starts, sizes, chunk, aliased, *refs):
     refs = list(refs)
     take = lambda n: [refs.pop(0) for _ in range(n)]
     if aliased:
         take(1)
-    keep_rows, recv_rows = take(chunk + 1), take(chunk + 1)
-    keep_cols, recv_cols = take(chunk + 1), take(chunk + 1)
+    keeps, recvs = take(chunk + 1), take(chunk + 1)
+    half = keeps[0].shape[0] - 1
     (out_ref,) = take(1)
     wide, sem = take(2)
     tall = take(1)[0] if chunk else None
@@ -251,29 +254,21 @@
         if chunk:
             tall_copy(r - 2, slot).wait()
 
-    def block(a_keep, a_recv, b_keep, b_recv, store):
-        height, width = a_keep.shape[1], b_keep.shape[1]
-        tile_m = math.gcd(height, 256)
-        tile_n = math.gcd(width, 512)
+    def block(up, across, target, top, left):
+        height, width = sizes[up], sizes[across]
+        tile_m, tile_n = math.gcd(height, 1024), math.gcd(width, 256)
         for i in range(0, height, tile_m):
-            left, left_other = a_keep[0, i : i + tile_m, :], a_recv[0, i : i + tile_m, :]
+            rows, rows_other = keeps[up][r, i : i + tile_m, :], recvs[up][r, i : i + tile_m, :]
             for k in range(0, width, tile_n):
-                total = nt_dot(left, b_keep[0, k : k + tile_n, :]) + nt_dot(left_other, b_recv[0, k : k + tile_n, :])
-                store(i, tile_m, k, tile_n, (total * scale).astype(jnp.bfloat16))
+                total = nt_dot(rows, keeps[across][half, k : k + tile_n, :])
+                total += nt_dot(rows_other, recvs[across][half, k : k + tile_n, :])
+                target[slot, top + i : top + i + tile_m, left + k : left + k + tile_n] = total.astype(jnp.bfloat16)
 
     for c in range(chunk + 1):
-
-        def store_wide(i, m, k, n, value):
-            wide[slot, i : i + m, starts[c] + k : starts[c] + k + n] = value
-
-        block(keep_rows[chunk], recv_rows[chunk], keep_cols[c], recv_cols[c], store_wide)
+        block(chunk, c, wide, 0, starts[c])
     wide_copy(r, slot).start()
     for c in range(chunk):
-
-        def store_tall(i, m, k, n, value):
-            tall[slot, starts[c] + i : starts[c] + i + m, k : k + n] = value
-
-        block(keep_rows[c], recv_rows[c], keep_cols[chunk], recv_cols[chunk], store_tall)
+        block(c, chunk, tall, starts[c], 0)
     if chunk:
         tall_copy(r, slot).start()
 
@@ -286,12 +281,10 @@
                 tall_copy(at, lax.rem(at, 2)).wait()
 
 
-def gram(out, keeps, recvs, starts, sizes, chunk, scale, shape):
+def gram(out, keeps, recvs, starts, sizes, chunk, shape):
     half = keeps[0].shape[0] - 1
     lanes = keeps[0].shape[2]
     first, size = starts[chunk], sizes[chunk]
-    row_spec = [pl.BlockSpec((1, sizes[c], lanes), lambda r: (r, 0, 0)) for c in range(chunk + 1)]
-    col_spec = [pl.BlockSpec((1, sizes[c], lanes), lambda r: (half, 0, 0)) for c in range(chunk + 1)]
     aliased = out is not None
     anywhere = pl.BlockSpec(memory_space=pl.ANY)
     scratch = [pltpu.VMEM((2, size, first + size), jnp.bfloat16), pltpu.SemaphoreType.DMA((2, 2))]
@@ -299,9 +292,9 @@
         scratch.append(pltpu.VMEM((2, first, size), jnp.bfloat16))
     area = half * (size * (first + size) + first * size)
     return pl.pallas_call(
-        functools.partial(gram_kernel, starts, sizes, chunk, scale, aliased),
+        functools.partial(gram_kernel, starts, sizes, chunk, aliased),
         grid=(half,),
-        in_specs=([anywhere] if aliased else []) + row_spec * 2 + col_spec * 2,
+        in_specs=([anywhere] if aliased else []) + [pl.BlockSpec(memory_space=pltpu.VMEM)] * (2 * chunk + 2),
         out_specs=anywhere,
         out_shape=jax.ShapeDtypeStruct(shape, jnp.bfloat16),
         scratch_shapes=scratch,
@@ -309,10 +302,10 @@
         compiler_params=pltpu.CompilerParams(vmem_limit_bytes=40 * MIB),
         cost_estimate=pl.CostEstimate(flops=20000000000, bytes_accessed=1024, transcendentals=0),
         name=f"gram{chunk}",
-    )(*(([out] if aliased else []) + keeps + recvs + keeps + recvs))
-
-
-PLANS = {(16, 4): ([4, 4, 4, 4], [0, 1, 0, 1, 0, 1, 0, 2, 1, 2, 3, 2, 3, 2, 3, 3])}
+    )(*(([out] if aliased else []) + keeps + recvs))
+
+
+PLANS = {(16, 4): ([4, 4, 4, 4], [0,1,0,1,0,2,1,0,2,1,3,2,3,2,3,3])}
 
 
 def plan(local_heads, hops):
@@ -343,22 +336,42 @@
     forward = [(order[i], order[(i + 1) % devices]) for i in range(devices)]
     backward = [(b, a) for a, b in forward]
     prev_keys, prev_values = lax.ppermute((key_rows, values), "tok", [(0, 1)])
-    mixed = attend(queries, key_rows, values, sign_bits.reshape(HEADS, DH), prev_keys, prev_values)
-
     heads_of, sequence = plan(width // DH, half)
+    mixed = attend(heads_of, queries, key_rows, values, sign_bits.reshape(HEADS, DH), prev_keys, prev_values)
     sizes = [c * DH for c in heads_of]
     chunks = len(sizes)
     starts = [sum(sizes[:c]) for c in range(chunks)]
-    held = [[mixed[starts[c] : starts[c] + sizes[c]]] * 2 for c in range(chunks)]
+    held = [[block, block] for block in mixed]
     pieces = [[] for _ in range(chunks)]
     scale = 2.0 / (rows * tok_count)
     keeps, recvs, out = [None] * chunks, [None] * chunks, None
-    landed, due, pending = [], {}, []
+    landed, due, sends = [], {}, [None] * chunks
+
+    def compute(kind, c, waits):
+        nonlocal out
+        if kind == "mix":
+            own = mixed[c]
+            if waits:
+                own, pieces[c] = after((own, pieces[c]), *waits)
+            keeps[c], sends[c] = mix(devices, scale, own, pieces[c])
+            return keeps[c]
+        if kind == "swap":
+            if waits:
+                sends[c] = after((sends[c],), *waits)[0]
+            with jax.named_scope(f"swap{c}"):
+                recvs[c] = lax.ppermute(sends[c], "tok", [(0, 1), (1, 0)])
+            return recvs[c]
+        if waits:
+            keeps[c] = after((keeps[c],), *waits)[0]
+        out = gram(out, keeps[: c + 1], recvs[: c + 1], starts, sizes, c, (half, width, width))
+        return out
+
+    pending = []
     for k, c in enumerate(sequence):
         going, coming = held[c]
         if len(pieces[c]) == 2 * (half - 1):
             going, coming = going[: sizes[c] // 2], coming[sizes[c] // 2 :]
-        waits = landed[max(0, k - 3) : max(0, k - 1)] + due.pop(k, [])
+        waits = landed[max(0, k - DEPTH - 1) : max(0, k - DEPTH + 1)] + due.pop(k, [])
         if waits:
             going, coming = after((going, coming), *waits)
         with jax.named_scope(f"up{k}c{c}"):
@@ -369,29 +382,15 @@
         held[c] = [going, coming]
         pieces[c] += [going, coming]
         if len(pieces[c]) == 2 * half:
-            pending.append(("mix", c, k + MIX_WAIT, k + MIX_DUE))
-            pending.append(("gram", c, k + GRAM_WAIT, k + GRAM_DUE))
-        final = k == len(sequence) - 1
+            for kind, (ready, deadline) in GATES.items():
+                pending.append((kind, c, k + ready, k + deadline))
         for task in list(pending):
             kind, which, ready, deadline = task
-            if ready > k and not final:
-                continue
-            pending.remove(task)
-            if kind == "mix":
-                own = mixed
-                if not final:
-                    own, pieces[which] = after((mixed, pieces[which]), landed[k])
-                keeps[which], send = mix(devices, starts[which], sizes[which], own, pieces[which])
-                with jax.named_scope(f"swap{which}"):
-                    recvs[which] = lax.ppermute(send, "tok", [(0, 1), (1, 0)])
-                done = keeps[which]
-            else:
-                n = which + 1
-                if not final:
-                    keeps[which] = after((keeps[which],), landed[k])[0]
-                out = gram(out, keeps[:n], recvs[:n], starts, sizes, which, scale, (half, width, width))
-                done = out
-            due.setdefault(deadline, []).append(done)
+            if ready == k:
+                pending.remove(task)
+                due.setdefault(deadline, []).append(compute(kind, which, [landed[k]]))
+    for kind, which, _, _ in pending:
+        compute(kind, which, [])
     return out.reshape(half * width, width)
 
 

time: 138 us -> 129 us (0.935)
  waiting for transfers between devices: 57.3 us -> 43 us
  starting transfers between devices: 37.5 us -> 42.2 us
    ppermute x16, waiting for transfers between devices: 42.1 us -> 31.7 us  [local(): going = lax.ppermute(going, 'head', forward)]
    ppermute x16, starting transfers between devices: 14.8 us -> 6.15 us  [local(): going = lax.ppermute(going, 'head', forward)]
    ppermute x16, starting transfers between devices: 18.3 us -> 26.3 us  [local(): coming = lax.ppermute(coming, 'head', backward)]
    ppermute x4, starting transfers between devices: 0.64 us -> 5.99 us  [compute(): recvs[c] = lax.ppermute(sends[c], 'tok', [(0, 1), (1, 0)])]
    ppermute x16, waiting for transfers between devices: 13.4 us -> 9.08 us  [local(): coming = lax.ppermute(coming, 'head', backward)]
  transfers between devices with their start and end apart: 38 -> 38, of which waited for: 24 -> 21; matrix products, arithmetic and copies ran while one was open for 0% -> 0% of each run, Pallas kernels for 16% -> 18%
where the time goes in v2:
time: 129 us; the launch traced here: 128 us
  waiting for transfers between devices  43 us (33%)
  starting transfers between devices  42.2 us (33%)
  Pallas kernels  41.1 us (32%)
  local copies, waits for them, and re-layouts  1.84 us (1%)
    ppermute x16, waiting for transfers between devices, local(): going = lax.ppermute(going, 'head', forward)  31.7 us
    ppermute x16, starting transfers between devices, local(): coming = lax.ppermute(coming, 'head', backward)  26.3 us
    pallas_call x4, Pallas kernels, gram(): pl.pallas_call(functools.partial(gram_kernel, starts, sizes, chunk, alias...  25.6 us
    ppermute x16, waiting for transfers between devices, local(): coming = lax.ppermute(coming, 'head', backward)  9.08 us
    pallas_call x1, Pallas kernels, attend(): pl.pallas_call(functools.partial(attend_kernel, kv_share, ATTEND_UNROLL,...  8.26 us
    pallas_call x4, Pallas kernels, mix(): pl.pallas_call(functools.partial(mix_kernel, devices, scale), in_specs=[p...  7.21 us
    ppermute x16, starting transfers between devices, local(): going = lax.ppermute(going, 'head', forward)  6.15 us
    ppermute x4, starting transfers between devices, compute(): recvs[c] = lax.ppermute(sends[c], 'tok', [(0, 1), (1, 0)])  5.99 us
  transfers between devices with their start and end apart: 38, of which 21 were waited for; matrix products, arithmetic and copies ran while one was open for 0% of the time, Pallas kernels for 18%

profile of v2, /device:TPU:0, one launch (start us, length us, event | category | flops | bytes accessed | tf_op | source)
XLA Modules:
  0.0 128.4 jit_solution(10654607974231775983)
XLA Ops:
  0.0 2.4 %collective-permute-start = (bf16[256,1024]{1,0:T(8,128)(2,1)}, bf16[256,1024]{1,0:T(8,128)(2,1)S(1)}, u32[]{:S(2)}, u32[]{:S(2)}) collective-permute-start(bf16[256,1024]{1,0:T(8,128)(2,1)} %ko_hbm.1), channel_id=1, source_target_pairs={{0,1},{2,3},{4,5},{6,7},{8,9},{10,11},{12,13},{14,15},{16,17},{18,... | collective-permute-start | bytes 1572872 | tf_op jit(solution)/shard_map/ppermute | solution.py:338
  6.2 8.3 %attend.1 = (bf16[512,256]{1,0:T(8,128)(2,1)}, bf16[512,256]{1,0:T(8,128)(2,1)}, bf16[512,256]{1,0:T(8,128)(2,1)}, bf16[512,256]{1,0:T(8,128)(2,1)}) custom-call(bf16[256,2048]{1,0:T(8,128)(2,1)} %q_hbm.1, bf16[256,1024]{1,0:T(8,128)(2,1)} %ko_hbm.1, bf16[256,1024]{1,0:T(8,128)(2,1)} %vo_hbm.1, s32[128,128]{1,0:T(8,128)} %bitcast.2, ...), custom_call_target="tpu_custom_call" | custom-call | flops 20000000000 | bytes 1024 | tf_op jit(solution)/shard_map/attend/pallas_call | solution.py:133
  14.5 2.4 %collective-permute-start.3 = (bf16[512,256]{1,0:T(8,128)(2,1)}, bf16[512,256]{1,0:T(8,128)(2,1)S(1)}, u32[]{:S(2)}, u32[]{:S(2)}) collective-permute-start(bf16[512,256]{1,0:T(8,128)(2,1)} %get-tuple-element.88.refs_0_), channel_id=1, source_target_pairs={{4,0},{8,4},{12,8},{14,12},{10,14},{6,10},{2,6},{0,2},{5,1},{9,5},... | collective-permute-start | bytes 786440 | tf_op jit(solution)/shard_map/down0c0/ppermute | solution.py:380
  17.0 1.9 %collective-permute-start.7 = (bf16[512,256]{1,0:T(8,128)(2,1)}, bf16[512,256]{1,0:T(8,128)(2,1)S(1)}, u32[]{:S(2)}, u32[]{:S(2)}) collective-permute-start(bf16[512,256]{1,0:T(8,128)(2,1)} %get-tuple-element.108.refs_0_), channel_id=1, source_target_pairs={{4,0},{8,4},{12,8},{14,12},{10,14},{6,10},{2,6},{0,2},{5,1},{9,5},... | collective-permute-start | bytes 786440 | tf_op jit(solution)/shard_map/down1c1/ppermute | solution.py:380
  19.0 2.5 %collective-permute-done.3.refs_2_ = bf16[512,256]{1,0:T(8,128)(2,1)S(1)} collective-permute-done((bf16[512,256]{1,0:T(8,128)(2,1)}, bf16[512,256]{1,0:T(8,128)(2,1)S(1)}, u32[]{:S(2)}, u32[]{:S(2)}) %collective-permute-start.3) | collective-permute-done | bytes 262176 | tf_op jit(solution)/shard_map/down0c0/ppermute | solution.py:380
  21.5 2.0 %collective-permute-start.5 = (bf16[512,256]{1,0:T(8,128)(2,1)S(1)}, bf16[512,256]{1,0:T(8,128)(2,1)S(1)}, u32[]{:S(2)}, u32[]{:S(2)}) collective-permute-start(bf16[512,256]{1,0:T(8,128)(2,1)S(1)} %collective-permute-done.3.refs_2_), channel_id=1, source_target_pairs={{4,0},{8,4},{12,8},{14,12},{10,14},{6,10},{2,6},{0,2},{5,1},{9,5},... | collective-permute-start | bytes 786440 | tf_op jit(solution)/shard_map/down2c0/ppermute | solution.py:380
  23.6 2.7 %collective-permute-done.7.refs_2_ = bf16[512,256]{1,0:T(8,128)(2,1)S(1)} collective-permute-done((bf16[512,256]{1,0:T(8,128)(2,1)}, bf16[512,256]{1,0:T(8,128)(2,1)S(1)}, u32[]{:S(2)}, u32[]{:S(2)}) %collective-permute-start.7) | collective-permute-done | bytes 262176 | tf_op jit(solution)/shard_map/down1c1/ppermute | solution.py:380
  26.2 2.5 %collective-permute-done.6.refs_1_ = bf16[512,256]{1,0:T(8,128)(2,1)S(1)} collective-permute-done((bf16[512,256]{1,0:T(8,128)(2,1)}, bf16[512,256]{1,0:T(8,128)(2,1)S(1)}, u32[]{:S(2)}, u32[]{:S(2)}) %collective-permute-start.6) | collective-permute-done | bytes 262176 | tf_op jit(solution)/shard_map/up1c1/ppermute | solution.py:378
  28.8 2.0 %collective-permute-start.11 = (bf16[512,256]{1,0:T(8,128)(2,1)S(1)}, bf16[512,256]{1,0:T(8,128)(2,1)S(1)}, u32[]{:S(2)}, u32[]{:S(2)}) collective-permute-start(bf16[512,256]{1,0:T(8,128)(2,1)S(1)} %collective-permute-done.7.refs_2_), channel_id=1, source_target_pairs={{4,0},{8,4},{12,8},{14,12},{10,14},{6,10},{2,6},{0,2},{5,1},{9,5},... | collective-permute-start | bytes 786440 | tf_op jit(solution)/shard_map/down3c1/ppermute | solution.py:380
  31.9 2.5 %collective-permute-done.4.refs_3_ = bf16[512,256]{1,0:T(8,128)(2,1)S(1)} collective-permute-done((bf16[512,256]{1,0:T(8,128)(2,1)S(1)}, bf16[512,256]{1,0:T(8,128)(2,1)S(1)}, u32[]{:S(2)}, u32[]{:S(2)}) %collective-permute-start.4) | collective-permute-done | bytes 262176 | tf_op jit(solution)/shard_map/up2c0/ppermute | solution.py:378
  34.4 2.0 %collective-permute-start.9 = (bf16[512,256]{1,0:T(8,128)(2,1)S(1)}, bf16[512,256]{1,0:T(8,128)(2,1)S(1)}, u32[]{:S(2)}, u32[]{:S(2)}) collective-permute-start(bf16[512,256]{1,0:T(8,128)(2,1)S(1)} %collective-permute-done.5.refs_4_), channel_id=1, source_target_pairs={{4,0},{8,4},{12,8},{14,12},{10,14},{6,10},{2,6},{0,2},{5,1},{9,5},... | collective-permute-start | bytes 786440 | tf_op jit(solution)/shard_map/down4c0/ppermute | solution.py:380
  36.5 3.6 %collective-permute-done.10.refs_3_ = bf16[512,256]{1,0:T(8,128)(2,1)S(1)} collective-permute-done((bf16[512,256]{1,0:T(8,128)(2,1)S(1)}, bf16[512,256]{1,0:T(8,128)(2,1)S(1)}, u32[]{:S(2)}, u32[]{:S(2)}) %collective-permute-start.10) | collective-permute-done | bytes 262176 | tf_op jit(solution)/shard_map/up3c1/ppermute | solution.py:378
  42.0 3.6 %collective-permute-done.8.refs_5_ = bf16[512,256]{1,0:T(8,128)(2,1)S(1)} collective-permute-done((bf16[512,256]{1,0:T(8,128)(2,1)S(1)}, bf16[512,256]{1,0:T(8,128)(2,1)S(1)}, u32[]{:S(2)}, u32[]{:S(2)}) %collective-permute-start.8) | collective-permute-done | bytes 262176 | tf_op jit(solution)/shard_map/up4c0/ppermute | solution.py:378
  47.2 4.0 %collective-permute-done.14.refs_1_ = bf16[512,256]{1,0:T(8,128)(2,1)S(1)} collective-permute-done((bf16[512,256]{1,0:T(8,128)(2,1)}, bf16[512,256]{1,0:T(8,128)(2,1)S(1)}, u32[]{:S(2)}, u32[]{:S(2)}) %collective-permute-start.14) | collective-permute-done | bytes 262176 | tf_op jit(solution)/shard_map/up5c2/ppermute | solution.py:378
  51.3 2.0 %collective-permute-start.17 = (bf16[512,256]{1,0:T(8,128)(2,1)S(1)}, bf16[512,256]{1,0:T(8,128)(2,1)S(1)}, u32[]{:S(2)}, u32[]{:S(2)}) collective-permute-start(bf16[512,256]{1,0:T(8,128)(2,1)S(1)} %collective-permute-done.15.refs_2_), channel_id=1, source_target_pairs={{4,0},{8,4},{12,8},{14,12},{10,14},{6,10},{2,6},{0,2},{5,1},{9,5},... | collective-permute-start | bytes 786440 | tf_op jit(solution)/shard_map/down8c2/ppermute | solution.py:380
  53.4 3.4 %collective-permute-done.18.refs_5_ = bf16[512,256]{1,0:T(8,128)(2,1)S(1)} collective-permute-done((bf16[512,256]{1,0:T(8,128)(2,1)S(1)}, bf16[512,256]{1,0:T(8,128)(2,1)S(1)}, u32[]{:S(2)}, u32[]{:S(2)}) %collective-permute-start.18) | collective-permute-done | bytes 262176 | tf_op jit(solution)/shard_map/up6c1/ppermute | solution.py:378
  59.0 6.3 %collective-permute-done.12.refs_7_ = bf16[256,256]{1,0:T(8,128)(2,1)S(1)} collective-permute-done((bf16[256,256]{1,0:T(8,128)(2,1)S(1)}, bf16[256,256]{1,0:T(8,128)(2,1)S(1)}, u32[]{:S(2)}, u32[]{:S(2)}) %collective-permute-start.12) | collective-permute-done | bytes 131104 | tf_op jit(solution)/shard_map/up7c0/ppermute | solution.py:378
  69.9 1.7 %mix.4 = (bf16[5,512,256]{2,1,0:T(8,128)(2,1)S(1)}, bf16[5,512,256]{2,1,0:T(8,128)(2,1)S(1)}) custom-call(bf16[512,256]{1,0:T(8,128)(2,1)S(1)} %copy-done.3, bf16[512,256]{1,0:T(8,128)(2,1)S(1)} %collective-permute-done.2.refs_1_, bf16[512,256]{1,0:T(8,128)(2,1)S(1)} %collective-permute-done.3.refs_2_, bf16[512,256]{1,0:T(8,128)(2,1)S(1)} %collective-permute-done.4.refs_3_, ...), custom_call_target="tpu_custom_call" | custom-call | flops 20000000000 | bytes 1024 | tf_op jit(solution)/shard_map/mix/pallas_call | solution.py:212
  73.7 3.2 %collective-permute-start.24 = (bf16[5,512,256]{2,1,0:T(8,128)(2,1)S(1)}, bf16[5,512,256]{2,1,0:T(8,128)(2,1)S(1)}, u32[]{:S(2)}, u32[]{:S(2)}) collective-permute-start(bf16[5,512,256]{2,1,0:T(8,128)(2,1)S(1)} %get-tuple-element.107), channel_id=1, source_target_pairs={{0,1},{1,0},{2,3},{3,2},{4,5},{5,4},{6,7},{7,6},{8,9},{9,8},{10,11... | collective-permute-start | bytes 3932168 | tf_op jit(solution)/shard_map/swap0/ppermute | solution.py:362
  77.0 1.8 %mix.5 = (bf16[5,512,256]{2,1,0:T(8,128)(2,1)S(1)}, bf16[5,512,256]{2,1,0:T(8,128)(2,1)S(1)}) custom-call(bf16[512,256]{1,0:T(8,128)(2,1)S(1)} %copy-done.2, bf16[512,256]{1,0:T(8,128)(2,1)S(1)} %collective-permute-done.6.refs_1_, bf16[512,256]{1,0:T(8,128)(2,1)S(1)} %collective-permute-done.7.refs_2_, bf16[512,256]{1,0:T(8,128)(2,1)S(1)} %collective-permute-done.10.refs_3_, ...), custom_call_target="tpu_custom_call" | custom-call | flops 20000000000 | bytes 1024 | tf_op jit(solution)/shard_map/mix/pallas_call | solution.py:212
  78.8 2.1 %collective-permute-done.27.refs_5_ = bf16[512,256]{1,0:T(8,128)(2,1)S(1)} collective-permute-done((bf16[512,256]{1,0:T(8,128)(2,1)S(1)}, bf16[512,256]{1,0:T(8,128)(2,1)S(1)}, u32[]{:S(2)}, u32[]{:S(2)}) %collective-permute-start.27) | collective-permute-done | bytes 262176 | tf_op jit(solution)/shard_map/up11c2/ppermute | solution.py:378
  81.4 2.2 %collective-permute-start.29 = (bf16[5,512,256]{2,1,0:T(8,128)(2,1)S(1)}, bf16[5,512,256]{2,1,0:T(8,128)(2,1)S(1)}, u32[]{:S(2)}, u32[]{:S(2)}) collective-permute-start(bf16[5,512,256]{2,1,0:T(8,128)(2,1)S(1)} %get-tuple-element.124), channel_id=1, source_target_pairs={{0,1},{1,0},{2,3},{3,2},{4,5},{5,4},{6,7},{7,6},{8,9},{9,8},{10,11... | collective-permute-start | bytes 3932168 | tf_op jit(solution)/shard_map/swap1/ppermute | solution.py:362
  83.8 1.9 %collective-permute-start.26 = (bf16[512,256]{1,0:T(8,128)(2,1)S(1)}, bf16[512,256]{1,0:T(8,128)(2,1)S(1)}, u32[]{:S(2)}, u32[]{:S(2)}) collective-permute-start(bf16[512,256]{1,0:T(8,128)(2,1)S(1)} %collective-permute-done.21.refs_2_), channel_id=1, source_target_pairs={{4,0},{8,4},{12,8},{14,12},{10,14},{6,10},{2,6},{0,2},{5,1},{9,5},... | collective-permute-start | bytes 786440 | tf_op jit(solution)/shard_map/down12c3/ppermute | solution.py:380
  85.7 3.0 %gram0.1.refs_0_ = bf16[4,2048,2048]{2,1,0:T(8,128)(2,1)} custom-call(bf16[5,512,256]{2,1,0:T(8,128)(2,1)S(1)} %get-tuple-element.103.refs_0_.refs_1_, bf16[5,512,256]{2,1,0:T(8,128)(2,1)S(1)} %collective-permute-done.24.refs_1_.refs_3_.refs_4_.refs_5_), custom_call_target="tpu_custom_call" | custom-call | flops 20000000000 | bytes 1024 | tf_op jit(solution)/shard_map/gram0/pallas_call | solution.py:294
  88.9 1.9 %collective-permute-start.31 = (bf16[256,256]{1,0:T(8,128)(2,1)S(1)}, bf16[256,256]{1,0:T(8,128)(2,1)S(1)}, u32[]{:S(2)}, u32[]{:S(2)}) collective-permute-start(bf16[256,256]{1,0:T(8,128)(2,1)S(1)} %slice.37), channel_id=1, source_target_pairs={{4,0},{8,4},{12,8},{14,12},{10,14},{6,10},{2,6},{0,2},{5,1},{9,5},... | collective-permute-start | bytes 393224 | tf_op jit(solution)/shard_map/down13c2/ppermute | solution.py:380
  90.8 2.0 %collective-permute-done.25.refs_3_ = bf16[512,256]{1,0:T(8,128)(2,1)S(1)} collective-permute-done((bf16[512,256]{1,0:T(8,128)(2,1)S(1)}, bf16[512,256]{1,0:T(8,128)(2,1)S(1)}, u32[]{:S(2)}, u32[]{:S(2)}) %collective-permute-start.25) | collective-permute-done | bytes 262176 | tf_op jit(solution)/shard_map/up12c3/ppermute | solution.py:378
  92.9 1.7 %collective-permute-start.32 = (bf16[512,256]{1,0:T(8,128)(2,1)S(1)}, bf16[512,256]{1,0:T(8,128)(2,1)S(1)}, u32[]{:S(2)}, u32[]{:S(2)}) collective-permute-start(bf16[512,256]{1,0:T(8,128)(2,1)S(1)} %collective-permute-done.25.refs_3_), channel_id=1, source_target_pairs={{0,4},{4,8},{8,12},{12,14},{14,10},{10,6},{6,2},{2,0},{1,5},{5,9},... | collective-permute-start | bytes 786440 | tf_op jit(solution)/shard_map/up14c3/ppermute | solution.py:378
  95.0 5.0 %gram1.1.refs_0_ = bf16[4,2048,2048]{2,1,0:T(8,128)(2,1)} custom-call(bf16[4,2048,2048]{2,1,0:T(8,128)(2,1)} %gram0.1.refs_0_, bf16[5,512,256]{2,1,0:T(8,128)(2,1)S(1)} %get-tuple-element.103.refs_0_.refs_1_, bf16[5,512,256]{2,1,0:T(8,128)(2,1)S(1)} %get-tuple-element.120.refs_2_, ...), custom_call_target="tpu_custom_call", output_to_operand_aliasing={{}: (0, {})} | custom-call | flops 20000000000 | bytes 1024 | tf_op jit(solution)/shard_map/gram1/pallas_call | solution.py:294
  103.1 1.7 %mix.6 = (bf16[5,512,256]{2,1,0:T(8,128)(2,1)S(1)}, bf16[5,512,256]{2,1,0:T(8,128)(2,1)S(1)}) custom-call(bf16[512,256]{1,0:T(8,128)(2,1)S(1)} %copy-done.1, bf16[512,256]{1,0:T(8,128)(2,1)S(1)} %collective-permute-done.14.refs_1_, bf16[512,256]{1,0:T(8,128)(2,1)S(1)} %collective-permute-done.15.refs_2_, ...), custom_call_target="tpu_custom_call" | custom-call | flops 20000000000 | bytes 1024 | tf_op jit(solution)/shard_map/mix/pallas_call | solution.py:212
  107.7 1.9 %mix.7 = (bf16[5,512,256]{2,1,0:T(8,128)(2,1)S(1)}, bf16[5,512,256]{2,1,0:T(8,128)(2,1)S(1)}) custom-call(bf16[512,256]{1,0:T(8,128)(2,1)S(1)} %copy-done, bf16[512,256]{1,0:T(8,128)(2,1)S(1)} %collective-permute-done.20.refs_1_, bf16[512,256]{1,0:T(8,128)(2,1)S(1)} %collective-permute-done.21.refs_2_, bf16[512,256]{1,0:T(8,128)(2,1)S(1)} %collective-permute-done.25.refs_3_, ...), custom_call_target="tpu_custom_call" | custom-call | flops 20000000000 | bytes 1024 | tf_op jit(solution)/shard_map/mix/pallas_call | solution.py:212
  110.7 7.5 %gram2.1.refs_0_ = bf16[4,2048,2048]{2,1,0:T(8,128)(2,1)} custom-call(bf16[4,2048,2048]{2,1,0:T(8,128)(2,1)} %gram1.1.refs_0_, bf16[5,512,256]{2,1,0:T(8,128)(2,1)S(1)} %get-tuple-element.103.refs_0_.refs_1_, bf16[5,512,256]{2,1,0:T(8,128)(2,1)S(1)} %get-tuple-element.120.refs_2_, ...), custom_call_target="tpu_custom_call", output_to_operand_aliasing={{}: (0, {})} | custom-call | flops 20000000000 | bytes 1024 | tf_op jit(solution)/shard_map/gram2/pallas_call | solution.py:294
  118.2 10.1 %gram3.1 = bf16[4,2048,2048]{2,1,0:T(8,128)(2,1)} custom-call(bf16[4,2048,2048]{2,1,0:T(8,128)(2,1)} %gram2.1.refs_0_, bf16[5,512,256]{2,1,0:T(8,128)(2,1)S(1)} %get-tuple-element.103.refs_0_.refs_1_, bf16[5,512,256]{2,1,0:T(8,128)(2,1)S(1)} %get-tuple-element.120.refs_2_, ...), custom_call_target="tpu_custom_call", output_to_operand_aliasing={{}: (0, {})} | custom-call | flops 20000000000 | bytes 1024 | tf_op jit(solution)/shard_map/gram3/pallas_call | solution.py:294
  (73 shorter events, 26.1 us)
Async XLA Ops:
  14.5 7.0 %collective-permute-start.3 = (bf16[512,256]{1,0:T(8,128)(2,1)}, bf16[512,256]{1,0:T(8,128)(2,1)S(1)}, u32[]{:S(2)}, u32[]{:S(2)}) collective-permute-start(bf16[512,256]{1,0:T(8,128)(2,1)} %get-tuple-element.88.refs_0_), channel_id=1, source_target_pairs={{4,0},{8,4},{12,8},{14,12},{10,14},{6,10},{2,6},{0,2},{5,1},{9,5},... | collective-permute-start | bytes 786440 | tf_op jit(solution)/shard_map/down0c0/ppermute | solution.py:380
  16.9 6.6 %collective-permute-start.2 = (bf16[512,256]{1,0:T(8,128)(2,1)}, bf16[512,256]{1,0:T(8,128)(2,1)S(1)}, u32[]{:S(2)}, u32[]{:S(2)}) collective-permute-start(bf16[512,256]{1,0:T(8,128)(2,1)} %get-tuple-element.88.refs_0_), channel_id=1, source_target_pairs={{0,4},{4,8},{8,12},{12,14},{14,10},{10,6},{6,2},{2,0},{1,5},{5,9},... | collective-permute-start | bytes 786440 | tf_op jit(solution)/shard_map/up0c0/ppermute | solution.py:378
  17.0 9.2 %collective-permute-start.7 = (bf16[512,256]{1,0:T(8,128)(2,1)}, bf16[512,256]{1,0:T(8,128)(2,1)S(1)}, u32[]{:S(2)}, u32[]{:S(2)}) collective-permute-start(bf16[512,256]{1,0:T(8,128)(2,1)} %get-tuple-element.108.refs_0_), channel_id=1, source_target_pairs={{4,0},{8,4},{12,8},{14,12},{10,14},{6,10},{2,6},{0,2},{5,1},{9,5},... | collective-permute-start | bytes 786440 | tf_op jit(solution)/shard_map/down1c1/ppermute | solution.py:380
  18.9 9.9 %collective-permute-start.6 = (bf16[512,256]{1,0:T(8,128)(2,1)}, bf16[512,256]{1,0:T(8,128)(2,1)S(1)}, u32[]{:S(2)}, u32[]{:S(2)}) collective-permute-start(bf16[512,256]{1,0:T(8,128)(2,1)} %get-tuple-element.108.refs_0_), channel_id=1, source_target_pairs={{0,4},{4,8},{8,12},{12,14},{14,10},{10,6},{6,2},{2,0},{1,5},{5,9},... | collective-permute-start | bytes 786440 | tf_op jit(solution)/shard_map/up1c1/ppermute | solution.py:378
  21.5 10.4 %collective-permute-start.5 = (bf16[512,256]{1,0:T(8,128)(2,1)S(1)}, bf16[512,256]{1,0:T(8,128)(2,1)S(1)}, u32[]{:S(2)}, u32[]{:S(2)}) collective-permute-start(bf16[512,256]{1,0:T(8,128)(2,1)S(1)} %collective-permute-done.3.refs_2_), channel_id=1, source_target_pairs={{4,0},{8,4},{12,8},{14,12},{10,14},{6,10},{2,6},{0,2},{5,1},{9,5},... | collective-permute-start | bytes 786440 | tf_op jit(solution)/shard_map/down2c0/ppermute | solution.py:380
  23.5 10.9 %collective-permute-start.4 = (bf16[512,256]{1,0:T(8,128)(2,1)S(1)}, bf16[512,256]{1,0:T(8,128)(2,1)S(1)}, u32[]{:S(2)}, u32[]{:S(2)}) collective-permute-start(bf16[512,256]{1,0:T(8,128)(2,1)S(1)} %collective-permute-done.2.refs_1_), channel_id=1, source_target_pairs={{0,4},{4,8},{8,12},{12,14},{14,10},{10,6},{6,2},{2,0},{1,5},{5,9},... | collective-permute-start | bytes 786440 | tf_op jit(solution)/shard_map/up2c0/ppermute | solution.py:378
  28.8 11.2 %collective-permute-start.10 = (bf16[512,256]{1,0:T(8,128)(2,1)S(1)}, bf16[512,256]{1,0:T(8,128)(2,1)S(1)}, u32[]{:S(2)}, u32[]{:S(2)}) collective-permute-start(bf16[512,256]{1,0:T(8,128)(2,1)S(1)} %collective-permute-done.6.refs_1_), channel_id=1, source_target_pairs={{0,4},{4,8},{8,12},{12,14},{14,10},{10,6},{6,2},{2,0},{1,5},{5,9},... | collective-permute-start | bytes 786440 | tf_op jit(solution)/shard_map/up3c1/ppermute | solution.py:378
  28.8 12.8 %collective-permute-start.11 = (bf16[512,256]{1,0:T(8,128)(2,1)S(1)}, bf16[512,256]{1,0:T(8,128)(2,1)S(1)}, u32[]{:S(2)}, u32[]{:S(2)}) collective-permute-start(bf16[512,256]{1,0:T(8,128)(2,1)S(1)} %collective-permute-done.7.refs_2_), channel_id=1, source_target_pairs={{4,0},{8,4},{12,8},{14,12},{10,14},{6,10},{2,6},{0,2},{5,1},{9,5},... | collective-permute-start | bytes 786440 | tf_op jit(solution)/shard_map/down3c1/ppermute | solution.py:380
  34.4 11.2 %collective-permute-start.8 = (bf16[512,256]{1,0:T(8,128)(2,1)S(1)}, bf16[512,256]{1,0:T(8,128)(2,1)S(1)}, u32[]{:S(2)}, u32[]{:S(2)}) collective-permute-start(bf16[512,256]{1,0:T(8,128)(2,1)S(1)} %collective-permute-done.4.refs_3_), channel_id=1, source_target_pairs={{0,4},{4,8},{8,12},{12,14},{14,10},{10,6},{6,2},{2,0},{1,5},{5,9},... | collective-permute-start | bytes 786440 | tf_op jit(solution)/shard_map/up4c0/ppermute | solution.py:378
  34.4 12.8 %collective-permute-start.9 = (bf16[512,256]{1,0:T(8,128)(2,1)S(1)}, bf16[512,256]{1,0:T(8,128)(2,1)S(1)}, u32[]{:S(2)}, u32[]{:S(2)}) collective-permute-start(bf16[512,256]{1,0:T(8,128)(2,1)S(1)} %collective-permute-done.5.refs_4_), channel_id=1, source_target_pairs={{4,0},{8,4},{12,8},{14,12},{10,14},{6,10},{2,6},{0,2},{5,1},{9,5},... | collective-permute-start | bytes 786440 | tf_op jit(solution)/shard_map/down4c0/ppermute | solution.py:380
  36.4 14.8 %collective-permute-start.14 = (bf16[512,256]{1,0:T(8,128)(2,1)}, bf16[512,256]{1,0:T(8,128)(2,1)S(1)}, u32[]{:S(2)}, u32[]{:S(2)}) collective-permute-start(bf16[512,256]{1,0:T(8,128)(2,1)} %get-tuple-element.129.refs_0_), channel_id=1, source_target_pairs={{0,4},{4,8},{8,12},{12,14},{14,10},{10,6},{6,2},{2,0},{1,5},{5,9},... | collective-permute-start | bytes 786440 | tf_op jit(solution)/shard_map/up5c2/ppermute | solution.py:378
  40.0 11.2 %collective-permute-start.15 = (bf16[512,256]{1,0:T(8,128)(2,1)}, bf16[512,256]{1,0:T(8,128)(2,1)S(1)}, u32[]{:S(2)}, u32[]{:S(2)}) collective-permute-start(bf16[512,256]{1,0:T(8,128)(2,1)} %get-tuple-element.129.refs_0_), channel_id=1, source_target_pairs={{4,0},{8,4},{12,8},{14,12},{10,14},{6,10},{2,6},{0,2},{5,1},{9,5},... | collective-permute-start | bytes 786440 | tf_op jit(solution)/shard_map/down5c2/ppermute | solution.py:380
  41.6 15.3 %collective-permute-start.18 = (bf16[512,256]{1,0:T(8,128)(2,1)S(1)}, bf16[512,256]{1,0:T(8,128)(2,1)S(1)}, u32[]{:S(2)}, u32[]{:S(2)}) collective-permute-start(bf16[512,256]{1,0:T(8,128)(2,1)S(1)} %collective-permute-done.10.refs_3_), channel_id=1, source_target_pairs={{0,4},{4,8},{8,12},{12,14},{14,10},{10,6},{6,2},{2,0},{1,5},{5,9},... | collective-permute-start | bytes 786440 | tf_op jit(solution)/shard_map/up6c1/ppermute | solution.py:378
  45.6 12.8 %collective-permute-start.19 = (bf16[512,256]{1,0:T(8,128)(2,1)S(1)}, bf16[512,256]{1,0:T(8,128)(2,1)S(1)}, u32[]{:S(2)}, u32[]{:S(2)}) collective-permute-start(bf16[512,256]{1,0:T(8,128)(2,1)S(1)} %collective-permute-done.11.refs_4_), channel_id=1, source_target_pairs={{4,0},{8,4},{12,8},{14,12},{10,14},{6,10},{2,6},{0,2},{5,1},{9,5},... | collective-permute-start | bytes 786440 | tf_op jit(solution)/shard_map/down6c1/ppermute | solution.py:380
  51.3 16.1 %collective-permute-start.16 = (bf16[512,256]{1,0:T(8,128)(2,1)S(1)}, bf16[512,256]{1,0:T(8,128)(2,1)S(1)}, u32[]{:S(2)}, u32[]{:S(2)}) collective-permute-start(bf16[512,256]{1,0:T(8,128)(2,1)S(1)} %collective-permute-done.14.refs_1_), channel_id=1, source_target_pairs={{0,4},{4,8},{8,12},{12,14},{14,10},{10,6},{6,2},{2,0},{1,5},{5,9},... | collective-permute-start | bytes 786440 | tf_op jit(solution)/shard_map/up8c2/ppermute | solution.py:378
  51.3 17.6 %collective-permute-start.17 = (bf16[512,256]{1,0:T(8,128)(2,1)S(1)}, bf16[512,256]{1,0:T(8,128)(2,1)S(1)}, u32[]{:S(2)}, u32[]{:S(2)}) collective-permute-start(bf16[512,256]{1,0:T(8,128)(2,1)S(1)} %collective-permute-done.15.refs_2_), channel_id=1, source_target_pairs={{4,0},{8,4},{12,8},{14,12},{10,14},{6,10},{2,6},{0,2},{5,1},{9,5},... | collective-permute-start | bytes 786440 | tf_op jit(solution)/shard_map/down8c2/ppermute | solution.py:380
  53.3 12.0 %collective-permute-start.12 = (bf16[256,256]{1,0:T(8,128)(2,1)S(1)}, bf16[256,256]{1,0:T(8,128)(2,1)S(1)}, u32[]{:S(2)}, u32[]{:S(2)}) collective-permute-start(bf16[256,256]{1,0:T(8,128)(2,1)S(1)} %slice.32), channel_id=1, source_target_pairs={{0,4},{4,8},{8,12},{12,14},{14,10},{10,6},{6,2},{2,0},{1,5},{5,9},... | collective-permute-start | bytes 393224 | tf_op jit(solution)/shard_map/up7c0/ppermute | solution.py:378
  56.9 10.0 %collective-permute-start.13 = (bf16[256,256]{1,0:T(8,128)(2,1)S(1)}, bf16[256,256]{1,0:T(8,128)(2,1)S(1)}, u32[]{:S(2)}, u32[]{:S(2)}) collective-permute-start(bf16[256,256]{1,0:T(8,128)(2,1)S(1)} %slice.33), channel_id=1, source_target_pairs={{4,0},{8,4},{12,8},{14,12},{10,14},{6,10},{2,6},{0,2},{5,1},{9,5},... | collective-permute-start | bytes 393224 | tf_op jit(solution)/shard_map/down7c0/ppermute | solution.py:380
  58.5 13.1 %collective-permute-start.22 = (bf16[256,256]{1,0:T(8,128)(2,1)S(1)}, bf16[256,256]{1,0:T(8,128)(2,1)S(1)}, u32[]{:S(2)}, u32[]{:S(2)}) collective-permute-start(bf16[256,256]{1,0:T(8,128)(2,1)S(1)} %slice.34), channel_id=1, source_target_pairs={{0,4},{4,8},{8,12},{12,14},{14,10},{10,6},{6,2},{2,0},{1,5},{5,9},... | collective-permute-start | bytes 393224 | tf_op jit(solution)/shard_map/up9c1/ppermute | solution.py:378
  66.9 10.1 %collective-permute-start.20 = (bf16[512,256]{1,0:T(8,128)(2,1)}, bf16[512,256]{1,0:T(8,128)(2,1)S(1)}, u32[]{:S(2)}, u32[]{:S(2)}) collective-permute-start(bf16[512,256]{1,0:T(8,128)(2,1)} %get-tuple-element.102.refs_0_), channel_id=1, source_target_pairs={{0,4},{4,8},{8,12},{12,14},{14,10},{10,6},{6,2},{2,0},{1,5},{5,9},... | collective-permute-start | bytes 786440 | tf_op jit(solution)/shard_map/up10c3/ppermute | solution.py:378
  67.3 9.6 %collective-permute-start.21 = (bf16[512,256]{1,0:T(8,128)(2,1)}, bf16[512,256]{1,0:T(8,128)(2,1)S(1)}, u32[]{:S(2)}, u32[]{:S(2)}) collective-permute-start(bf16[512,256]{1,0:T(8,128)(2,1)} %get-tuple-element.102.refs_0_), channel_id=1, source_target_pairs={{4,0},{8,4},{12,8},{14,12},{10,14},{6,10},{2,6},{0,2},{5,1},{9,5},... | collective-permute-start | bytes 786440 | tf_op jit(solution)/shard_map/down10c3/ppermute | solution.py:380
  71.6 9.3 %collective-permute-start.27 = (bf16[512,256]{1,0:T(8,128)(2,1)S(1)}, bf16[512,256]{1,0:T(8,128)(2,1)S(1)}, u32[]{:S(2)}, u32[]{:S(2)}) collective-permute-start(bf16[512,256]{1,0:T(8,128)(2,1)S(1)} %collective-permute-done.16.refs_3_), channel_id=1, source_target_pairs={{0,4},{4,8},{8,12},{12,14},{14,10},{10,6},{6,2},{2,0},{1,5},{5,9},... | collective-permute-start | bytes 786440 | tf_op jit(solution)/shard_map/up11c2/ppermute | solution.py:378
  72.1 9.2 %collective-permute-start.28 = (bf16[512,256]{1,0:T(8,128)(2,1)S(1)}, bf16[512,256]{1,0:T(8,128)(2,1)S(1)}, u32[]{:S(2)}, u32[]{:S(2)}) collective-permute-start(bf16[512,256]{1,0:T(8,128)(2,1)S(1)} %collective-permute-done.17.refs_4_), channel_id=1, source_target_pairs={{4,0},{8,4},{12,8},{14,12},{10,14},{6,10},{2,6},{0,2},{5,1},{9,5},... | collective-permute-start | bytes 786440 | tf_op jit(solution)/shard_map/down11c2/ppermute | solution.py:380
  73.7 9.9 %collective-permute-start.24 = (bf16[5,512,256]{2,1,0:T(8,128)(2,1)S(1)}, bf16[5,512,256]{2,1,0:T(8,128)(2,1)S(1)}, u32[]{:S(2)}, u32[]{:S(2)}) collective-permute-start(bf16[5,512,256]{2,1,0:T(8,128)(2,1)S(1)} %get-tuple-element.107), channel_id=1, source_target_pairs={{0,1},{1,0},{2,3},{3,2},{4,5},{5,4},{6,7},{7,6},{8,9},{9,8},{10,11... | collective-permute-start | bytes 3932168 | tf_op jit(solution)/shard_map/swap0/ppermute | solution.py:362
  81.4 9.4 %collective-permute-start.29 = (bf16[5,512,256]{2,1,0:T(8,128)(2,1)S(1)}, bf16[5,512,256]{2,1,0:T(8,128)(2,1)S(1)}, u32[]{:S(2)}, u32[]{:S(2)}) collective-permute-start(bf16[5,512,256]{2,1,0:T(8,128)(2,1)S(1)} %get-tuple-element.124), channel_id=1, source_target_pairs={{0,1},{1,0},{2,3},{3,2},{4,5},{5,4},{6,7},{7,6},{8,9},{9,8},{10,11... | collective-permute-start | bytes 3932168 | tf_op jit(solution)/shard_map/swap1/ppermute | solution.py:362
  83.6 9.2 %collective-permute-start.25 = (bf16[512,256]{1,0:T(8,128)(2,1)S(1)}, bf16[512,256]{1,0:T(8,128)(2,1)S(1)}, u32[]{:S(2)}, u32[]{:S(2)}) collective-permute-start(bf16[512,256]{1,0:T(8,128)(2,1)S(1)} %collective-permute-done.20.refs_1_), channel_id=1, source_target_pairs={{0,4},{4,8},{8,12},{12,14},{14,10},{10,6},{6,2},{2,0},{1,5},{5,9},... | collective-permute-start | bytes 786440 | tf_op jit(solution)/shard_map/up12c3/ppermute | solution.py:378
  83.8 9.2 %collective-permute-start.26 = (bf16[512,256]{1,0:T(8,128)(2,1)S(1)}, bf16[512,256]{1,0:T(8,128)(2,1)S(1)}, u32[]{:S(2)}, u32[]{:S(2)}) collective-permute-start(bf16[512,256]{1,0:T(8,128)(2,1)S(1)} %collective-permute-done.21.refs_2_), channel_id=1, source_target_pairs={{4,0},{8,4},{12,8},{14,12},{10,14},{6,10},{2,6},{0,2},{5,1},{9,5},... | collective-permute-start | bytes 786440 | tf_op jit(solution)/shard_map/down12c3/ppermute | solution.py:380
  88.7 11.2 %collective-permute-start.30 = (bf16[256,256]{1,0:T(8,128)(2,1)S(1)}, bf16[256,256]{1,0:T(8,128)(2,1)S(1)}, u32[]{:S(2)}, u32[]{:S(2)}) collective-permute-start(bf16[256,256]{1,0:T(8,128)(2,1)S(1)} %slice.36), channel_id=1, source_target_pairs={{0,4},{4,8},{8,12},{12,14},{14,10},{10,6},{6,2},{2,0},{1,5},{5,9},... | collective-permute-start | bytes 393224 | tf_op jit(solution)/shard_map/up13c2/ppermute | solution.py:378
  88.9 11.1 %collective-permute-start.31 = (bf16[256,256]{1,0:T(8,128)(2,1)S(1)}, bf16[256,256]{1,0:T(8,128)(2,1)S(1)}, u32[]{:S(2)}, u32[]{:S(2)}) collective-permute-start(bf16[256,256]{1,0:T(8,128)(2,1)S(1)} %slice.37), channel_id=1, source_target_pairs={{4,0},{8,4},{12,8},{14,12},{10,14},{6,10},{2,6},{0,2},{5,1},{9,5},... | collective-permute-start | bytes 393224 | tf_op jit(solution)/shard_map/down13c2/ppermute | solution.py:380
  92.9 7.4 %collective-permute-start.32 = (bf16[512,256]{1,0:T(8,128)(2,1)S(1)}, bf16[512,256]{1,0:T(8,128)(2,1)S(1)}, u32[]{:S(2)}, u32[]{:S(2)}) collective-permute-start(bf16[512,256]{1,0:T(8,128)(2,1)S(1)} %collective-permute-done.25.refs_3_), channel_id=1, source_target_pairs={{0,4},{4,8},{8,12},{12,14},{14,10},{10,6},{6,2},{2,0},{1,5},{5,9},... | collective-permute-start | bytes 786440 | tf_op jit(solution)/shard_map/up14c3/ppermute | solution.py:378
  94.6 6.4 %collective-permute-start.33 = (bf16[512,256]{1,0:T(8,128)(2,1)S(1)}, bf16[512,256]{1,0:T(8,128)(2,1)S(1)}, u32[]{:S(2)}, u32[]{:S(2)}) collective-permute-start(bf16[512,256]{1,0:T(8,128)(2,1)S(1)} %collective-permute-done.26.refs_4_), channel_id=1, source_target_pairs={{4,0},{8,4},{12,8},{14,12},{10,14},{6,10},{2,6},{0,2},{5,1},{9,5},... | collective-permute-start | bytes 786440 | tf_op jit(solution)/shard_map/down14c3/ppermute | solution.py:380
  109.6 8.6 %collective-permute-start.37 = (bf16[5,512,256]{2,1,0:T(8,128)(2,1)S(1)}, bf16[5,512,256]{2,1,0:T(8,128)(2,1)S(1)}, u32[]{:S(2)}, u32[]{:S(2)}) collective-permute-start(bf16[5,512,256]{2,1,0:T(8,128)(2,1)S(1)} %get-tuple-element.144), channel_id=1, source_target_pairs={{0,1},{1,0},{2,3},{3,2},{4,5},{5,4},{6,7},{7,6},{8,9},{9,8},{10,11... | collective-permute-start | bytes 3932168 | tf_op jit(solution)/shard_map/swap3/ppermute | solution.py:362
  (12 other events, 60.6 us)

commit v3 on v2

--- a/solution.py
+++ b/solution.py
@@ -42,7 +42,7 @@
     return jnp.where(place < devices // 2, 2 * place, 2 * (devices - 1 - place) + 1)
 
 
-def attend_kernel(kv_share, unroll, heads_of, q_hbm, ko_hbm, vo_hbm, sign_hbm, kp_any, vp_any, *scratch):
+def attend_kernel(unroll, heads_of, q_hbm, sign_hbm, own_any, prev_any, *scratch):
     out_refs, scratch = scratch[: len(heads_of)], scratch[len(heads_of) :]
     homes = [(ref, h) for ref, count in zip(out_refs, heads_of) for h in range(count)]
     q_ref, kv_ref, sign_ref, inner_ref, vt_ref, bar_ref, sem = scratch
@@ -50,14 +50,11 @@
     heads = width // DH
     scale = math.log2(math.e) / math.sqrt(DH)
     first_head = lax.axis_index("head") * heads
-    columns = pl.ds(pl.multiple_of(first_head // kv_share * DH, DH), DH)
     copies = [
-        pltpu.make_async_copy(ko_hbm.at[:, columns], kv_ref.at[0], sem.at[0]),
-        pltpu.make_async_copy(kp_any.at[:, columns], kv_ref.at[1], sem.at[1]),
-        pltpu.make_async_copy(vo_hbm.at[:, columns], kv_ref.at[2], sem.at[2]),
-        pltpu.make_async_copy(vp_any.at[:, columns], kv_ref.at[3], sem.at[3]),
-        pltpu.make_async_copy(sign_hbm, sign_ref, sem.at[4]),
-        pltpu.make_async_copy(q_hbm, q_ref, sem.at[5]),
+        pltpu.make_async_copy(own_any, kv_ref.at[0], sem.at[0]),
+        pltpu.make_async_copy(prev_any, kv_ref.at[1], sem.at[1]),
+        pltpu.make_async_copy(sign_hbm, sign_ref, sem.at[2]),
+        pltpu.make_async_copy(q_hbm, q_ref, sem.at[3]),
     ]
     for copy in copies:
         copy.start()
@@ -70,19 +67,19 @@
     for level in range(7):
         odd = odd ^ (anded >> level) & 1
     table = (1 - 2 * odd).astype(jnp.float32)
-    for copy in copies[2:4]:
+    for copy in copies[:2]:
         copy.wait()
-    vt_ref[:, :rows] = kv_ref[3].astype(jnp.float32).T.astype(jnp.bfloat16)
-    vt_ref[:, rows:] = kv_ref[2].astype(jnp.float32).T.astype(jnp.bfloat16)
-    for copy in copies[:2] + copies[4:]:
+    vt_ref[:, :rows] = kv_ref[1, :, DH:].astype(jnp.float32).T.astype(jnp.bfloat16)
+    vt_ref[:, rows:] = kv_ref[0, :, DH:].astype(jnp.float32).T.astype(jnp.bfloat16)
+    for copy in copies[2:]:
         copy.wait()
 
     def one(h, earlier):
         q = q_ref[:, pl.ds(pl.multiple_of(h * DH, DH), DH)]
-        own = nt_dot(kv_ref[0], q) + bar_ref[...]
+        own = nt_dot(kv_ref[0, :, :DH], q) + bar_ref[...]
         top = jnp.max(own, axis=0, keepdims=True)
         if earlier:
-            before = nt_dot(kv_ref[1], q)
+            before = nt_dot(kv_ref[1, :, :DH], q)
             top = jnp.maximum(top, jnp.max(before, axis=0, keepdims=True))
         weights = jnp.exp2((own - top) * scale)
         total = jnp.sum(weights, axis=0, keepdims=True)
@@ -125,29 +122,28 @@
                 out_ref[at, lane : lane + 128] = (tile * shrink).astype(jnp.bfloat16)
 
 
-def attend(heads_of, queries, own_keys, own_values, signs, prev_keys, prev_values):
+def attend(heads_of, queries, signs, own, prev):
     rows, width = queries.shape
-    kv_share = HEADS // (own_keys.shape[1] // DH)
     heads = width // DH
     hbm, anywhere = pl.BlockSpec(memory_space=pltpu.HBM), pl.BlockSpec(memory_space=pl.ANY)
     return pl.pallas_call(
-        functools.partial(attend_kernel, kv_share, ATTEND_UNROLL, heads_of),
-        in_specs=[hbm] * 4 + [anywhere] * 2,
+        functools.partial(attend_kernel, ATTEND_UNROLL, heads_of),
+        in_specs=[hbm] * 2 + [anywhere] * 2,
         out_specs=[pl.BlockSpec(memory_space=pltpu.VMEM)] * len(heads_of),
         scratch_shapes=[
             pltpu.VMEM((rows, width), jnp.bfloat16),
-            pltpu.VMEM((4, rows, DH), jnp.bfloat16),
+            pltpu.VMEM((2, rows, 2 * DH), jnp.bfloat16),
             pltpu.VMEM((HEADS, DH), jnp.int32),
             pltpu.VMEM((heads, DH, rows), jnp.bfloat16),
             pltpu.VMEM((DH, 2 * rows), jnp.bfloat16),
             pltpu.VMEM((rows, rows), jnp.float32),
-            pltpu.SemaphoreType.DMA((6,)),
+            pltpu.SemaphoreType.DMA((4,)),
         ],
         out_shape=[jax.ShapeDtypeStruct((count * DH, rows), jnp.bfloat16) for count in heads_of],
         compiler_params=pltpu.CompilerParams(vmem_limit_bytes=60 * MIB),
         cost_estimate=pl.CostEstimate(flops=20000000000, bytes_accessed=1024, transcendentals=0),
         name="attend",
-    )(queries, own_keys, own_values, signs, prev_keys, prev_values)
+    )(queries, signs, own, prev)
 
 
 def mix_kernel(devices, scale, *refs):
@@ -305,7 +301,7 @@
     )(*(([out] if aliased else []) + keeps + recvs))
 
 
-PLANS = {(16, 4): ([4, 4, 4, 4], [0,1,0,1,0,2,1,0,2,1,3,2,3,2,3,3])}
+PLANS = {(16, 4): ([4, 4, 4, 4], [0, 1, 0, 1, 2, 0, 1, 2, 0, 1, 3, 2, 3, 2, 3, 3])}
 
 
 def plan(local_heads, hops):
@@ -335,9 +331,12 @@
         order = order[0::2] + order[:0:-2]
     forward = [(order[i], order[(i + 1) % devices]) for i in range(devices)]
     backward = [(b, a) for a, b in forward]
-    prev_keys, prev_values = lax.ppermute((key_rows, values), "tok", [(0, 1)])
+    kv_share = HEADS // (key_rows.shape[1] // DH)
+    first = lax.axis_index("head") * (width // DH) // kv_share * DH
+    own = jnp.concatenate([lax.dynamic_slice_in_dim(x, first, DH, 1) for x in (key_rows, values)], 1)
+    prev = lax.ppermute(own, "tok", [(0, 1)])
     heads_of, sequence = plan(width // DH, half)
-    mixed = attend(heads_of, queries, key_rows, values, sign_bits.reshape(HEADS, DH), prev_keys, prev_values)
+    mixed = attend(heads_of, queries, sign_bits.reshape(HEADS, DH), own, prev)
     sizes = [c * DH for c in heads_of]
     chunks = len(sizes)
     starts = [sum(sizes[:c]) for c in range(chunks)]

time: 129 us -> 126 us (0.977)
  waiting for transfers between devices: 43 us -> 38.6 us
  starting transfers between devices: 42.2 us -> 43.5 us
    ppermute x16, waiting for transfers between devices: 31.7 us -> 28.2 us  [local(): going = lax.ppermute(going, 'head', forward)]
    ppermute x4, starting transfers between devices: 5.99 us -> 8.12 us  [compute(): recvs[c] = lax.ppermute(sends[c], 'tok', [(0, 1), (1, 0)])]
    ppermute x2 -> x1, starting transfers between devices: 3.7 us -> 2.36 us  [local(): prev = lax.ppermute(own, 'tok', [(0, 1)])]
  transfers between devices with their start and end apart: 38 -> 37, of which waited for: 21 -> 20; matrix products, arithmetic and copies ran while one was open for 0% -> 0% of each run, Pallas kernels for 18% -> 18%
where the time goes in v3:
time: 126 us
  starting transfers between devices  43.5 us (35%)
  Pallas kernels  40.9 us (32%)
  waiting for transfers between devices  38.6 us (31%)
  local copies, waits for them, and re-layouts  2.58 us (2%)
    ppermute x16, waiting for transfers between devices, local(): going = lax.ppermute(going, 'head', forward)  28.2 us
    ppermute x16, starting transfers between devices, local(): coming = lax.ppermute(coming, 'head', backward)  26.8 us
    pallas_call x4, Pallas kernels, gram(): pl.pallas_call(functools.partial(gram_kernel, starts, sizes, chunk, alias...  25.6 us
    ppermute x16, waiting for transfers between devices, local(): coming = lax.ppermute(coming, 'head', backward)  8.91 us
    pallas_call x1, Pallas kernels, attend(): pl.pallas_call(functools.partial(attend_kernel, ATTEND_UNROLL, heads_of),...  8.18 us
    ppermute x4, starting transfers between devices, compute(): recvs[c] = lax.ppermute(sends[c], 'tok', [(0, 1), (1, 0)])  8.12 us
    pallas_call x4, Pallas kernels, mix(): pl.pallas_call(functools.partial(mix_kernel, devices, scale), in_specs=[p...  7.16 us
    ppermute x16, starting transfers between devices, local(): going = lax.ppermute(going, 'head', forward)  6.27 us
  transfers between devices with their start and end apart: 37, of which 20 were waited for; matrix products, arithmetic and copies ran while one was open for 0% of the time, Pallas kernels for 18%

profile of v3, /device:TPU:0, one launch (start us, length us, event | category | flops | bytes accessed | tf_op | source)
XLA Modules:
  0.0 126.1 jit_solution(409698216460970662)
XLA Ops:
  0.9 2.4 %collective-permute-start = (bf16[256,256]{1,0:T(8,128)(2,1)S(1)}, bf16[256,256]{1,0:T(8,128)(2,1)S(1)}, u32[]{:S(2)}, u32[]{:S(2)}) collective-permute-start(bf16[256,256]{1,0:T(8,128)(2,1)S(1)} %pad_maximum_fusion.own_any), channel_id=1, source_target_pairs={{0,1},{2,3},{4,5},{6,7},{8,9},{10,11},{12,13},{14,15},{16,17},{18,... | collective-permute-start | bytes 393224 | tf_op jit(solution)/shard_map/ppermute | solution.py:337
  4.9 8.2 %attend.1 = (bf16[512,256]{1,0:T(8,128)(2,1)}, bf16[512,256]{1,0:T(8,128)(2,1)}, bf16[512,256]{1,0:T(8,128)(2,1)}, bf16[512,256]{1,0:T(8,128)(2,1)}) custom-call(bf16[256,2048]{1,0:T(8,128)(2,1)} %q_hbm.1, s32[128,128]{1,0:T(8,128)} %bitcast.2, bf16[256,256]{1,0:T(8,128)(2,1)} %copy-done.4, bf16[256,256]{1,0:T(8,128)(2,1)} %copy-done.5), custom_call_target="tpu_custom_call" | custom-call | flops 20000000000 | bytes 1024 | tf_op jit(solution)/shard_map/attend/pallas_call | solution.py:129
  13.1 2.4 %collective-permute-start.2 = (bf16[512,256]{1,0:T(8,128)(2,1)}, bf16[512,256]{1,0:T(8,128)(2,1)S(1)}, u32[]{:S(2)}, u32[]{:S(2)}) collective-permute-start(bf16[512,256]{1,0:T(8,128)(2,1)} %get-tuple-element.90.refs_0_), channel_id=1, source_target_pairs={{4,0},{8,4},{12,8},{14,12},{10,14},{6,10},{2,6},{0,2},{5,1},{9,5},... | collective-permute-start | bytes 786440 | tf_op jit(solution)/shard_map/down0c0/ppermute | solution.py:379
  15.6 1.9 %collective-permute-start.6 = (bf16[512,256]{1,0:T(8,128)(2,1)}, bf16[512,256]{1,0:T(8,128)(2,1)S(1)}, u32[]{:S(2)}, u32[]{:S(2)}) collective-permute-start(bf16[512,256]{1,0:T(8,128)(2,1)} %get-tuple-element.110.refs_0_), channel_id=1, source_target_pairs={{4,0},{8,4},{12,8},{14,12},{10,14},{6,10},{2,6},{0,2},{5,1},{9,5},... | collective-permute-start | bytes 786440 | tf_op jit(solution)/shard_map/down1c1/ppermute | solution.py:379
  17.7 2.5 %collective-permute-done.2.refs_2_ = bf16[512,256]{1,0:T(8,128)(2,1)S(1)} collective-permute-done((bf16[512,256]{1,0:T(8,128)(2,1)}, bf16[512,256]{1,0:T(8,128)(2,1)S(1)}, u32[]{:S(2)}, u32[]{:S(2)}) %collective-permute-start.2) | collective-permute-done | bytes 262176 | tf_op jit(solution)/shard_map/down0c0/ppermute | solution.py:379
  20.1 2.0 %collective-permute-start.4 = (bf16[512,256]{1,0:T(8,128)(2,1)S(1)}, bf16[512,256]{1,0:T(8,128)(2,1)S(1)}, u32[]{:S(2)}, u32[]{:S(2)}) collective-permute-start(bf16[512,256]{1,0:T(8,128)(2,1)S(1)} %collective-permute-done.2.refs_2_), channel_id=1, source_target_pairs={{4,0},{8,4},{12,8},{14,12},{10,14},{6,10},{2,6},{0,2},{5,1},{9,5},... | collective-permute-start | bytes 786440 | tf_op jit(solution)/shard_map/down2c0/ppermute | solution.py:379
  22.2 2.7 %collective-permute-done.6.refs_2_ = bf16[512,256]{1,0:T(8,128)(2,1)S(1)} collective-permute-done((bf16[512,256]{1,0:T(8,128)(2,1)}, bf16[512,256]{1,0:T(8,128)(2,1)S(1)}, u32[]{:S(2)}, u32[]{:S(2)}) %collective-permute-start.6) | collective-permute-done | bytes 262176 | tf_op jit(solution)/shard_map/down1c1/ppermute | solution.py:379
  24.9 2.5 %collective-permute-done.5.refs_1_ = bf16[512,256]{1,0:T(8,128)(2,1)S(1)} collective-permute-done((bf16[512,256]{1,0:T(8,128)(2,1)}, bf16[512,256]{1,0:T(8,128)(2,1)S(1)}, u32[]{:S(2)}, u32[]{:S(2)}) %collective-permute-start.5) | collective-permute-done | bytes 262176 | tf_op jit(solution)/shard_map/up1c1/ppermute | solution.py:377
  27.4 2.0 %collective-permute-start.14 = (bf16[512,256]{1,0:T(8,128)(2,1)S(1)}, bf16[512,256]{1,0:T(8,128)(2,1)S(1)}, u32[]{:S(2)}, u32[]{:S(2)}) collective-permute-start(bf16[512,256]{1,0:T(8,128)(2,1)S(1)} %collective-permute-done.6.refs_2_), channel_id=1, source_target_pairs={{4,0},{8,4},{12,8},{14,12},{10,14},{6,10},{2,6},{0,2},{5,1},{9,5},... | collective-permute-start | bytes 786440 | tf_op jit(solution)/shard_map/down3c1/ppermute | solution.py:379
  30.5 2.2 %collective-permute-start.10 = (bf16[512,256]{1,0:T(8,128)(2,1)}, bf16[512,256]{1,0:T(8,128)(2,1)S(1)}, u32[]{:S(2)}, u32[]{:S(2)}) collective-permute-start(bf16[512,256]{1,0:T(8,128)(2,1)} %get-tuple-element.129.refs_0_), channel_id=1, source_target_pairs={{4,0},{8,4},{12,8},{14,12},{10,14},{6,10},{2,6},{0,2},{5,1},{9,5},... | collective-permute-start | bytes 786440 | tf_op jit(solution)/shard_map/down4c2/ppermute | solution.py:379
  33.0 5.6 %collective-permute-done.13.refs_3_ = bf16[512,256]{1,0:T(8,128)(2,1)S(1)} collective-permute-done((bf16[512,256]{1,0:T(8,128)(2,1)S(1)}, bf16[512,256]{1,0:T(8,128)(2,1)S(1)}, u32[]{:S(2)}, u32[]{:S(2)}) %collective-permute-start.13) | collective-permute-done | bytes 262176 | tf_op jit(solution)/shard_map/up3c1/ppermute | solution.py:377
  38.7 1.6 %collective-permute-start.8 = (bf16[512,256]{1,0:T(8,128)(2,1)S(1)}, bf16[512,256]{1,0:T(8,128)(2,1)S(1)}, u32[]{:S(2)}, u32[]{:S(2)}) collective-permute-start(bf16[512,256]{1,0:T(8,128)(2,1)S(1)} %collective-permute-done.4.refs_4_), channel_id=1, source_target_pairs={{4,0},{8,4},{12,8},{14,12},{10,14},{6,10},{2,6},{0,2},{5,1},{9,5},... | collective-permute-start | bytes 786440 | tf_op jit(solution)/shard_map/down5c0/ppermute | solution.py:379
  40.7 3.6 %collective-permute-done.9.refs_1_ = bf16[512,256]{1,0:T(8,128)(2,1)S(1)} collective-permute-done((bf16[512,256]{1,0:T(8,128)(2,1)}, bf16[512,256]{1,0:T(8,128)(2,1)S(1)}, u32[]{:S(2)}, u32[]{:S(2)}) %collective-permute-start.9) | collective-permute-done | bytes 262176 | tf_op jit(solution)/shard_map/up4c2/ppermute | solution.py:377
  46.3 3.6 %collective-permute-done.7.refs_5_ = bf16[512,256]{1,0:T(8,128)(2,1)S(1)} collective-permute-done((bf16[512,256]{1,0:T(8,128)(2,1)S(1)}, bf16[512,256]{1,0:T(8,128)(2,1)S(1)}, u32[]{:S(2)}, u32[]{:S(2)}) %collective-permute-start.7) | collective-permute-done | bytes 262176 | tf_op jit(solution)/shard_map/up5c0/ppermute | solution.py:377
  49.9 1.6 %collective-permute-start.20 = (bf16[512,256]{1,0:T(8,128)(2,1)S(1)}, bf16[512,256]{1,0:T(8,128)(2,1)S(1)}, u32[]{:S(2)}, u32[]{:S(2)}) collective-permute-start(bf16[512,256]{1,0:T(8,128)(2,1)S(1)} %collective-permute-done.10.refs_2_), channel_id=1, source_target_pairs={{4,0},{8,4},{12,8},{14,12},{10,14},{6,10},{2,6},{0,2},{5,1},{9,5},... | collective-permute-start | bytes 786440 | tf_op jit(solution)/shard_map/down7c2/ppermute | solution.py:379
  52.0 3.5 %collective-permute-done.15.refs_5_ = bf16[512,256]{1,0:T(8,128)(2,1)S(1)} collective-permute-done((bf16[512,256]{1,0:T(8,128)(2,1)S(1)}, bf16[512,256]{1,0:T(8,128)(2,1)S(1)}, u32[]{:S(2)}, u32[]{:S(2)}) %collective-permute-start.15) | collective-permute-done | bytes 262176 | tf_op jit(solution)/shard_map/up6c1/ppermute | solution.py:377
  55.5 1.6 %collective-permute-start.12 = (bf16[256,256]{1,0:T(8,128)(2,1)S(1)}, bf16[256,256]{1,0:T(8,128)(2,1)S(1)}, u32[]{:S(2)}, u32[]{:S(2)}) collective-permute-start(bf16[256,256]{1,0:T(8,128)(2,1)S(1)} %slice.33), channel_id=1, source_target_pairs={{4,0},{8,4},{12,8},{14,12},{10,14},{6,10},{2,6},{0,2},{5,1},{9,5},... | collective-permute-start | bytes 393224 | tf_op jit(solution)/shard_map/down8c0/ppermute | solution.py:379
  57.6 3.5 %collective-permute-done.19.refs_3_ = bf16[512,256]{1,0:T(8,128)(2,1)S(1)} collective-permute-done((bf16[512,256]{1,0:T(8,128)(2,1)S(1)}, bf16[512,256]{1,0:T(8,128)(2,1)S(1)}, u32[]{:S(2)}, u32[]{:S(2)}) %collective-permute-start.19) | collective-permute-done | bytes 262176 | tf_op jit(solution)/shard_map/up7c2/ppermute | solution.py:377
  61.1 1.6 %collective-permute-start.18 = (bf16[256,256]{1,0:T(8,128)(2,1)S(1)}, bf16[256,256]{1,0:T(8,128)(2,1)S(1)}, u32[]{:S(2)}, u32[]{:S(2)}) collective-permute-start(bf16[256,256]{1,0:T(8,128)(2,1)S(1)} %slice.35), channel_id=1, source_target_pairs={{4,0},{8,4},{12,8},{14,12},{10,14},{6,10},{2,6},{0,2},{5,1},{9,5},... | collective-permute-start | bytes 393224 | tf_op jit(solution)/shard_map/down9c1/ppermute | solution.py:379
  67.6 1.6 %collective-permute-start.22 = (bf16[512,256]{1,0:T(8,128)(2,1)S(1)}, bf16[512,256]{1,0:T(8,128)(2,1)S(1)}, u32[]{:S(2)}, u32[]{:S(2)}) collective-permute-start(bf16[512,256]{1,0:T(8,128)(2,1)S(1)} %collective-permute-done.20.refs_4_), channel_id=1, source_target_pairs={{4,0},{8,4},{12,8},{14,12},{10,14},{6,10},{2,6},{0,2},{5,1},{9,5},... | collective-permute-start | bytes 786440 | tf_op jit(solution)/shard_map/down11c2/ppermute | solution.py:379
  70.2 1.7 %mix.4 = (bf16[5,512,256]{2,1,0:T(8,128)(2,1)S(1)}, bf16[5,512,256]{2,1,0:T(8,128)(2,1)S(1)}) custom-call(bf16[512,256]{1,0:T(8,128)(2,1)S(1)} %copy-done.3, bf16[512,256]{1,0:T(8,128)(2,1)S(1)} %collective-permute-done.1.refs_1_, bf16[512,256]{1,0:T(8,128)(2,1)S(1)} %collective-permute-done.2.refs_2_, bf16[512,256]{1,0:T(8,128)(2,1)S(1)} %collective-permute-done.3.refs_3_, ...), custom_call_target="tpu_custom_call" | custom-call | flops 20000000000 | bytes 1024 | tf_op jit(solution)/shard_map/mix/pallas_call | solution.py:208
  72.6 1.8 %collective-permute-start.27 = (bf16[512,256]{1,0:T(8,128)(2,1)S(1)}, bf16[512,256]{1,0:T(8,128)(2,1)S(1)}, u32[]{:S(2)}, u32[]{:S(2)}) collective-permute-start(bf16[512,256]{1,0:T(8,128)(2,1)S(1)} %collective-permute-done.24.refs_2_), channel_id=1, source_target_pairs={{4,0},{8,4},{12,8},{14,12},{10,14},{6,10},{2,6},{0,2},{5,1},{9,5},... | collective-permute-start | bytes 786440 | tf_op jit(solution)/shard_map/down12c3/ppermute | solution.py:379
  74.4 5.9 %collective-permute-start.25 = (bf16[5,512,256]{2,1,0:T(8,128)(2,1)S(1)}, bf16[5,512,256]{2,1,0:T(8,128)(2,1)S(1)}, u32[]{:S(2)}, u32[]{:S(2)}) collective-permute-start(bf16[5,512,256]{2,1,0:T(8,128)(2,1)S(1)} %get-tuple-element.109), channel_id=1, source_target_pairs={{0,1},{1,0},{2,3},{3,2},{4,5},{5,4},{6,7},{7,6},{8,9},{9,8},{10,11... | collective-permute-start | bytes 3932168 | tf_op jit(solution)/shard_map/swap0/ppermute | solution.py:361
  80.3 1.7 %mix.5 = (bf16[5,512,256]{2,1,0:T(8,128)(2,1)S(1)}, bf16[5,512,256]{2,1,0:T(8,128)(2,1)S(1)}) custom-call(bf16[512,256]{1,0:T(8,128)(2,1)S(1)} %copy-done.2, bf16[512,256]{1,0:T(8,128)(2,1)S(1)} %collective-permute-done.5.refs_1_, bf16[512,256]{1,0:T(8,128)(2,1)S(1)} %collective-permute-done.6.refs_2_, bf16[512,256]{1,0:T(8,128)(2,1)S(1)} %collective-permute-done.13.refs_3_, ...), custom_call_target="tpu_custom_call" | custom-call | flops 20000000000 | bytes 1024 | tf_op jit(solution)/shard_map/mix/pallas_call | solution.py:208
  82.1 1.6 %collective-permute-start.28 = (bf16[5,512,256]{2,1,0:T(8,128)(2,1)S(1)}, bf16[5,512,256]{2,1,0:T(8,128)(2,1)S(1)}, u32[]{:S(2)}, u32[]{:S(2)}) collective-permute-start(bf16[5,512,256]{2,1,0:T(8,128)(2,1)S(1)} %get-tuple-element.124), channel_id=1, source_target_pairs={{0,1},{1,0},{2,3},{3,2},{4,5},{5,4},{6,7},{7,6},{8,9},{9,8},{10,11... | collective-permute-start | bytes 3932168 | tf_op jit(solution)/shard_map/swap1/ppermute | solution.py:361
  85.9 3.0 %gram0.1.refs_0_ = bf16[4,2048,2048]{2,1,0:T(8,128)(2,1)} custom-call(bf16[5,512,256]{2,1,0:T(8,128)(2,1)S(1)} %get-tuple-element.104.refs_0_.refs_1_, bf16[5,512,256]{2,1,0:T(8,128)(2,1)S(1)} %collective-permute-done.25.refs_1_.refs_3_.refs_4_.refs_5_), custom_call_target="tpu_custom_call" | custom-call | flops 20000000000 | bytes 1024 | tf_op jit(solution)/shard_map/gram0/pallas_call | solution.py:290
  91.0 5.0 %gram1.1.refs_0_ = bf16[4,2048,2048]{2,1,0:T(8,128)(2,1)} custom-call(bf16[4,2048,2048]{2,1,0:T(8,128)(2,1)} %gram0.1.refs_0_, bf16[5,512,256]{2,1,0:T(8,128)(2,1)S(1)} %get-tuple-element.104.refs_0_.refs_1_, bf16[5,512,256]{2,1,0:T(8,128)(2,1)S(1)} %get-tuple-element.122.refs_2_, ...), custom_call_target="tpu_custom_call", output_to_operand_aliasing={{}: (0, {})} | custom-call | flops 20000000000 | bytes 1024 | tf_op jit(solution)/shard_map/gram1/pallas_call | solution.py:290
  100.1 1.7 %mix.6 = (bf16[5,512,256]{2,1,0:T(8,128)(2,1)S(1)}, bf16[5,512,256]{2,1,0:T(8,128)(2,1)S(1)}) custom-call(bf16[512,256]{1,0:T(8,128)(2,1)S(1)} %copy-done.1, bf16[512,256]{1,0:T(8,128)(2,1)S(1)} %collective-permute-done.9.refs_1_, bf16[512,256]{1,0:T(8,128)(2,1)S(1)} %collective-permute-done.10.refs_2_, ...), custom_call_target="tpu_custom_call" | custom-call | flops 20000000000 | bytes 1024 | tf_op jit(solution)/shard_map/mix/pallas_call | solution.py:208
  101.9 2.2 %collective-permute-done.33.refs_7_ = bf16[256,256]{1,0:T(8,128)(2,1)S(1)} collective-permute-done((bf16[256,256]{1,0:T(8,128)(2,1)S(1)}, bf16[256,256]{1,0:T(8,128)(2,1)S(1)}, u32[]{:S(2)}, u32[]{:S(2)}) %collective-permute-start.33) | collective-permute-done | bytes 131104 | tf_op jit(solution)/shard_map/up15c3/ppermute | solution.py:377
  105.3 1.9 %mix.7 = (bf16[5,512,256]{2,1,0:T(8,128)(2,1)S(1)}, bf16[5,512,256]{2,1,0:T(8,128)(2,1)S(1)}) custom-call(bf16[512,256]{1,0:T(8,128)(2,1)S(1)} %copy-done, bf16[512,256]{1,0:T(8,128)(2,1)S(1)} %collective-permute-done.23.refs_1_, bf16[512,256]{1,0:T(8,128)(2,1)S(1)} %collective-permute-done.24.refs_2_, bf16[512,256]{1,0:T(8,128)(2,1)S(1)} %collective-permute-done.26.refs_3_, ...), custom_call_target="tpu_custom_call" | custom-call | flops 20000000000 | bytes 1024 | tf_op jit(solution)/shard_map/mix/pallas_call | solution.py:208
  108.4 7.5 %gram2.1.refs_0_ = bf16[4,2048,2048]{2,1,0:T(8,128)(2,1)} custom-call(bf16[4,2048,2048]{2,1,0:T(8,128)(2,1)} %gram1.1.refs_0_, bf16[5,512,256]{2,1,0:T(8,128)(2,1)S(1)} %get-tuple-element.104.refs_0_.refs_1_, bf16[5,512,256]{2,1,0:T(8,128)(2,1)S(1)} %get-tuple-element.122.refs_2_, ...), custom_call_target="tpu_custom_call", output_to_operand_aliasing={{}: (0, {})} | custom-call | flops 20000000000 | bytes 1024 | tf_op jit(solution)/shard_map/gram2/pallas_call | solution.py:290
  115.9 10.1 %gram3.1 = bf16[4,2048,2048]{2,1,0:T(8,128)(2,1)} custom-call(bf16[4,2048,2048]{2,1,0:T(8,128)(2,1)} %gram2.1.refs_0_, bf16[5,512,256]{2,1,0:T(8,128)(2,1)S(1)} %get-tuple-element.104.refs_0_.refs_1_, bf16[5,512,256]{2,1,0:T(8,128)(2,1)S(1)} %get-tuple-element.122.refs_2_, ...), custom_call_target="tpu_custom_call", output_to_operand_aliasing={{}: (0, {})} | custom-call | flops 20000000000 | bytes 1024 | tf_op jit(solution)/shard_map/gram3/pallas_call | solution.py:290
  (73 shorter events, 25.0 us)
Async XLA Ops:
  13.1 7.0 %collective-permute-start.2 = (bf16[512,256]{1,0:T(8,128)(2,1)}, bf16[512,256]{1,0:T(8,128)(2,1)S(1)}, u32[]{:S(2)}, u32[]{:S(2)}) collective-permute-start(bf16[512,256]{1,0:T(8,128)(2,1)} %get-tuple-element.90.refs_0_), channel_id=1, source_target_pairs={{4,0},{8,4},{12,8},{14,12},{10,14},{6,10},{2,6},{0,2},{5,1},{9,5},... | collective-permute-start | bytes 786440 | tf_op jit(solution)/shard_map/down0c0/ppermute | solution.py:379
  15.5 6.6 %collective-permute-start.1 = (bf16[512,256]{1,0:T(8,128)(2,1)}, bf16[512,256]{1,0:T(8,128)(2,1)S(1)}, u32[]{:S(2)}, u32[]{:S(2)}) collective-permute-start(bf16[512,256]{1,0:T(8,128)(2,1)} %get-tuple-element.90.refs_0_), channel_id=1, source_target_pairs={{0,4},{4,8},{8,12},{12,14},{14,10},{10,6},{6,2},{2,0},{1,5},{5,9},... | collective-permute-start | bytes 786440 | tf_op jit(solution)/shard_map/up0c0/ppermute | solution.py:377
  15.6 9.3 %collective-permute-start.6 = (bf16[512,256]{1,0:T(8,128)(2,1)}, bf16[512,256]{1,0:T(8,128)(2,1)S(1)}, u32[]{:S(2)}, u32[]{:S(2)}) collective-permute-start(bf16[512,256]{1,0:T(8,128)(2,1)} %get-tuple-element.110.refs_0_), channel_id=1, source_target_pairs={{4,0},{8,4},{12,8},{14,12},{10,14},{6,10},{2,6},{0,2},{5,1},{9,5},... | collective-permute-start | bytes 786440 | tf_op jit(solution)/shard_map/down1c1/ppermute | solution.py:379
  17.5 9.9 %collective-permute-start.5 = (bf16[512,256]{1,0:T(8,128)(2,1)}, bf16[512,256]{1,0:T(8,128)(2,1)S(1)}, u32[]{:S(2)}, u32[]{:S(2)}) collective-permute-start(bf16[512,256]{1,0:T(8,128)(2,1)} %get-tuple-element.110.refs_0_), channel_id=1, source_target_pairs={{0,4},{4,8},{8,12},{12,14},{14,10},{10,6},{6,2},{2,0},{1,5},{5,9},... | collective-permute-start | bytes 786440 | tf_op jit(solution)/shard_map/up1c1/ppermute | solution.py:377
  20.1 10.4 %collective-permute-start.4 = (bf16[512,256]{1,0:T(8,128)(2,1)S(1)}, bf16[512,256]{1,0:T(8,128)(2,1)S(1)}, u32[]{:S(2)}, u32[]{:S(2)}) collective-permute-start(bf16[512,256]{1,0:T(8,128)(2,1)S(1)} %collective-permute-done.2.refs_2_), channel_id=1, source_target_pairs={{4,0},{8,4},{12,8},{14,12},{10,14},{6,10},{2,6},{0,2},{5,1},{9,5},... | collective-permute-start | bytes 786440 | tf_op jit(solution)/shard_map/down2c0/ppermute | solution.py:379
  22.1 10.9 %collective-permute-start.3 = (bf16[512,256]{1,0:T(8,128)(2,1)S(1)}, bf16[512,256]{1,0:T(8,128)(2,1)S(1)}, u32[]{:S(2)}, u32[]{:S(2)}) collective-permute-start(bf16[512,256]{1,0:T(8,128)(2,1)S(1)} %collective-permute-done.1.refs_1_), channel_id=1, source_target_pairs={{0,4},{4,8},{8,12},{12,14},{14,10},{10,6},{6,2},{2,0},{1,5},{5,9},... | collective-permute-start | bytes 786440 | tf_op jit(solution)/shard_map/up2c0/ppermute | solution.py:377
  27.4 11.2 %collective-permute-start.13 = (bf16[512,256]{1,0:T(8,128)(2,1)S(1)}, bf16[512,256]{1,0:T(8,128)(2,1)S(1)}, u32[]{:S(2)}, u32[]{:S(2)}) collective-permute-start(bf16[512,256]{1,0:T(8,128)(2,1)S(1)} %collective-permute-done.5.refs_1_), channel_id=1, source_target_pairs={{0,4},{4,8},{8,12},{12,14},{14,10},{10,6},{6,2},{2,0},{1,5},{5,9},... | collective-permute-start | bytes 786440 | tf_op jit(solution)/shard_map/up3c1/ppermute | solution.py:377
  27.4 12.8 %collective-permute-start.14 = (bf16[512,256]{1,0:T(8,128)(2,1)S(1)}, bf16[512,256]{1,0:T(8,128)(2,1)S(1)}, u32[]{:S(2)}, u32[]{:S(2)}) collective-permute-start(bf16[512,256]{1,0:T(8,128)(2,1)S(1)} %collective-permute-done.6.refs_2_), channel_id=1, source_target_pairs={{4,0},{8,4},{12,8},{14,12},{10,14},{6,10},{2,6},{0,2},{5,1},{9,5},... | collective-permute-start | bytes 786440 | tf_op jit(solution)/shard_map/down3c1/ppermute | solution.py:379
  29.4 14.8 %collective-permute-start.9 = (bf16[512,256]{1,0:T(8,128)(2,1)}, bf16[512,256]{1,0:T(8,128)(2,1)S(1)}, u32[]{:S(2)}, u32[]{:S(2)}) collective-permute-start(bf16[512,256]{1,0:T(8,128)(2,1)} %get-tuple-element.129.refs_0_), channel_id=1, source_target_pairs={{0,4},{4,8},{8,12},{12,14},{14,10},{10,6},{6,2},{2,0},{1,5},{5,9},... | collective-permute-start | bytes 786440 | tf_op jit(solution)/shard_map/up4c2/ppermute | solution.py:377
  30.5 15.3 %collective-permute-start.10 = (bf16[512,256]{1,0:T(8,128)(2,1)}, bf16[512,256]{1,0:T(8,128)(2,1)S(1)}, u32[]{:S(2)}, u32[]{:S(2)}) collective-permute-start(bf16[512,256]{1,0:T(8,128)(2,1)} %get-tuple-element.129.refs_0_), channel_id=1, source_target_pairs={{4,0},{8,4},{12,8},{14,12},{10,14},{6,10},{2,6},{0,2},{5,1},{9,5},... | collective-permute-start | bytes 786440 | tf_op jit(solution)/shard_map/down4c2/ppermute | solution.py:379
  33.0 16.9 %collective-permute-start.7 = (bf16[512,256]{1,0:T(8,128)(2,1)S(1)}, bf16[512,256]{1,0:T(8,128)(2,1)S(1)}, u32[]{:S(2)}, u32[]{:S(2)}) collective-permute-start(bf16[512,256]{1,0:T(8,128)(2,1)S(1)} %collective-permute-done.3.refs_3_), channel_id=1, source_target_pairs={{0,4},{4,8},{8,12},{12,14},{14,10},{10,6},{6,2},{2,0},{1,5},{5,9},... | collective-permute-start | bytes 786440 | tf_op jit(solution)/shard_map/up5c0/ppermute | solution.py:377
  38.7 12.8 %collective-permute-start.8 = (bf16[512,256]{1,0:T(8,128)(2,1)S(1)}, bf16[512,256]{1,0:T(8,128)(2,1)S(1)}, u32[]{:S(2)}, u32[]{:S(2)}) collective-permute-start(bf16[512,256]{1,0:T(8,128)(2,1)S(1)} %collective-permute-done.4.refs_4_), channel_id=1, source_target_pairs={{4,0},{8,4},{12,8},{14,12},{10,14},{6,10},{2,6},{0,2},{5,1},{9,5},... | collective-permute-start | bytes 786440 | tf_op jit(solution)/shard_map/down5c0/ppermute | solution.py:379
  40.2 15.3 %collective-permute-start.15 = (bf16[512,256]{1,0:T(8,128)(2,1)S(1)}, bf16[512,256]{1,0:T(8,128)(2,1)S(1)}, u32[]{:S(2)}, u32[]{:S(2)}) collective-permute-start(bf16[512,256]{1,0:T(8,128)(2,1)S(1)} %collective-permute-done.13.refs_3_), channel_id=1, source_target_pairs={{0,4},{4,8},{8,12},{12,14},{14,10},{10,6},{6,2},{2,0},{1,5},{5,9},... | collective-permute-start | bytes 786440 | tf_op jit(solution)/shard_map/up6c1/ppermute | solution.py:377
  44.3 12.8 %collective-permute-start.16 = (bf16[512,256]{1,0:T(8,128)(2,1)S(1)}, bf16[512,256]{1,0:T(8,128)(2,1)S(1)}, u32[]{:S(2)}, u32[]{:S(2)}) collective-permute-start(bf16[512,256]{1,0:T(8,128)(2,1)S(1)} %collective-permute-done.14.refs_4_), channel_id=1, source_target_pairs={{4,0},{8,4},{12,8},{14,12},{10,14},{6,10},{2,6},{0,2},{5,1},{9,5},... | collective-permute-start | bytes 786440 | tf_op jit(solution)/shard_map/down6c1/ppermute | solution.py:379
  45.8 15.3 %collective-permute-start.19 = (bf16[512,256]{1,0:T(8,128)(2,1)S(1)}, bf16[512,256]{1,0:T(8,128)(2,1)S(1)}, u32[]{:S(2)}, u32[]{:S(2)}) collective-permute-start(bf16[512,256]{1,0:T(8,128)(2,1)S(1)} %collective-permute-done.9.refs_1_), channel_id=1, source_target_pairs={{0,4},{4,8},{8,12},{12,14},{14,10},{10,6},{6,2},{2,0},{1,5},{5,9},... | collective-permute-start | bytes 786440 | tf_op jit(solution)/shard_map/up7c2/ppermute | solution.py:377
  49.9 12.8 %collective-permute-start.20 = (bf16[512,256]{1,0:T(8,128)(2,1)S(1)}, bf16[512,256]{1,0:T(8,128)(2,1)S(1)}, u32[]{:S(2)}, u32[]{:S(2)}) collective-permute-start(bf16[512,256]{1,0:T(8,128)(2,1)S(1)} %collective-permute-done.10.refs_2_), channel_id=1, source_target_pairs={{4,0},{8,4},{12,8},{14,12},{10,14},{6,10},{2,6},{0,2},{5,1},{9,5},... | collective-permute-start | bytes 786440 | tf_op jit(solution)/shard_map/down7c2/ppermute | solution.py:379
  51.5 12.4 %collective-permute-start.11 = (bf16[256,256]{1,0:T(8,128)(2,1)S(1)}, bf16[256,256]{1,0:T(8,128)(2,1)S(1)}, u32[]{:S(2)}, u32[]{:S(2)}) collective-permute-start(bf16[256,256]{1,0:T(8,128)(2,1)S(1)} %slice.32), channel_id=1, source_target_pairs={{0,4},{4,8},{8,12},{12,14},{14,10},{10,6},{6,2},{2,0},{1,5},{5,9},... | collective-permute-start | bytes 393224 | tf_op jit(solution)/shard_map/up8c0/ppermute | solution.py:377
  55.5 10.0 %collective-permute-start.12 = (bf16[256,256]{1,0:T(8,128)(2,1)S(1)}, bf16[256,256]{1,0:T(8,128)(2,1)S(1)}, u32[]{:S(2)}, u32[]{:S(2)}) collective-permute-start(bf16[256,256]{1,0:T(8,128)(2,1)S(1)} %slice.33), channel_id=1, source_target_pairs={{4,0},{8,4},{12,8},{14,12},{10,14},{6,10},{2,6},{0,2},{5,1},{9,5},... | collective-permute-start | bytes 393224 | tf_op jit(solution)/shard_map/down8c0/ppermute | solution.py:379
  57.1 9.6 %collective-permute-start.17 = (bf16[256,256]{1,0:T(8,128)(2,1)S(1)}, bf16[256,256]{1,0:T(8,128)(2,1)S(1)}, u32[]{:S(2)}, u32[]{:S(2)}) collective-permute-start(bf16[256,256]{1,0:T(8,128)(2,1)S(1)} %slice.34), channel_id=1, source_target_pairs={{0,4},{4,8},{8,12},{12,14},{14,10},{10,6},{6,2},{2,0},{1,5},{5,9},... | collective-permute-start | bytes 393224 | tf_op jit(solution)/shard_map/up9c1/ppermute | solution.py:377
  62.7 9.7 %collective-permute-start.23 = (bf16[512,256]{1,0:T(8,128)(2,1)}, bf16[512,256]{1,0:T(8,128)(2,1)S(1)}, u32[]{:S(2)}, u32[]{:S(2)}) collective-permute-start(bf16[512,256]{1,0:T(8,128)(2,1)} %get-tuple-element.108.refs_0_), channel_id=1, source_target_pairs={{0,4},{4,8},{8,12},{12,14},{14,10},{10,6},{6,2},{2,0},{1,5},{5,9},... | collective-permute-start | bytes 786440 | tf_op jit(solution)/shard_map/up10c3/ppermute | solution.py:377
  63.9 8.4 %collective-permute-start.24 = (bf16[512,256]{1,0:T(8,128)(2,1)}, bf16[512,256]{1,0:T(8,128)(2,1)S(1)}, u32[]{:S(2)}, u32[]{:S(2)}) collective-permute-start(bf16[512,256]{1,0:T(8,128)(2,1)} %get-tuple-element.108.refs_0_), channel_id=1, source_target_pairs={{4,0},{8,4},{12,8},{14,12},{10,14},{6,10},{2,6},{0,2},{5,1},{9,5},... | collective-permute-start | bytes 786440 | tf_op jit(solution)/shard_map/down10c3/ppermute | solution.py:379
  67.2 14.9 %collective-permute-start.21 = (bf16[512,256]{1,0:T(8,128)(2,1)S(1)}, bf16[512,256]{1,0:T(8,128)(2,1)S(1)}, u32[]{:S(2)}, u32[]{:S(2)}) collective-permute-start(bf16[512,256]{1,0:T(8,128)(2,1)S(1)} %collective-permute-done.19.refs_3_), channel_id=1, source_target_pairs={{0,4},{4,8},{8,12},{12,14},{14,10},{10,6},{6,2},{2,0},{1,5},{5,9},... | collective-permute-start | bytes 786440 | tf_op jit(solution)/shard_map/up11c2/ppermute | solution.py:377
  67.6 14.5 %collective-permute-start.22 = (bf16[512,256]{1,0:T(8,128)(2,1)S(1)}, bf16[512,256]{1,0:T(8,128)(2,1)S(1)}, u32[]{:S(2)}, u32[]{:S(2)}) collective-permute-start(bf16[512,256]{1,0:T(8,128)(2,1)S(1)} %collective-permute-done.20.refs_4_), channel_id=1, source_target_pairs={{4,0},{8,4},{12,8},{14,12},{10,14},{6,10},{2,6},{0,2},{5,1},{9,5},... | collective-permute-start | bytes 786440 | tf_op jit(solution)/shard_map/down11c2/ppermute | solution.py:379
  72.4 11.4 %collective-permute-start.26 = (bf16[512,256]{1,0:T(8,128)(2,1)S(1)}, bf16[512,256]{1,0:T(8,128)(2,1)S(1)}, u32[]{:S(2)}, u32[]{:S(2)}) collective-permute-start(bf16[512,256]{1,0:T(8,128)(2,1)S(1)} %collective-permute-done.23.refs_1_), channel_id=1, source_target_pairs={{0,4},{4,8},{8,12},{12,14},{14,10},{10,6},{6,2},{2,0},{1,5},{5,9},... | collective-permute-start | bytes 786440 | tf_op jit(solution)/shard_map/up12c3/ppermute | solution.py:377
  72.6 11.1 %collective-permute-start.27 = (bf16[512,256]{1,0:T(8,128)(2,1)S(1)}, bf16[512,256]{1,0:T(8,128)(2,1)S(1)}, u32[]{:S(2)}, u32[]{:S(2)}) collective-permute-start(bf16[512,256]{1,0:T(8,128)(2,1)S(1)} %collective-permute-done.24.refs_2_), channel_id=1, source_target_pairs={{4,0},{8,4},{12,8},{14,12},{10,14},{6,10},{2,6},{0,2},{5,1},{9,5},... | collective-permute-start | bytes 786440 | tf_op jit(solution)/shard_map/down12c3/ppermute | solution.py:379
  74.4 9.4 %collective-permute-start.25 = (bf16[5,512,256]{2,1,0:T(8,128)(2,1)S(1)}, bf16[5,512,256]{2,1,0:T(8,128)(2,1)S(1)}, u32[]{:S(2)}, u32[]{:S(2)}) collective-permute-start(bf16[5,512,256]{2,1,0:T(8,128)(2,1)S(1)} %get-tuple-element.109), channel_id=1, source_target_pairs={{0,1},{1,0},{2,3},{3,2},{4,5},{5,4},{6,7},{7,6},{8,9},{9,8},{10,11... | collective-permute-start | bytes 3932168 | tf_op jit(solution)/shard_map/swap0/ppermute | solution.py:361
  82.1 6.8 %collective-permute-start.28 = (bf16[5,512,256]{2,1,0:T(8,128)(2,1)S(1)}, bf16[5,512,256]{2,1,0:T(8,128)(2,1)S(1)}, u32[]{:S(2)}, u32[]{:S(2)}) collective-permute-start(bf16[5,512,256]{2,1,0:T(8,128)(2,1)S(1)} %get-tuple-element.124), channel_id=1, source_target_pairs={{0,1},{1,0},{2,3},{3,2},{4,5},{5,4},{6,7},{7,6},{8,9},{9,8},{10,11... | collective-permute-start | bytes 3932168 | tf_op jit(solution)/shard_map/swap1/ppermute | solution.py:361
  83.8 12.2 %collective-permute-start.29 = (bf16[256,256]{1,0:T(8,128)(2,1)S(1)}, bf16[256,256]{1,0:T(8,128)(2,1)S(1)}, u32[]{:S(2)}, u32[]{:S(2)}) collective-permute-start(bf16[256,256]{1,0:T(8,128)(2,1)S(1)} %slice.36), channel_id=1, source_target_pairs={{0,4},{4,8},{8,12},{12,14},{14,10},{10,6},{6,2},{2,0},{1,5},{5,9},... | collective-permute-start | bytes 393224 | tf_op jit(solution)/shard_map/up13c2/ppermute | solution.py:377
  84.5 11.5 %collective-permute-start.30 = (bf16[256,256]{1,0:T(8,128)(2,1)S(1)}, bf16[256,256]{1,0:T(8,128)(2,1)S(1)}, u32[]{:S(2)}, u32[]{:S(2)}) collective-permute-start(bf16[256,256]{1,0:T(8,128)(2,1)S(1)} %slice.37), channel_id=1, source_target_pairs={{4,0},{8,4},{12,8},{14,12},{10,14},{6,10},{2,6},{0,2},{5,1},{9,5},... | collective-permute-start | bytes 393224 | tf_op jit(solution)/shard_map/down13c2/ppermute | solution.py:379
  88.9 8.1 %collective-permute-start.31 = (bf16[512,256]{1,0:T(8,128)(2,1)S(1)}, bf16[512,256]{1,0:T(8,128)(2,1)S(1)}, u32[]{:S(2)}, u32[]{:S(2)}) collective-permute-start(bf16[512,256]{1,0:T(8,128)(2,1)S(1)} %collective-permute-done.26.refs_3_), channel_id=1, source_target_pairs={{0,4},{4,8},{8,12},{12,14},{14,10},{10,6},{6,2},{2,0},{1,5},{5,9},... | collective-permute-start | bytes 786440 | tf_op jit(solution)/shard_map/up14c3/ppermute | solution.py:377
  89.6 8.4 %collective-permute-start.32 = (bf16[512,256]{1,0:T(8,128)(2,1)S(1)}, bf16[512,256]{1,0:T(8,128)(2,1)S(1)}, u32[]{:S(2)}, u32[]{:S(2)}) collective-permute-start(bf16[512,256]{1,0:T(8,128)(2,1)S(1)} %collective-permute-done.27.refs_4_), channel_id=1, source_target_pairs={{4,0},{8,4},{12,8},{14,12},{10,14},{6,10},{2,6},{0,2},{5,1},{9,5},... | collective-permute-start | bytes 786440 | tf_op jit(solution)/shard_map/down14c3/ppermute | solution.py:379
  107.3 8.6 %collective-permute-start.36 = (bf16[5,512,256]{2,1,0:T(8,128)(2,1)S(1)}, bf16[5,512,256]{2,1,0:T(8,128)(2,1)S(1)}, u32[]{:S(2)}, u32[]{:S(2)}) collective-permute-start(bf16[5,512,256]{2,1,0:T(8,128)(2,1)S(1)} %get-tuple-element.144), channel_id=1, source_target_pairs={{0,1},{1,0},{2,3},{3,2},{4,5},{5,4},{6,7},{7,6},{8,9},{9,8},{10,11... | collective-permute-start | bytes 3932168 | tf_op jit(solution)/shard_map/swap3/ppermute | solution.py:361
  (11 other events, 65.4 us)

commit v4 on v3

--- a/solution.py
+++ b/solution.py
@@ -301,7 +301,7 @@
     )(*(([out] if aliased else []) + keeps + recvs))
 
 
-PLANS = {(16, 4): ([4, 4, 4, 4], [0, 1, 0, 1, 2, 0, 1, 2, 0, 1, 3, 2, 3, 2, 3, 3])}
+PLANS = {(16, 4): ([4, 4, 4, 4], [0, 1, 0, 1, 2, 0, 1, 0, 2, 1, 3, 2, 3, 2, 3, 3])}
 
 
 def plan(local_heads, hops):

time: 126 us -> 127 us (level)
  waiting for transfers between devices: 38.6 us -> 42 us
  starting transfers between devices: 43.5 us -> 41.1 us
    ppermute x16, waiting for transfers between devices: 28.2 us -> 31.5 us  [local(): going = lax.ppermute(going, 'head', forward)]
    ppermute x4, starting transfers between devices: 8.12 us -> 5.99 us  [compute(): recvs[c] = lax.ppermute(sends[c], 'tok', [(0, 1), (1, 0)])]
where the time goes in v4:
time: 127 us
  waiting for transfers between devices  42 us (33%)
  starting transfers between devices  41.1 us (32%)
  Pallas kernels  41 us (32%)
  local copies, waits for them, and re-layouts  2.58 us (2%)
    ppermute x16, waiting for transfers between devices, local(): going = lax.ppermute(going, 'head', forward)  31.5 us
    ppermute x16, starting transfers between devices, local(): coming = lax.ppermute(coming, 'head', backward)  26.5 us
    pallas_call x4, Pallas kernels, gram(): pl.pallas_call(functools.partial(gram_kernel, starts, sizes, chunk, alias...  25.6 us
    ppermute x16, waiting for transfers between devices, local(): coming = lax.ppermute(coming, 'head', backward)  9.07 us
    pallas_call x1, Pallas kernels, attend(): pl.pallas_call(functools.partial(attend_kernel, ATTEND_UNROLL, heads_of),...  8.18 us
    pallas_call x4, Pallas kernels, mix(): pl.pallas_call(functools.partial(mix_kernel, devices, scale), in_specs=[p...  7.21 us
    ppermute x16, starting transfers between devices, local(): going = lax.ppermute(going, 'head', forward)  6.22 us
    ppermute x4, starting transfers between devices, compute(): recvs[c] = lax.ppermute(sends[c], 'tok', [(0, 1), (1, 0)])  5.99 us
  transfers between devices with their start and end apart: 37, of which 20 were waited for; matrix products, arithmetic and copies ran while one was open for 0% of the time, Pallas kernels for 18%

profile of v4, /device:TPU:0, one launch (start us, length us, event | category | flops | bytes accessed | tf_op | source)
XLA Modules:
  0.0 127.1 jit_solution(3585400402286775898)
XLA Ops:
  0.9 2.4 %collective-permute-start = (bf16[256,256]{1,0:T(8,128)(2,1)S(1)}, bf16[256,256]{1,0:T(8,128)(2,1)S(1)}, u32[]{:S(2)}, u32[]{:S(2)}) collective-permute-start(bf16[256,256]{1,0:T(8,128)(2,1)S(1)} %pad_maximum_fusion.own_any), channel_id=1, source_target_pairs={{0,1},{2,3},{4,5},{6,7},{8,9},{10,11},{12,13},{14,15},{16,17},{18,... | collective-permute-start | bytes 393224 | tf_op jit(solution)/shard_map/ppermute | solution.py:337
  4.9 8.2 %attend.1 = (bf16[512,256]{1,0:T(8,128)(2,1)}, bf16[512,256]{1,0:T(8,128)(2,1)}, bf16[512,256]{1,0:T(8,128)(2,1)}, bf16[512,256]{1,0:T(8,128)(2,1)}) custom-call(bf16[256,2048]{1,0:T(8,128)(2,1)} %q_hbm.1, s32[128,128]{1,0:T(8,128)} %bitcast.2, bf16[256,256]{1,0:T(8,128)(2,1)} %copy-done.4, bf16[256,256]{1,0:T(8,128)(2,1)} %copy-done.5), custom_call_target="tpu_custom_call" | custom-call | flops 20000000000 | bytes 1024 | tf_op jit(solution)/shard_map/attend/pallas_call | solution.py:129
  13.1 2.4 %collective-permute-start.2 = (bf16[512,256]{1,0:T(8,128)(2,1)}, bf16[512,256]{1,0:T(8,128)(2,1)S(1)}, u32[]{:S(2)}, u32[]{:S(2)}) collective-permute-start(bf16[512,256]{1,0:T(8,128)(2,1)} %get-tuple-element.88.refs_0_), channel_id=1, source_target_pairs={{4,0},{8,4},{12,8},{14,12},{10,14},{6,10},{2,6},{0,2},{5,1},{9,5},... | collective-permute-start | bytes 786440 | tf_op jit(solution)/shard_map/down0c0/ppermute | solution.py:379
  15.6 1.9 %collective-permute-start.6 = (bf16[512,256]{1,0:T(8,128)(2,1)}, bf16[512,256]{1,0:T(8,128)(2,1)S(1)}, u32[]{:S(2)}, u32[]{:S(2)}) collective-permute-start(bf16[512,256]{1,0:T(8,128)(2,1)} %get-tuple-element.108.refs_0_), channel_id=1, source_target_pairs={{4,0},{8,4},{12,8},{14,12},{10,14},{6,10},{2,6},{0,2},{5,1},{9,5},... | collective-permute-start | bytes 786440 | tf_op jit(solution)/shard_map/down1c1/ppermute | solution.py:379
  17.7 2.5 %collective-permute-done.2.refs_2_ = bf16[512,256]{1,0:T(8,128)(2,1)S(1)} collective-permute-done((bf16[512,256]{1,0:T(8,128)(2,1)}, bf16[512,256]{1,0:T(8,128)(2,1)S(1)}, u32[]{:S(2)}, u32[]{:S(2)}) %collective-permute-start.2) | collective-permute-done | bytes 262176 | tf_op jit(solution)/shard_map/down0c0/ppermute | solution.py:379
  20.1 2.0 %collective-permute-start.4 = (bf16[512,256]{1,0:T(8,128)(2,1)S(1)}, bf16[512,256]{1,0:T(8,128)(2,1)S(1)}, u32[]{:S(2)}, u32[]{:S(2)}) collective-permute-start(bf16[512,256]{1,0:T(8,128)(2,1)S(1)} %collective-permute-done.2.refs_2_), channel_id=1, source_target_pairs={{4,0},{8,4},{12,8},{14,12},{10,14},{6,10},{2,6},{0,2},{5,1},{9,5},... | collective-permute-start | bytes 786440 | tf_op jit(solution)/shard_map/down2c0/ppermute | solution.py:379
  22.2 2.7 %collective-permute-done.6.refs_2_ = bf16[512,256]{1,0:T(8,128)(2,1)S(1)} collective-permute-done((bf16[512,256]{1,0:T(8,128)(2,1)}, bf16[512,256]{1,0:T(8,128)(2,1)S(1)}, u32[]{:S(2)}, u32[]{:S(2)}) %collective-permute-start.6) | collective-permute-done | bytes 262176 | tf_op jit(solution)/shard_map/down1c1/ppermute | solution.py:379
  24.9 2.5 %collective-permute-done.5.refs_1_ = bf16[512,256]{1,0:T(8,128)(2,1)S(1)} collective-permute-done((bf16[512,256]{1,0:T(8,128)(2,1)}, bf16[512,256]{1,0:T(8,128)(2,1)S(1)}, u32[]{:S(2)}, u32[]{:S(2)}) %collective-permute-start.5) | collective-permute-done | bytes 262176 | tf_op jit(solution)/shard_map/up1c1/ppermute | solution.py:377
  27.4 2.0 %collective-permute-start.10 = (bf16[512,256]{1,0:T(8,128)(2,1)S(1)}, bf16[512,256]{1,0:T(8,128)(2,1)S(1)}, u32[]{:S(2)}, u32[]{:S(2)}) collective-permute-start(bf16[512,256]{1,0:T(8,128)(2,1)S(1)} %collective-permute-done.6.refs_2_), channel_id=1, source_target_pairs={{4,0},{8,4},{12,8},{14,12},{10,14},{6,10},{2,6},{0,2},{5,1},{9,5},... | collective-permute-start | bytes 786440 | tf_op jit(solution)/shard_map/down3c1/ppermute | solution.py:379
  30.5 2.2 %collective-permute-start.12 = (bf16[512,256]{1,0:T(8,128)(2,1)}, bf16[512,256]{1,0:T(8,128)(2,1)S(1)}, u32[]{:S(2)}, u32[]{:S(2)}) collective-permute-start(bf16[512,256]{1,0:T(8,128)(2,1)} %get-tuple-element.129.refs_0_), channel_id=1, source_target_pairs={{4,0},{8,4},{12,8},{14,12},{10,14},{6,10},{2,6},{0,2},{5,1},{9,5},... | collective-permute-start | bytes 786440 | tf_op jit(solution)/shard_map/down4c2/ppermute | solution.py:379
  33.0 5.6 %collective-permute-done.9.refs_3_ = bf16[512,256]{1,0:T(8,128)(2,1)S(1)} collective-permute-done((bf16[512,256]{1,0:T(8,128)(2,1)S(1)}, bf16[512,256]{1,0:T(8,128)(2,1)S(1)}, u32[]{:S(2)}, u32[]{:S(2)}) %collective-permute-start.9) | collective-permute-done | bytes 262176 | tf_op jit(solution)/shard_map/up3c1/ppermute | solution.py:377
  40.7 3.6 %collective-permute-done.11.refs_1_ = bf16[512,256]{1,0:T(8,128)(2,1)S(1)} collective-permute-done((bf16[512,256]{1,0:T(8,128)(2,1)}, bf16[512,256]{1,0:T(8,128)(2,1)S(1)}, u32[]{:S(2)}, u32[]{:S(2)}) %collective-permute-start.11) | collective-permute-done | bytes 262176 | tf_op jit(solution)/shard_map/up4c2/ppermute | solution.py:377
  45.8 4.0 %collective-permute-done.7.refs_5_ = bf16[512,256]{1,0:T(8,128)(2,1)S(1)} collective-permute-done((bf16[512,256]{1,0:T(8,128)(2,1)S(1)}, bf16[512,256]{1,0:T(8,128)(2,1)S(1)}, u32[]{:S(2)}, u32[]{:S(2)}) %collective-permute-start.7) | collective-permute-done | bytes 262176 | tf_op jit(solution)/shard_map/up5c0/ppermute | solution.py:377
  50.0 1.9 %collective-permute-start.16 = (bf16[512,256]{1,0:T(8,128)(2,1)S(1)}, bf16[512,256]{1,0:T(8,128)(2,1)S(1)}, u32[]{:S(2)}, u32[]{:S(2)}) collective-permute-start(bf16[512,256]{1,0:T(8,128)(2,1)S(1)} %collective-permute-done.12.refs_2_), channel_id=1, source_target_pairs={{4,0},{8,4},{12,8},{14,12},{10,14},{6,10},{2,6},{0,2},{5,1},{9,5},... | collective-permute-start | bytes 786440 | tf_op jit(solution)/shard_map/down8c2/ppermute | solution.py:379
  52.1 3.4 %collective-permute-done.17.refs_5_ = bf16[512,256]{1,0:T(8,128)(2,1)S(1)} collective-permute-done((bf16[512,256]{1,0:T(8,128)(2,1)S(1)}, bf16[512,256]{1,0:T(8,128)(2,1)S(1)}, u32[]{:S(2)}, u32[]{:S(2)}) %collective-permute-start.17) | collective-permute-done | bytes 262176 | tf_op jit(solution)/shard_map/up6c1/ppermute | solution.py:377
  57.6 6.3 %collective-permute-done.13.refs_7_ = bf16[256,256]{1,0:T(8,128)(2,1)S(1)} collective-permute-done((bf16[256,256]{1,0:T(8,128)(2,1)S(1)}, bf16[256,256]{1,0:T(8,128)(2,1)S(1)}, u32[]{:S(2)}, u32[]{:S(2)}) %collective-permute-start.13) | collective-permute-done | bytes 131104 | tf_op jit(solution)/shard_map/up7c0/ppermute | solution.py:377
  68.5 1.7 %mix.4 = (bf16[5,512,256]{2,1,0:T(8,128)(2,1)S(1)}, bf16[5,512,256]{2,1,0:T(8,128)(2,1)S(1)}) custom-call(bf16[512,256]{1,0:T(8,128)(2,1)S(1)} %copy-done.3, bf16[512,256]{1,0:T(8,128)(2,1)S(1)} %collective-permute-done.1.refs_1_, bf16[512,256]{1,0:T(8,128)(2,1)S(1)} %collective-permute-done.2.refs_2_, bf16[512,256]{1,0:T(8,128)(2,1)S(1)} %collective-permute-done.3.refs_3_, ...), custom_call_target="tpu_custom_call" | custom-call | flops 20000000000 | bytes 1024 | tf_op jit(solution)/shard_map/mix/pallas_call | solution.py:208
  72.3 3.2 %collective-permute-start.23 = (bf16[5,512,256]{2,1,0:T(8,128)(2,1)S(1)}, bf16[5,512,256]{2,1,0:T(8,128)(2,1)S(1)}, u32[]{:S(2)}, u32[]{:S(2)}) collective-permute-start(bf16[5,512,256]{2,1,0:T(8,128)(2,1)S(1)} %get-tuple-element.107), channel_id=1, source_target_pairs={{0,1},{1,0},{2,3},{3,2},{4,5},{5,4},{6,7},{7,6},{8,9},{9,8},{10,11... | collective-permute-start | bytes 3932168 | tf_op jit(solution)/shard_map/swap0/ppermute | solution.py:361
  75.6 1.8 %mix.5 = (bf16[5,512,256]{2,1,0:T(8,128)(2,1)S(1)}, bf16[5,512,256]{2,1,0:T(8,128)(2,1)S(1)}) custom-call(bf16[512,256]{1,0:T(8,128)(2,1)S(1)} %copy-done.2, bf16[512,256]{1,0:T(8,128)(2,1)S(1)} %collective-permute-done.5.refs_1_, bf16[512,256]{1,0:T(8,128)(2,1)S(1)} %collective-permute-done.6.refs_2_, bf16[512,256]{1,0:T(8,128)(2,1)S(1)} %collective-permute-done.9.refs_3_, ...), custom_call_target="tpu_custom_call" | custom-call | flops 20000000000 | bytes 1024 | tf_op jit(solution)/shard_map/mix/pallas_call | solution.py:208
  77.4 2.1 %collective-permute-done.26.refs_5_ = bf16[512,256]{1,0:T(8,128)(2,1)S(1)} collective-permute-done((bf16[512,256]{1,0:T(8,128)(2,1)S(1)}, bf16[512,256]{1,0:T(8,128)(2,1)S(1)}, u32[]{:S(2)}, u32[]{:S(2)}) %collective-permute-start.26) | collective-permute-done | bytes 262176 | tf_op jit(solution)/shard_map/up11c2/ppermute | solution.py:377
  80.0 2.2 %collective-permute-start.28 = (bf16[5,512,256]{2,1,0:T(8,128)(2,1)S(1)}, bf16[5,512,256]{2,1,0:T(8,128)(2,1)S(1)}, u32[]{:S(2)}, u32[]{:S(2)}) collective-permute-start(bf16[5,512,256]{2,1,0:T(8,128)(2,1)S(1)} %get-tuple-element.124), channel_id=1, source_target_pairs={{0,1},{1,0},{2,3},{3,2},{4,5},{5,4},{6,7},{7,6},{8,9},{9,8},{10,11... | collective-permute-start | bytes 3932168 | tf_op jit(solution)/shard_map/swap1/ppermute | solution.py:361
  82.4 1.9 %collective-permute-start.25 = (bf16[512,256]{1,0:T(8,128)(2,1)S(1)}, bf16[512,256]{1,0:T(8,128)(2,1)S(1)}, u32[]{:S(2)}, u32[]{:S(2)}) collective-permute-start(bf16[512,256]{1,0:T(8,128)(2,1)S(1)} %collective-permute-done.20.refs_2_), channel_id=1, source_target_pairs={{4,0},{8,4},{12,8},{14,12},{10,14},{6,10},{2,6},{0,2},{5,1},{9,5},... | collective-permute-start | bytes 786440 | tf_op jit(solution)/shard_map/down12c3/ppermute | solution.py:379
  84.3 3.0 %gram0.1.refs_0_ = bf16[4,2048,2048]{2,1,0:T(8,128)(2,1)} custom-call(bf16[5,512,256]{2,1,0:T(8,128)(2,1)S(1)} %get-tuple-element.103.refs_0_.refs_1_, bf16[5,512,256]{2,1,0:T(8,128)(2,1)S(1)} %collective-permute-done.23.refs_1_.refs_3_.refs_4_.refs_5_), custom_call_target="tpu_custom_call" | custom-call | flops 20000000000 | bytes 1024 | tf_op jit(solution)/shard_map/gram0/pallas_call | solution.py:290
  87.5 1.9 %collective-permute-start.30 = (bf16[256,256]{1,0:T(8,128)(2,1)S(1)}, bf16[256,256]{1,0:T(8,128)(2,1)S(1)}, u32[]{:S(2)}, u32[]{:S(2)}) collective-permute-start(bf16[256,256]{1,0:T(8,128)(2,1)S(1)} %slice.37), channel_id=1, source_target_pairs={{4,0},{8,4},{12,8},{14,12},{10,14},{6,10},{2,6},{0,2},{5,1},{9,5},... | collective-permute-start | bytes 393224 | tf_op jit(solution)/shard_map/down13c2/ppermute | solution.py:379
  89.5 2.0 %collective-permute-done.24.refs_3_ = bf16[512,256]{1,0:T(8,128)(2,1)S(1)} collective-permute-done((bf16[512,256]{1,0:T(8,128)(2,1)S(1)}, bf16[512,256]{1,0:T(8,128)(2,1)S(1)}, u32[]{:S(2)}, u32[]{:S(2)}) %collective-permute-start.24) | collective-permute-done | bytes 262176 | tf_op jit(solution)/shard_map/up12c3/ppermute | solution.py:377
  91.6 1.7 %collective-permute-start.31 = (bf16[512,256]{1,0:T(8,128)(2,1)S(1)}, bf16[512,256]{1,0:T(8,128)(2,1)S(1)}, u32[]{:S(2)}, u32[]{:S(2)}) collective-permute-start(bf16[512,256]{1,0:T(8,128)(2,1)S(1)} %collective-permute-done.24.refs_3_), channel_id=1, source_target_pairs={{0,4},{4,8},{8,12},{12,14},{14,10},{10,6},{6,2},{2,0},{1,5},{5,9},... | collective-permute-start | bytes 786440 | tf_op jit(solution)/shard_map/up14c3/ppermute | solution.py:377
  93.6 5.0 %gram1.1.refs_0_ = bf16[4,2048,2048]{2,1,0:T(8,128)(2,1)} custom-call(bf16[4,2048,2048]{2,1,0:T(8,128)(2,1)} %gram0.1.refs_0_, bf16[5,512,256]{2,1,0:T(8,128)(2,1)S(1)} %get-tuple-element.103.refs_0_.refs_1_, bf16[5,512,256]{2,1,0:T(8,128)(2,1)S(1)} %get-tuple-element.120.refs_2_, ...), custom_call_target="tpu_custom_call", output_to_operand_aliasing={{}: (0, {})} | custom-call | flops 20000000000 | bytes 1024 | tf_op jit(solution)/shard_map/gram1/pallas_call | solution.py:290
  99.7 1.6 %collective-permute-start.33 = (bf16[256,256]{1,0:T(8,128)(2,1)S(1)}, bf16[256,256]{1,0:T(8,128)(2,1)S(1)}, u32[]{:S(2)}, u32[]{:S(2)}) collective-permute-start(bf16[256,256]{1,0:T(8,128)(2,1)S(1)} %slice.38), channel_id=1, source_target_pairs={{0,4},{4,8},{8,12},{12,14},{14,10},{10,6},{6,2},{2,0},{1,5},{5,9},... | collective-permute-start | bytes 393224 | tf_op jit(solution)/shard_map/up15c3/ppermute | solution.py:377
  101.8 1.7 %mix.6 = (bf16[5,512,256]{2,1,0:T(8,128)(2,1)S(1)}, bf16[5,512,256]{2,1,0:T(8,128)(2,1)S(1)}) custom-call(bf16[512,256]{1,0:T(8,128)(2,1)S(1)} %copy-done.1, bf16[512,256]{1,0:T(8,128)(2,1)S(1)} %collective-permute-done.11.refs_1_, bf16[512,256]{1,0:T(8,128)(2,1)S(1)} %collective-permute-done.12.refs_2_, ...), custom_call_target="tpu_custom_call" | custom-call | flops 20000000000 | bytes 1024 | tf_op jit(solution)/shard_map/mix/pallas_call | solution.py:208
  106.3 1.9 %mix.7 = (bf16[5,512,256]{2,1,0:T(8,128)(2,1)S(1)}, bf16[5,512,256]{2,1,0:T(8,128)(2,1)S(1)}) custom-call(bf16[512,256]{1,0:T(8,128)(2,1)S(1)} %copy-done, bf16[512,256]{1,0:T(8,128)(2,1)S(1)} %collective-permute-done.19.refs_1_, bf16[512,256]{1,0:T(8,128)(2,1)S(1)} %collective-permute-done.20.refs_2_, bf16[512,256]{1,0:T(8,128)(2,1)S(1)} %collective-permute-done.24.refs_3_, ...), custom_call_target="tpu_custom_call" | custom-call | flops 20000000000 | bytes 1024 | tf_op jit(solution)/shard_map/mix/pallas_call | solution.py:208
  109.3 7.5 %gram2.1.refs_0_ = bf16[4,2048,2048]{2,1,0:T(8,128)(2,1)} custom-call(bf16[4,2048,2048]{2,1,0:T(8,128)(2,1)} %gram1.1.refs_0_, bf16[5,512,256]{2,1,0:T(8,128)(2,1)S(1)} %get-tuple-element.103.refs_0_.refs_1_, bf16[5,512,256]{2,1,0:T(8,128)(2,1)S(1)} %get-tuple-element.120.refs_2_, ...), custom_call_target="tpu_custom_call", output_to_operand_aliasing={{}: (0, {})} | custom-call | flops 20000000000 | bytes 1024 | tf_op jit(solution)/shard_map/gram2/pallas_call | solution.py:290
  116.9 10.1 %gram3.1 = bf16[4,2048,2048]{2,1,0:T(8,128)(2,1)} custom-call(bf16[4,2048,2048]{2,1,0:T(8,128)(2,1)} %gram2.1.refs_0_, bf16[5,512,256]{2,1,0:T(8,128)(2,1)S(1)} %get-tuple-element.103.refs_0_.refs_1_, bf16[5,512,256]{2,1,0:T(8,128)(2,1)S(1)} %get-tuple-element.120.refs_2_, ...), custom_call_target="tpu_custom_call", output_to_operand_aliasing={{}: (0, {})} | custom-call | flops 20000000000 | bytes 1024 | tf_op jit(solution)/shard_map/gram3/pallas_call | solution.py:290
  (73 shorter events, 23.5 us)
Async XLA Ops:
  13.1 7.0 %collective-permute-start.2 = (bf16[512,256]{1,0:T(8,128)(2,1)}, bf16[512,256]{1,0:T(8,128)(2,1)S(1)}, u32[]{:S(2)}, u32[]{:S(2)}) collective-permute-start(bf16[512,256]{1,0:T(8,128)(2,1)} %get-tuple-element.88.refs_0_), channel_id=1, source_target_pairs={{4,0},{8,4},{12,8},{14,12},{10,14},{6,10},{2,6},{0,2},{5,1},{9,5},... | collective-permute-start | bytes 786440 | tf_op jit(solution)/shard_map/down0c0/ppermute | solution.py:379
  15.5 6.6 %collective-permute-start.1 = (bf16[512,256]{1,0:T(8,128)(2,1)}, bf16[512,256]{1,0:T(8,128)(2,1)S(1)}, u32[]{:S(2)}, u32[]{:S(2)}) collective-permute-start(bf16[512,256]{1,0:T(8,128)(2,1)} %get-tuple-element.88.refs_0_), channel_id=1, source_target_pairs={{0,4},{4,8},{8,12},{12,14},{14,10},{10,6},{6,2},{2,0},{1,5},{5,9},... | collective-permute-start | bytes 786440 | tf_op jit(solution)/shard_map/up0c0/ppermute | solution.py:377
  15.6 9.3 %collective-permute-start.6 = (bf16[512,256]{1,0:T(8,128)(2,1)}, bf16[512,256]{1,0:T(8,128)(2,1)S(1)}, u32[]{:S(2)}, u32[]{:S(2)}) collective-permute-start(bf16[512,256]{1,0:T(8,128)(2,1)} %get-tuple-element.108.refs_0_), channel_id=1, source_target_pairs={{4,0},{8,4},{12,8},{14,12},{10,14},{6,10},{2,6},{0,2},{5,1},{9,5},... | collective-permute-start | bytes 786440 | tf_op jit(solution)/shard_map/down1c1/ppermute | solution.py:379
  17.5 9.9 %collective-permute-start.5 = (bf16[512,256]{1,0:T(8,128)(2,1)}, bf16[512,256]{1,0:T(8,128)(2,1)S(1)}, u32[]{:S(2)}, u32[]{:S(2)}) collective-permute-start(bf16[512,256]{1,0:T(8,128)(2,1)} %get-tuple-element.108.refs_0_), channel_id=1, source_target_pairs={{0,4},{4,8},{8,12},{12,14},{14,10},{10,6},{6,2},{2,0},{1,5},{5,9},... | collective-permute-start | bytes 786440 | tf_op jit(solution)/shard_map/up1c1/ppermute | solution.py:377
  20.1 10.4 %collective-permute-start.4 = (bf16[512,256]{1,0:T(8,128)(2,1)S(1)}, bf16[512,256]{1,0:T(8,128)(2,1)S(1)}, u32[]{:S(2)}, u32[]{:S(2)}) collective-permute-start(bf16[512,256]{1,0:T(8,128)(2,1)S(1)} %collective-permute-done.2.refs_2_), channel_id=1, source_target_pairs={{4,0},{8,4},{12,8},{14,12},{10,14},{6,10},{2,6},{0,2},{5,1},{9,5},... | collective-permute-start | bytes 786440 | tf_op jit(solution)/shard_map/down2c0/ppermute | solution.py:379
  22.1 10.9 %collective-permute-start.3 = (bf16[512,256]{1,0:T(8,128)(2,1)S(1)}, bf16[512,256]{1,0:T(8,128)(2,1)S(1)}, u32[]{:S(2)}, u32[]{:S(2)}) collective-permute-start(bf16[512,256]{1,0:T(8,128)(2,1)S(1)} %collective-permute-done.1.refs_1_), channel_id=1, source_target_pairs={{0,4},{4,8},{8,12},{12,14},{14,10},{10,6},{6,2},{2,0},{1,5},{5,9},... | collective-permute-start | bytes 786440 | tf_op jit(solution)/shard_map/up2c0/ppermute | solution.py:377
  27.4 11.2 %collective-permute-start.9 = (bf16[512,256]{1,0:T(8,128)(2,1)S(1)}, bf16[512,256]{1,0:T(8,128)(2,1)S(1)}, u32[]{:S(2)}, u32[]{:S(2)}) collective-permute-start(bf16[512,256]{1,0:T(8,128)(2,1)S(1)} %collective-permute-done.5.refs_1_), channel_id=1, source_target_pairs={{0,4},{4,8},{8,12},{12,14},{14,10},{10,6},{6,2},{2,0},{1,5},{5,9},... | collective-permute-start | bytes 786440 | tf_op jit(solution)/shard_map/up3c1/ppermute | solution.py:377
  27.4 12.8 %collective-permute-start.10 = (bf16[512,256]{1,0:T(8,128)(2,1)S(1)}, bf16[512,256]{1,0:T(8,128)(2,1)S(1)}, u32[]{:S(2)}, u32[]{:S(2)}) collective-permute-start(bf16[512,256]{1,0:T(8,128)(2,1)S(1)} %collective-permute-done.6.refs_2_), channel_id=1, source_target_pairs={{4,0},{8,4},{12,8},{14,12},{10,14},{6,10},{2,6},{0,2},{5,1},{9,5},... | collective-permute-start | bytes 786440 | tf_op jit(solution)/shard_map/down3c1/ppermute | solution.py:379
  29.4 14.8 %collective-permute-start.11 = (bf16[512,256]{1,0:T(8,128)(2,1)}, bf16[512,256]{1,0:T(8,128)(2,1)S(1)}, u32[]{:S(2)}, u32[]{:S(2)}) collective-permute-start(bf16[512,256]{1,0:T(8,128)(2,1)} %get-tuple-element.129.refs_0_), channel_id=1, source_target_pairs={{0,4},{4,8},{8,12},{12,14},{14,10},{10,6},{6,2},{2,0},{1,5},{5,9},... | collective-permute-start | bytes 786440 | tf_op jit(solution)/shard_map/up4c2/ppermute | solution.py:377
  30.5 15.3 %collective-permute-start.12 = (bf16[512,256]{1,0:T(8,128)(2,1)}, bf16[512,256]{1,0:T(8,128)(2,1)S(1)}, u32[]{:S(2)}, u32[]{:S(2)}) collective-permute-start(bf16[512,256]{1,0:T(8,128)(2,1)} %get-tuple-element.129.refs_0_), channel_id=1, source_target_pairs={{4,0},{8,4},{12,8},{14,12},{10,14},{6,10},{2,6},{0,2},{5,1},{9,5},... | collective-permute-start | bytes 786440 | tf_op jit(solution)/shard_map/down4c2/ppermute | solution.py:379
  33.0 16.9 %collective-permute-start.7 = (bf16[512,256]{1,0:T(8,128)(2,1)S(1)}, bf16[512,256]{1,0:T(8,128)(2,1)S(1)}, u32[]{:S(2)}, u32[]{:S(2)}) collective-permute-start(bf16[512,256]{1,0:T(8,128)(2,1)S(1)} %collective-permute-done.3.refs_3_), channel_id=1, source_target_pairs={{0,4},{4,8},{8,12},{12,14},{14,10},{10,6},{6,2},{2,0},{1,5},{5,9},... | collective-permute-start | bytes 786440 | tf_op jit(solution)/shard_map/up5c0/ppermute | solution.py:377
  38.7 11.2 %collective-permute-start.8 = (bf16[512,256]{1,0:T(8,128)(2,1)S(1)}, bf16[512,256]{1,0:T(8,128)(2,1)S(1)}, u32[]{:S(2)}, u32[]{:S(2)}) collective-permute-start(bf16[512,256]{1,0:T(8,128)(2,1)S(1)} %collective-permute-done.4.refs_4_), channel_id=1, source_target_pairs={{4,0},{8,4},{12,8},{14,12},{10,14},{6,10},{2,6},{0,2},{5,1},{9,5},... | collective-permute-start | bytes 786440 | tf_op jit(solution)/shard_map/down5c0/ppermute | solution.py:379
  40.2 15.3 %collective-permute-start.17 = (bf16[512,256]{1,0:T(8,128)(2,1)S(1)}, bf16[512,256]{1,0:T(8,128)(2,1)S(1)}, u32[]{:S(2)}, u32[]{:S(2)}) collective-permute-start(bf16[512,256]{1,0:T(8,128)(2,1)S(1)} %collective-permute-done.9.refs_3_), channel_id=1, source_target_pairs={{0,4},{4,8},{8,12},{12,14},{14,10},{10,6},{6,2},{2,0},{1,5},{5,9},... | collective-permute-start | bytes 786440 | tf_op jit(solution)/shard_map/up6c1/ppermute | solution.py:377
  44.3 12.8 %collective-permute-start.18 = (bf16[512,256]{1,0:T(8,128)(2,1)S(1)}, bf16[512,256]{1,0:T(8,128)(2,1)S(1)}, u32[]{:S(2)}, u32[]{:S(2)}) collective-permute-start(bf16[512,256]{1,0:T(8,128)(2,1)S(1)} %collective-permute-done.10.refs_4_), channel_id=1, source_target_pairs={{4,0},{8,4},{12,8},{14,12},{10,14},{6,10},{2,6},{0,2},{5,1},{9,5},... | collective-permute-start | bytes 786440 | tf_op jit(solution)/shard_map/down6c1/ppermute | solution.py:379
  49.9 16.1 %collective-permute-start.15 = (bf16[512,256]{1,0:T(8,128)(2,1)S(1)}, bf16[512,256]{1,0:T(8,128)(2,1)S(1)}, u32[]{:S(2)}, u32[]{:S(2)}) collective-permute-start(bf16[512,256]{1,0:T(8,128)(2,1)S(1)} %collective-permute-done.11.refs_1_), channel_id=1, source_target_pairs={{0,4},{4,8},{8,12},{12,14},{14,10},{10,6},{6,2},{2,0},{1,5},{5,9},... | collective-permute-start | bytes 786440 | tf_op jit(solution)/shard_map/up8c2/ppermute | solution.py:377
  50.0 17.6 %collective-permute-start.16 = (bf16[512,256]{1,0:T(8,128)(2,1)S(1)}, bf16[512,256]{1,0:T(8,128)(2,1)S(1)}, u32[]{:S(2)}, u32[]{:S(2)}) collective-permute-start(bf16[512,256]{1,0:T(8,128)(2,1)S(1)} %collective-permute-done.12.refs_2_), channel_id=1, source_target_pairs={{4,0},{8,4},{12,8},{14,12},{10,14},{6,10},{2,6},{0,2},{5,1},{9,5},... | collective-permute-start | bytes 786440 | tf_op jit(solution)/shard_map/down8c2/ppermute | solution.py:379
  51.9 12.0 %collective-permute-start.13 = (bf16[256,256]{1,0:T(8,128)(2,1)S(1)}, bf16[256,256]{1,0:T(8,128)(2,1)S(1)}, u32[]{:S(2)}, u32[]{:S(2)}) collective-permute-start(bf16[256,256]{1,0:T(8,128)(2,1)S(1)} %slice.32), channel_id=1, source_target_pairs={{0,4},{4,8},{8,12},{12,14},{14,10},{10,6},{6,2},{2,0},{1,5},{5,9},... | collective-permute-start | bytes 393224 | tf_op jit(solution)/shard_map/up7c0/ppermute | solution.py:377
  55.5 10.0 %collective-permute-start.14 = (bf16[256,256]{1,0:T(8,128)(2,1)S(1)}, bf16[256,256]{1,0:T(8,128)(2,1)S(1)}, u32[]{:S(2)}, u32[]{:S(2)}) collective-permute-start(bf16[256,256]{1,0:T(8,128)(2,1)S(1)} %slice.33), channel_id=1, source_target_pairs={{4,0},{8,4},{12,8},{14,12},{10,14},{6,10},{2,6},{0,2},{5,1},{9,5},... | collective-permute-start | bytes 393224 | tf_op jit(solution)/shard_map/down7c0/ppermute | solution.py:379
  57.1 13.1 %collective-permute-start.21 = (bf16[256,256]{1,0:T(8,128)(2,1)S(1)}, bf16[256,256]{1,0:T(8,128)(2,1)S(1)}, u32[]{:S(2)}, u32[]{:S(2)}) collective-permute-start(bf16[256,256]{1,0:T(8,128)(2,1)S(1)} %slice.34), channel_id=1, source_target_pairs={{0,4},{4,8},{8,12},{12,14},{14,10},{10,6},{6,2},{2,0},{1,5},{5,9},... | collective-permute-start | bytes 393224 | tf_op jit(solution)/shard_map/up9c1/ppermute | solution.py:377
  65.5 10.1 %collective-permute-start.19 = (bf16[512,256]{1,0:T(8,128)(2,1)}, bf16[512,256]{1,0:T(8,128)(2,1)S(1)}, u32[]{:S(2)}, u32[]{:S(2)}) collective-permute-start(bf16[512,256]{1,0:T(8,128)(2,1)} %get-tuple-element.102.refs_0_), channel_id=1, source_target_pairs={{0,4},{4,8},{8,12},{12,14},{14,10},{10,6},{6,2},{2,0},{1,5},{5,9},... | collective-permute-start | bytes 786440 | tf_op jit(solution)/shard_map/up10c3/ppermute | solution.py:377
  66.0 9.6 %collective-permute-start.20 = (bf16[512,256]{1,0:T(8,128)(2,1)}, bf16[512,256]{1,0:T(8,128)(2,1)S(1)}, u32[]{:S(2)}, u32[]{:S(2)}) collective-permute-start(bf16[512,256]{1,0:T(8,128)(2,1)} %get-tuple-element.102.refs_0_), channel_id=1, source_target_pairs={{4,0},{8,4},{12,8},{14,12},{10,14},{6,10},{2,6},{0,2},{5,1},{9,5},... | collective-permute-start | bytes 786440 | tf_op jit(solution)/shard_map/down10c3/ppermute | solution.py:379
  70.3 9.3 %collective-permute-start.26 = (bf16[512,256]{1,0:T(8,128)(2,1)S(1)}, bf16[512,256]{1,0:T(8,128)(2,1)S(1)}, u32[]{:S(2)}, u32[]{:S(2)}) collective-permute-start(bf16[512,256]{1,0:T(8,128)(2,1)S(1)} %collective-permute-done.15.refs_3_), channel_id=1, source_target_pairs={{0,4},{4,8},{8,12},{12,14},{14,10},{10,6},{6,2},{2,0},{1,5},{5,9},... | collective-permute-start | bytes 786440 | tf_op jit(solution)/shard_map/up11c2/ppermute | solution.py:377
  70.8 9.2 %collective-permute-start.27 = (bf16[512,256]{1,0:T(8,128)(2,1)S(1)}, bf16[512,256]{1,0:T(8,128)(2,1)S(1)}, u32[]{:S(2)}, u32[]{:S(2)}) collective-permute-start(bf16[512,256]{1,0:T(8,128)(2,1)S(1)} %collective-permute-done.16.refs_4_), channel_id=1, source_target_pairs={{4,0},{8,4},{12,8},{14,12},{10,14},{6,10},{2,6},{0,2},{5,1},{9,5},... | collective-permute-start | bytes 786440 | tf_op jit(solution)/shard_map/down11c2/ppermute | solution.py:379
  72.3 9.9 %collective-permute-start.23 = (bf16[5,512,256]{2,1,0:T(8,128)(2,1)S(1)}, bf16[5,512,256]{2,1,0:T(8,128)(2,1)S(1)}, u32[]{:S(2)}, u32[]{:S(2)}) collective-permute-start(bf16[5,512,256]{2,1,0:T(8,128)(2,1)S(1)} %get-tuple-element.107), channel_id=1, source_target_pairs={{0,1},{1,0},{2,3},{3,2},{4,5},{5,4},{6,7},{7,6},{8,9},{9,8},{10,11... | collective-permute-start | bytes 3932168 | tf_op jit(solution)/shard_map/swap0/ppermute | solution.py:361
  80.0 11.6 %collective-permute-start.28 = (bf16[5,512,256]{2,1,0:T(8,128)(2,1)S(1)}, bf16[5,512,256]{2,1,0:T(8,128)(2,1)S(1)}, u32[]{:S(2)}, u32[]{:S(2)}) collective-permute-start(bf16[5,512,256]{2,1,0:T(8,128)(2,1)S(1)} %get-tuple-element.124), channel_id=1, source_target_pairs={{0,1},{1,0},{2,3},{3,2},{4,5},{5,4},{6,7},{7,6},{8,9},{9,8},{10,11... | collective-permute-start | bytes 3932168 | tf_op jit(solution)/shard_map/swap1/ppermute | solution.py:361
  82.2 9.2 %collective-permute-start.24 = (bf16[512,256]{1,0:T(8,128)(2,1)S(1)}, bf16[512,256]{1,0:T(8,128)(2,1)S(1)}, u32[]{:S(2)}, u32[]{:S(2)}) collective-permute-start(bf16[512,256]{1,0:T(8,128)(2,1)S(1)} %collective-permute-done.19.refs_1_), channel_id=1, source_target_pairs={{0,4},{4,8},{8,12},{12,14},{14,10},{10,6},{6,2},{2,0},{1,5},{5,9},... | collective-permute-start | bytes 786440 | tf_op jit(solution)/shard_map/up12c3/ppermute | solution.py:377
  82.4 9.2 %collective-permute-start.25 = (bf16[512,256]{1,0:T(8,128)(2,1)S(1)}, bf16[512,256]{1,0:T(8,128)(2,1)S(1)}, u32[]{:S(2)}, u32[]{:S(2)}) collective-permute-start(bf16[512,256]{1,0:T(8,128)(2,1)S(1)} %collective-permute-done.20.refs_2_), channel_id=1, source_target_pairs={{4,0},{8,4},{12,8},{14,12},{10,14},{6,10},{2,6},{0,2},{5,1},{9,5},... | collective-permute-start | bytes 786440 | tf_op jit(solution)/shard_map/down12c3/ppermute | solution.py:379
  87.4 11.2 %collective-permute-start.29 = (bf16[256,256]{1,0:T(8,128)(2,1)S(1)}, bf16[256,256]{1,0:T(8,128)(2,1)S(1)}, u32[]{:S(2)}, u32[]{:S(2)}) collective-permute-start(bf16[256,256]{1,0:T(8,128)(2,1)S(1)} %slice.36), channel_id=1, source_target_pairs={{0,4},{4,8},{8,12},{12,14},{14,10},{10,6},{6,2},{2,0},{1,5},{5,9},... | collective-permute-start | bytes 393224 | tf_op jit(solution)/shard_map/up13c2/ppermute | solution.py:377
  87.5 11.1 %collective-permute-start.30 = (bf16[256,256]{1,0:T(8,128)(2,1)S(1)}, bf16[256,256]{1,0:T(8,128)(2,1)S(1)}, u32[]{:S(2)}, u32[]{:S(2)}) collective-permute-start(bf16[256,256]{1,0:T(8,128)(2,1)S(1)} %slice.37), channel_id=1, source_target_pairs={{4,0},{8,4},{12,8},{14,12},{10,14},{6,10},{2,6},{0,2},{5,1},{9,5},... | collective-permute-start | bytes 393224 | tf_op jit(solution)/shard_map/down13c2/ppermute | solution.py:379
  91.6 7.3 %collective-permute-start.31 = (bf16[512,256]{1,0:T(8,128)(2,1)S(1)}, bf16[512,256]{1,0:T(8,128)(2,1)S(1)}, u32[]{:S(2)}, u32[]{:S(2)}) collective-permute-start(bf16[512,256]{1,0:T(8,128)(2,1)S(1)} %collective-permute-done.24.refs_3_), channel_id=1, source_target_pairs={{0,4},{4,8},{8,12},{12,14},{14,10},{10,6},{6,2},{2,0},{1,5},{5,9},... | collective-permute-start | bytes 786440 | tf_op jit(solution)/shard_map/up14c3/ppermute | solution.py:377
  93.3 6.4 %collective-permute-start.32 = (bf16[512,256]{1,0:T(8,128)(2,1)S(1)}, bf16[512,256]{1,0:T(8,128)(2,1)S(1)}, u32[]{:S(2)}, u32[]{:S(2)}) collective-permute-start(bf16[512,256]{1,0:T(8,128)(2,1)S(1)} %collective-permute-done.25.refs_4_), channel_id=1, source_target_pairs={{4,0},{8,4},{12,8},{14,12},{10,14},{6,10},{2,6},{0,2},{5,1},{9,5},... | collective-permute-start | bytes 786440 | tf_op jit(solution)/shard_map/down14c3/ppermute | solution.py:379
  108.2 8.6 %collective-permute-start.36 = (bf16[5,512,256]{2,1,0:T(8,128)(2,1)S(1)}, bf16[5,512,256]{2,1,0:T(8,128)(2,1)S(1)}, u32[]{:S(2)}, u32[]{:S(2)}) collective-permute-start(bf16[5,512,256]{2,1,0:T(8,128)(2,1)S(1)} %get-tuple-element.144), channel_id=1, source_target_pairs={{0,1},{1,0},{2,3},{3,2},{4,5},{5,4},{6,7},{7,6},{8,9},{9,8},{10,11... | collective-permute-start | bytes 3932168 | tf_op jit(solution)/shard_map/swap3/ppermute | solution.py:361
  (11 other events, 58.7 us)
